TPU v7x, 32 devices: a whole 2x2x4 slice. The times are simulated.
32 devices in a mesh: row: 2 (over x), col: 16 (over z, y, core).
Axes of the slice: x: 2, y: 2, z: 4, core: 2. Of those that a mesh axis runs over, the one named last changes fastest.
Arguments:
- wave_field: float32 [64, 64, 16, 128], P(None, 'col', 'row'), may hold values from -6 to 6
- medium_term: float32 [64, 16, 128], P('col', 'row'), may hold values from 0.5 to 4
- node_flux: float32 [64, 16, 2, 384], P(None, 'col', 'row'), may hold values from -6 to 6
- node_cell: int32 [16, 2, 384], P('col', 'row'), may hold values from 0 to 4095
- block_target: int32 [16, 2, 16], P('col', 'row'), may hold values from 0 to 15, as said below
- boundary_matrix: bfloat16 [2, 1024, 12288], P(None, 'row', 'col'), may hold values from -0.078125 to 0.078125
Outputs:
- volume_image: float32 [64, 64, 16, 128], P(None, 'col', 'row')
- boundary_image: float32 [1024, 64], P(('row', 'col'))
Inputs may be any that keep to these rules, and one draw needn't show every extreme that they name: For every brick (c, r), block_target[c, r, :] is a permutation of the 16 column blocks.
All inputs are finite; a program needn't handle non-finite values.
Results may differ from a plain program's by a relative error of at most 0.0029.
Values may be sent and summed in bfloat16 or wider, within the bound.
No kernel may reach another device: no remote copies, remote signals or barrier semaphores. Data moves between devices by JAX's collectives and lax.ppermute only.
A program may use at most 64 MiB of HBM per device.

v0:
```python
import jax
import jax.numpy as jnp
from jax import lax
from jax.sharding import PartitionSpec as P


def padded_2(block, sides, width):
    for axis, dim in sides:
        count = lax.axis_size(axis)
        forward = [(i, i + 1) for i in range(count - 1)]
        backward = [(target, source) for source, target in forward]
        low = lax.ppermute(
            lax.slice_in_dim(block, block.shape[dim] - width, None, axis=dim), axis, forward
        )
        high = lax.ppermute(lax.slice_in_dim(block, 0, width, axis=dim), axis, backward)
        block = jnp.concatenate([low, block, high], axis=dim)
    return block


def three_tap(values, axis, side_weight, centre_weight):
    length = values.shape[axis]
    lower = lax.slice_in_dim(values, 0, length - 2, axis=axis)
    middle = lax.slice_in_dim(values, 1, length - 1, axis=axis)
    upper = lax.slice_in_dim(values, 2, length, axis=axis)
    return side_weight * (lower + upper) + centre_weight * middle


def on_device(wave_field, medium_term, node_flux, node_cell, block_target, boundary_matrix):
    components, width_x, width_y, depth_cells = wave_field.shape
    cell_total = width_x * width_y * depth_cells
    angles = components // 2
    col_count = lax.axis_size("col")
    node_total = node_cell.shape[-1]
    slot_len = node_total // col_count
    targets = block_target.reshape(col_count)
    block_ids = jnp.arange(col_count, dtype=jnp.int32)
    matches = targets[None, :] == block_ids[:, None]
    slot_cells = node_cell.reshape(col_count, slot_len)
    ordered = jnp.sum(jnp.where(matches[:, :, None], slot_cells[None, :, :], 0), axis=1).reshape(
        node_total
    )
    flat_field = wave_field.reshape(components, cell_total)
    traces = jnp.take(flat_field, ordered, axis=1).astype(jnp.bfloat16)
    received = lax.all_to_all(traces, "col", split_axis=1, concat_axis=1, tiled=True)
    column_traces = lax.all_gather(received, "row", axis=1, tiled=True)
    padded = padded_2(wave_field, (("row", 2), ("col", 1)), 1)
    padded = jnp.pad(padded, ((0, 0), (0, 0), (0, 0), (1, 1)))
    elem_z = three_tap(padded, 3, 1.0 / 6.0, 2.0 / 3.0)
    lapl_z = three_tap(padded, 3, -1.0, 2.0)
    lump_z = three_tap(padded, 3, 1.0 / 3.0, 2.0 / 3.0)
    elem_yz = three_tap(elem_z, 2, 1.0 / 6.0, 2.0 / 3.0)
    lapl_y_elem_z = three_tap(elem_z, 2, -1.0, 2.0)
    elem_y_lapl_z = three_tap(lapl_z, 2, 1.0 / 6.0, 2.0 / 3.0)
    lump_yz = three_tap(lump_z, 2, 1.0 / 3.0, 2.0 / 3.0)
    stiffness = three_tap(elem_yz, 1, -1.0, 2.0) + three_tap(
        lapl_y_elem_z + elem_y_lapl_z, 1, 1.0 / 6.0, 2.0 / 3.0
    )
    mass_sum = three_tap(lump_yz, 1, 1.0 / 3.0, 2.0 / 3.0)
    volume_image = stiffness - medium_term[None] * mass_sum
    flat_image = volume_image.reshape(components, cell_total)
    flat_image = flat_image.at[:, node_cell.reshape(node_total)].add(
        -node_flux.reshape(components, node_total)
    )
    volume_image = flat_image.reshape(components, width_x, width_y, depth_cells)
    slab_rows = boundary_matrix.shape[1]
    column_span = boundary_matrix.shape[2]
    own_rows = slab_rows // col_count
    products = lax.dot_general(
        boundary_matrix.reshape(2 * (own_rows * lax.axis_size("col")), column_span),
        column_traces,
        (((1,), (1,)), ((), ())),
        preferred_element_type=jnp.float32,
    )
    real_part = products[: own_rows * lax.axis_size("col")]
    imag_part = products[own_rows * lax.axis_size("col") :]
    boundary_image = lax.psum_scatter(
        jnp.concatenate(
            [
                real_part[:, :angles] - imag_part[:, angles:],
                imag_part[:, :angles] + real_part[:, angles:],
            ],
            axis=1,
        ),
        "col",
        scatter_dimension=0,
        tiled=True,
    )
    return (volume_image, boundary_image)


def solution(mesh):
    in_specs = (
        P(None, "col", "row", None),
        P("col", "row", None),
        P(None, "col", "row", None),
        P("col", "row", None),
        P("col", "row", None),
        P(None, "row", "col"),
    )
    out_specs = (P(None, "col", "row", None), P(("row", "col"), None))
    return jax.shard_map(
        on_device, mesh=mesh, in_specs=in_specs, out_specs=out_specs, check_vma=False
    )
```

profile of v0, /device:TPU:0, one launch (start us, length us, event | category | flops | bytes accessed | tf_op | source)
XLA Modules:
  0.0 109.9 jit_solution(11465096322440212866)
XLA Ops:
  7.2 2.1 %fusion.19 = (f32[64,4,1,128]{3,2,1,0:T(1,128)S(1)}, f32[64,4,1,128]{3,2,1,0:T(1,128)S(1)}) fusion(f32[64,4,8,128]{3,2,1,0:T(8,128)} %param.6), kind=kLoop, calls=%fused_computation.54 | loop fusion | bytes 524288 | tf_op jit(solution)/shard_map/slice | solution.py:13
  9.3 1.3 %collective-permute-start.1 = (f32[64,4,1,128]{3,0,2,1:T(8,128)S(1)}, f32[64,4,1,128]{3,0,2,1:T(8,128)S(1)}, u32[]{:S(2)}, u32[]{:S(2)}) collective-permute-start(f32[64,4,1,128]{3,0,2,1:T(8,128)S(1)} %copy.35), channel_id=1, source_target_pairs={{16,0},{17,1},{18,2},{19,3},{20,4},{21,5},{22,6},{23,7},{24,8},{25... | collective-permute-start | bytes 393224 | tf_op jit(solution)/shard_map/ppermute | solution.py:15
  10.6 5.5 %collective-permute-start = (f32[64,4,1,128]{3,0,2,1:T(8,128)S(1)}, f32[64,4,1,128]{3,0,2,1:T(8,128)}, u32[]{:S(2)}, u32[]{:S(2)}) collective-permute-start(f32[64,4,1,128]{3,0,2,1:T(8,128)S(1)} %copy.34), channel_id=1, source_target_pairs={{0,16},{1,17},{2,18},{3,19},{4,20},{5,21},{6,22},{7,23},{8,24},{9,... | collective-permute-start | bytes 393224 | tf_op jit(solution)/shard_map/ppermute | solution.py:12
  16.1 2.7 %copy.28 = bf16[64,4,8,128]{0,3,2,1:T(8,128)(2,1)} copy(f32[64,4,8,128]{3,2,1,0:T(8,128)} %param.6) | data formatting | bytes 1572864 | tf_op args[0]
  18.9 0.1 select_reduce_fusion
  19.1 0.1 reshape.120
  19.2 2.6 %gather_fusion = bf16[384,64]{1,0:T(8,128)(2,1)S(1)} fusion(bf16[64,4096]{0,1:T(8,128)(2,1)} %bitcast.28, s32[1024]{0:T(1024)S(1)} %pad_clamp_fusion), kind=kCustom, calls=%fused_computation | custom fusion | bytes 99840 | tf_op jit(solution)/shard_map/jit(_take)/gather | solution.py:43
  21.8 0.1 fusion.20
  22.0 0.7 reshape.145
  22.7 7.1 %all-to-all-start = ((bf16[16,2,768]{2,1,0:T(2,128)(2,1)}), bf16[16,2,768]{2,1,0:T(2,128)(2,1)S(1)}, u32[]{:S(2)}, u32[]{:S(2)}) async-start(bf16[16,2,768]{2,1,0:T(2,128)(2,1)} %reshape.145), calls=%async_computation | async-start | bytes 98304 | tf_op jit(solution)/shard_map/all_to_all | solution.py:44
  29.9 0.1 neg.6
  29.9 0.1 copy.36
  30.1 6.4 %all-to-all-done = bf16[16,2,768]{2,1,0:T(2,128)(2,1)S(1)} async-done(((bf16[16,2,768]{2,1,0:T(2,128)(2,1)}), bf16[16,2,768]{2,1,0:T(2,128)(2,1)S(1)}, u32[]{:S(2)}, u32[]{:S(2)}) %all-to-all-start) | async-done | bytes 49184 | tf_op jit(solution)/shard_map/all_to_all | solution.py:44
  36.6 0.1 reshape.146
  36.7 5.3 %all_gather.3 = bf16[64,768]{0,1:T(8,128)(2,1)S(1)} all-gather(bf16[64,384]{0,1:T(8,128)(2,1)S(1)} %bitcast.29), channel_id=1, replica_groups=mesh['row'=2,'col'=16] {'row'}, dimensions={1}, use_global_device_ids=true | all-gather | bytes 147456 | tf_op jit(solution)/shard_map/all_gather | solution.py:45
  42.0 0.6 convolution_bitcast_fusion
  42.6 0.1 copy.25
  42.8 1.0 copy.24
  43.8 1.2 %pad_maximum_fusion.3 = (f32[64,1,10,128]{3,2,1,0:T(8,128)}, f32[64,1,10,128]{3,2,1,0:T(8,128)}) fusion(f32[64,4,1,128]{3,2,1,0:T(1,128)S(1)} %copy.25, f32[64,4,8,128]{3,2,1,0:T(8,128)S(1)} %copy-done.1, f32[64,4,1,128]{3,2,1,0:T(1,128)S(1)} %copy.24), kind=kLoop, calls=%fused_computation.38 | loop fusion | flops 327680 | bytes 1966080 | tf_op jit(solution)/shard_map/slice | solution.py:13
  45.0 1.3 %collective-permute-start.3 = (f32[64,1,10,128]{3,2,1,0:T(8,128)}, f32[64,1,10,128]{3,2,1,0:T(8,128)}, u32[]{:S(2)}, u32[]{:S(2)}) collective-permute-start(f32[64,1,10,128]{3,2,1,0:T(8,128)} %get-tuple-element.14), channel_id=1, source_target_pairs={{1,0},{2,1},{3,2},{4,3},{5,4},{6,5},{7,6},{8,7},{9,8},{10,9},{11,1... | collective-permute-start | bytes 983048 | tf_op jit(solution)/shard_map/ppermute | solution.py:15
  46.2 3.8 %collective-permute-start.2 = (f32[64,1,10,128]{3,2,1,0:T(8,128)}, f32[64,1,10,128]{3,2,1,0:T(8,128)}, u32[]{:S(2)}, u32[]{:S(2)}) collective-permute-start(f32[64,1,10,128]{3,2,1,0:T(8,128)} %get-tuple-element.13), channel_id=1, source_target_pairs={{0,1},{1,2},{2,3},{3,4},{4,5},{5,6},{6,7},{7,8},{8,9},{9,10},{10,1... | collective-permute-start | bytes 983048 | tf_op jit(solution)/shard_map/ppermute | solution.py:12
  50.1 0.9 copy.31
  51.0 0.1 collective-permute-done.2
  51.2 1.7 %pad_maximum_fusion = f32[64,6,10,128]{3,2,1,0:T(8,128)S(1)} fusion(f32[64,1,10,128]{3,2,1,0:T(8,128)} %collective-permute-done.3, f32[64,4,1,128]{3,2,1,0:T(1,128)S(1)} %copy.25, f32[64,4,8,128]{3,2,1,0:T(8,128)S(1)} %copy-done.1, f32[64,4,1,128]{3,2,1,0:T(1,128)S(1)} %copy.24, f32[64,1,10,128]{3,2,1,0:T(8,128)} %collective-permute-done.2), kind=kLoop, calls=%fused_computation.5 | loop fusion | flops 1966080 | bytes 3932160 | tf_op jit(solution)/shard_map/concatenate | solution.py:16
  52.8 5.0 %multiply_add_fusion.2 = (f32[64,6,10,128]{3,2,1,0:T(8,128)S(1)}, f32[64,6,10,128]{3,2,1,0:T(8,128)S(1)}, f32[64,6,10,128]{3,2,1,0:T(8,128)S(1)}) fusion(f32[64,6,10,128]{3,2,1,0:T(8,128)S(1)} %pad_maximum_fusion), kind=kLoop, calls=%fused_computation.8 | loop fusion | flops 5406720 | bytes 7864320 | tf_op jit(solution)/shard_map/add | solution.py:25
  57.9 0.4 fusion.1
  58.3 1.0 multiply_add_fusion.3
  59.3 0.5 fusion.8
  59.8 2.0 %copy.26 = f32[64,4,8,128]{0,3,2,1:T(8,128)} copy(f32[64,4,8,128]{3,2,1,0:T(8,128)S(1)} %fusion.8) | data formatting | bytes 2097152 | tf_op jit(solution)/shard_map/sub | solution.py:59
  61.9 5.3 %scatter_custom_fusion = f32[64,4096]{0,1:T(8,128)} fusion(f32[64,4096]{0,1:T(8,128)} %bitcast.26, s32[384]{0:T(512)S(1)} %fusion.17, f32[64,1,1,384]{0,3,1,2:T(8,128)S(1)} %copy.36), kind=kCustom, calls=%fused_computation.39 | custom fusion | flops 24576 | bytes 1245184 | tf_op jit(solution)/shard_map/scatter-add | solution.py:61
  67.2 3.4 %copy.29 = f32[64,4,8,128]{3,2,1,0:T(8,128)} copy(f32[64,4,8,128]{0,3,2,1:T(8,128)} %bitcast.27) | data formatting | bytes 2097152
  70.6 32.5 %reduce-scatter.4.cloned.1.call-done = f32[32,64]{1,0:T(8,128)} async-done(((f32[512,64]{1,0:T(8,128)}), f32[32,64]{1,0:T(8,128)}) %reduce-scatter.4.cloned.1.call-update) | async-done | bytes 8208
  (28 shorter events, 0.3 us)
Async XLA Ops:
  7.2 34.8 %copy-start = (bf16[2,512,768]{2,1,0:T(8,128)(2,1)S(1)}, bf16[2,512,768]{2,1,0:T(8,128)(2,1)}, u32[]{:S(2)}) copy-start(bf16[2,512,768]{2,1,0:T(8,128)(2,1)} %param.11) | copy-start | bytes 4718596
  7.2 11.6 %copy-start.4 = (s32[1,1,384]{2,1,0:T(1,128)S(1)}, s32[1,1,384]{2,1,0:T(1,128)}, u32[]{:S(2)}) copy-start(s32[1,1,384]{2,1,0:T(1,128)} %param.9) | copy-start | bytes 4612
  7.2 11.7 %copy-start.5 = (s32[1,1,16]{2,1,0:T(1,128)S(1)}, s32[1,1,16]{2,1,0:T(1,128)}, u32[]{:S(2)}) copy-start(s32[1,1,16]{2,1,0:T(1,128)} %param.10) | copy-start | bytes 196
  7.2 22.6 %copy-start.2 = (f32[64,1,1,384]{3,2,1,0:T(1,128)S(1)}, f32[64,1,1,384]{3,2,1,0:T(1,128)}, u32[]{:S(2)}) copy-start(f32[64,1,1,384]{3,2,1,0:T(1,128)} %param.8) | copy-start | bytes 294916
  9.3 33.3 %collective-permute-start.1 = (f32[64,4,1,128]{3,0,2,1:T(8,128)S(1)}, f32[64,4,1,128]{3,0,2,1:T(8,128)S(1)}, u32[]{:S(2)}, u32[]{:S(2)}) collective-permute-start(f32[64,4,1,128]{3,0,2,1:T(8,128)S(1)} %copy.35), channel_id=1, source_target_pairs={{16,0},{17,1},{18,2},{19,3},{20,4},{21,5},{22,6},{23,7},{24,8},{25... | collective-permute-start | bytes 393224 | tf_op jit(solution)/shard_map/ppermute | solution.py:15
  10.6 32.1 %collective-permute-start = (f32[64,4,1,128]{3,0,2,1:T(8,128)S(1)}, f32[64,4,1,128]{3,0,2,1:T(8,128)}, u32[]{:S(2)}, u32[]{:S(2)}) collective-permute-start(f32[64,4,1,128]{3,0,2,1:T(8,128)S(1)} %copy.34), channel_id=1, source_target_pairs={{0,16},{1,17},{2,18},{3,19},{4,20},{5,21},{6,22},{7,23},{8,24},{9,... | collective-permute-start | bytes 393224 | tf_op jit(solution)/shard_map/ppermute | solution.py:12
  19.2 24.6 %copy-start.1 = (f32[64,4,8,128]{3,2,1,0:T(8,128)S(1)}, f32[64,4,8,128]{3,2,1,0:T(8,128)}, u32[]{:S(2)}) copy-start(f32[64,4,8,128]{3,2,1,0:T(8,128)} %param.6) | copy-start | bytes 3145732
  22.7 13.9 %all-to-all-start = ((bf16[16,2,768]{2,1,0:T(2,128)(2,1)}), bf16[16,2,768]{2,1,0:T(2,128)(2,1)S(1)}, u32[]{:S(2)}, u32[]{:S(2)}) async-start(bf16[16,2,768]{2,1,0:T(2,128)(2,1)} %reshape.145), calls=%async_computation | async-start | bytes 98304 | tf_op jit(solution)/shard_map/all_to_all | solution.py:44
  29.8 73.3 %reduce-scatter.4.cloned.1.call-start = ((), (), s32[]{:S(2)}) async-start(), calls=%async_computation.2 | async-start | bytes 278528
  45.0 6.1 %collective-permute-start.3 = (f32[64,1,10,128]{3,2,1,0:T(8,128)}, f32[64,1,10,128]{3,2,1,0:T(8,128)}, u32[]{:S(2)}, u32[]{:S(2)}) collective-permute-start(f32[64,1,10,128]{3,2,1,0:T(8,128)} %get-tuple-element.14), channel_id=1, source_target_pairs={{1,0},{2,1},{3,2},{4,3},{5,4},{6,5},{7,6},{8,7},{9,8},{10,9},{11,1... | collective-permute-start | bytes 983048 | tf_op jit(solution)/shard_map/ppermute | solution.py:15
  46.2 4.9 %collective-permute-start.2 = (f32[64,1,10,128]{3,2,1,0:T(8,128)}, f32[64,1,10,128]{3,2,1,0:T(8,128)}, u32[]{:S(2)}, u32[]{:S(2)}) collective-permute-start(f32[64,1,10,128]{3,2,1,0:T(8,128)} %get-tuple-element.13), channel_id=1, source_target_pairs={{0,1},{1,2},{2,3},{3,4},{4,5},{5,6},{6,7},{7,8},{8,9},{9,10},{10,1... | collective-permute-start | bytes 983048 | tf_op jit(solution)/shard_map/ppermute | solution.py:12
  58.3 1.0 copy-start.3
Sparse Core Ops, SparseCore 0:
  51.1 51.9 reduce-scatter.3
where the time goes:
time: 110 us
  waiting for transfers between devices  39.1 us (36%)
  starting transfers between devices  19 us (17%)
  local copies, waits for them, and re-layouts  16 us (15%)
  other arithmetic  15.5 us (14%)
  between operations  14.3 us (13%)
  blocking collectives  5.29 us (5%)
    unnamed x2, waiting for transfers between devices  32.5 us
    ppermute x2, starting transfers between devices, padded_2(): lax.ppermute(lax.slice_in_dim(block, block.shape[dim] - width, None, axis...  9.34 us
    unnamed x19, local copies, waits for them, and re-layouts  7.8 us
    all_to_all x1, starting transfers between devices, on_device(): lax.all_to_all(traces, 'col', split_axis=1, concat_axis=1, tiled=True)  7.09 us
    add x3, other arithmetic, three_tap(): return side_weight * (lower + upper) + centre_weight * middle  6.45 us
    all_to_all x1, waiting for transfers between devices, on_device(): lax.all_to_all(traces, 'col', split_axis=1, concat_axis=1, tiled=True)  6.44 us
    scatter-add x1, other arithmetic, on_device(): flat_image.at[:, node_cell.reshape(node_total)]  5.32 us
    all_gather x1, blocking collectives, on_device(): column_traces = lax.all_gather(received, 'row', axis=1, tiled=True)  5.29 us
  transfers between devices with their start and end apart: 6, of which 3 were waited for; matrix products, arithmetic and copies ran while one was open for 25% of the time, Pallas kernels for 0%

commit v1 on v0

v1 whole, which is shorter than its diff:
```python
import functools

import jax
import jax.numpy as jnp
from jax import lax
from jax.experimental import pallas as pl
from jax.experimental.pallas import tpu as pltpu
from jax.sharding import PartitionSpec as P

TILE_ROWS = 16
SMALL = 8 * 2**20


def vmem():
    return pl.BlockSpec(memory_space=pltpu.VMEM)


def one_hot_depth(cells, depth):
    lanes = jnp.bitwise_and(cells, depth - 1)
    at = lax.broadcasted_iota(jnp.int32, (depth, cells.shape[1]), 0)
    return jnp.where(at == lanes, 1.0, 0.0).astype(jnp.bfloat16)


def line_of(cells, depth):
    return jnp.right_shift(cells, depth.bit_length() - 1)


def trace_kernel(dims, target_ref, cell_ref, field_ref, tile_ref, *rest):
    comps, width_x, width_y, depth, rows, cols = dims
    face_refs, (lhs_ref,) = rest[:-1], rest[-1:]
    lines = width_x * width_y
    nodes = cell_ref.shape[1]
    slot_len = nodes // cols
    odd = lax.rem(lax.axis_index("row"), 2)
    for swap, face_ref in enumerate(face_refs):
        at_high = odd == swap
        layer = jnp.where(at_high, width_y - 1, 0)
        face_ref[...] = field_ref[pl.ds(layer, comps * width_x, stride=width_y), :]
    cells = cell_ref[...]
    hot = one_hot_depth(cells, depth)
    for line in range(lines):
        lhs_ref[pl.ds(line * comps, comps), :] = field_ref[
            pl.ds(line, comps, stride=lines), :
        ].astype(jnp.bfloat16)
    node_line = jnp.broadcast_to(line_of(cells, depth), (8, nodes))
    total = jnp.zeros((comps // 8, 8, nodes), jnp.float32)
    group = 4
    for first in range(0, lines, group):
        block = jnp.dot(
            lhs_ref[pl.ds(first * comps, group * comps), :], hot, preferred_element_type=jnp.float32
        ).reshape(group, comps // 8, 8, nodes)
        for line in range(group):
            total = jnp.where((node_line == first + line)[None], block[line], total)
    by_node = total.reshape(comps, nodes).T
    left_len = min(slot_len, TILE_ROWS)
    for slot in range(cols):
        piece = by_node[slot * slot_len : (slot + 1) * slot_len]
        left = piece[:left_len]
        right = piece[left_len:]
        if left_len < TILE_ROWS:
            left = jnp.concatenate(
                [left, jnp.zeros((TILE_ROWS - left_len, comps), jnp.float32)], axis=0
            )
        gap = TILE_ROWS - (slot_len - left_len)
        if slot_len == left_len:
            right = jnp.zeros((TILE_ROWS, comps), jnp.float32)
        elif gap:
            right = jnp.concatenate([right, jnp.zeros((gap, comps), jnp.float32)], axis=0)
        tile = jnp.concatenate([left, right], axis=1).astype(jnp.bfloat16)
        for row in range(rows):
            tile_ref[row * cols + target_ref[0, slot]] = tile


def face_kernel(dims, *refs):
    comps, width_x, width_y, depth, rows, cols = dims
    field_ref, row_refs, out_refs = refs[0], refs[1:-2], refs[-2:]
    odd = lax.rem(lax.axis_index("col"), 2)
    for swap, out_ref in enumerate(out_refs):
        layer = jnp.where(odd == swap, width_x - 1, 0)
        for comp in range(comps):
            start = pl.multiple_of(layer * width_y + comp * (width_x * width_y), width_y)
            out_ref[pl.ds(comp * width_y, width_y), :] = field_ref[pl.ds(start, width_y), :]
        for index, row_ref in enumerate(row_refs):
            out_ref[pl.ds(comps * width_y + index * comps, comps), :] = row_ref[
                pl.ds(layer, comps, stride=width_x), :
            ]


def unpack_tiles(tiles, slot_len, comps):
    left_len = min(slot_len, TILE_ROWS)
    parts = [tiles[:, :left_len, :comps]]
    if slot_len > left_len:
        parts.append(tiles[:, : slot_len - left_len, comps:])
    both = jnp.concatenate(parts, axis=1) if len(parts) > 1 else parts[0]
    return both.reshape(tiles.shape[0] * slot_len, comps)


def boundary_kernel(slot_len, own_rows, trace_ref, matrix_ref, out_ref):
    if len(trace_ref.shape) == 3:
        traces = unpack_tiles(
            trace_ref[...].astype(jnp.float32), slot_len, trace_ref.shape[2] // 2
        )
    else:
        traces = trace_ref[...].astype(jnp.float32)
    comps = traces.shape[1]
    angles = comps // 2
    turned = jnp.concatenate([-traces[:, angles:], traces[:, :angles]], axis=1)
    image = jnp.dot(
        matrix_ref[0], traces.astype(jnp.bfloat16), preferred_element_type=jnp.float32
    ) + jnp.dot(matrix_ref[1], turned.astype(jnp.bfloat16), preferred_element_type=jnp.float32)
    image = image.reshape(image.shape[0] // own_rows, own_rows, comps)
    half = own_rows // 2
    out_ref[...] = jnp.concatenate([image[:, :half], image[:, half:]], axis=2)


def sum_kernel(part_ref, out_ref):
    total = jnp.sum(part_ref[...], axis=0)
    half, lanes = total.shape
    out_ref[:half] = total[:, : lanes // 2]
    out_ref[half:] = total[:, lanes // 2 :]


def volume_kernel(dims, row_swaps, *refs):
    comps, width_x, width_y, depth, rows, cols = dims
    field_ref, medium_ref, flux_ref, cell_ref = refs[:4]
    row_refs = refs[4 : 4 + row_swaps]
    first_ref, second_ref = refs[4 + row_swaps : 6 + row_swaps]
    out_ref, lhs_ref, taken_ref = refs[6 + row_swaps :]
    lines = width_x * width_y
    nodes = cell_ref.shape[1]
    cells = cell_ref[...]
    hot = one_hot_depth(cells, depth)
    at_line = lax.broadcasted_iota(jnp.int32, (lines, nodes), 0)
    line_hot = jnp.where(at_line == line_of(cells, depth), 1.0, 0.0)

    for comp in range(comps):
        lhs_ref[pl.ds(comp * lines, lines), :] = (
            line_hot * jnp.broadcast_to(flux_ref[pl.ds(comp, 1), :], (lines, nodes))
        ).astype(jnp.bfloat16)
    chunk = 8 * lines

    def scatter(step, carry):
        here = pl.ds(pl.multiple_of(step * chunk, chunk), chunk)
        taken_ref[here, :] = lax.dot_general(
            lhs_ref[here, :], hot, (((1,), (1,)), ((), ())), preferred_element_type=jnp.float32
        )
        return carry

    lax.fori_loop(0, comps * lines // chunk, scatter, 0)

    row_odd = lax.rem(lax.axis_index("row"), 2) == 1
    col_odd = lax.rem(lax.axis_index("col"), 2) == 1
    shape = (width_y, depth)
    at_y = lax.broadcasted_iota(jnp.int32, shape, 0)
    at_z = lax.broadcasted_iota(jnp.int32, shape, 1)
    low_y, high_y = at_y == 0, at_y == width_y - 1
    low_z, high_z = at_z == 0, at_z == depth - 1
    weight = [1.0 / 12.0 + medium_ref[pl.ds(x * width_y, width_y), :] / 27.0 for x in range(width_x)]
    from_first = jnp.logical_or(
        jnp.logical_and(high_y, jnp.logical_not(row_odd)), jnp.logical_and(low_y, row_odd)
    )
    at_end = jnp.logical_or(low_y, high_y)

    def side_z(values):
        lower = jnp.where(low_z, 0.0, pltpu.roll(values, 1, 1))
        upper = jnp.where(high_z, 0.0, pltpu.roll(values, depth - 1, 1))
        return lower + upper

    def side_y(values, ends):
        lower = jnp.where(low_y, ends, pltpu.roll(values, 1, 0))
        upper = jnp.where(high_y, ends, pltpu.roll(values, width_y - 1, 0))
        return lower + upper

    def wide(ref, index):
        return jnp.broadcast_to(ref[pl.ds(index, 1), :], shape)

    def ends_of(first, second):
        if second is None:
            return jnp.where(from_first, first, 0.0)
        return jnp.where(from_first, first, second)

    def component(comp, carry):
        base = comp * lines
        planes = [
            field_ref[pl.ds(pl.multiple_of(base + x * width_y, width_y), width_y), :]
            for x in range(width_x)
        ]
        face = pl.ds(pl.multiple_of(comp * width_y, width_y), width_y)
        first, second = first_ref[face, :], second_ref[face, :]
        planes = (
            [jnp.where(col_odd, first, second)] + planes + [jnp.where(col_odd, second, first)]
        )
        ends = []
        tail = comps * width_y
        for index in range(row_swaps):
            inner = [wide(row_refs[index], comp * width_x + x) for x in range(width_x)]
            corner_first = wide(first_ref, tail + index * comps + comp)
            corner_second = wide(second_ref, tail + index * comps + comp)
            ends.append(
                [jnp.where(col_odd, corner_first, corner_second)]
                + inner
                + [jnp.where(col_odd, corner_second, corner_first)]
            )
        ends = [
            ends_of(ends[0][x], ends[1][x] if row_swaps > 1 else None) for x in range(width_x + 2)
        ]
        for x in range(width_x):
            centre = planes[x + 1]
            sides = planes[x] + planes[x + 2]
            over_x = 2.0 * centre + sides
            ends_x = 2.0 * ends[x + 1] + (ends[x] + ends[x + 2])
            over_xy = 2.0 * over_x + side_y(over_x, ends_x)
            over_xyz = 2.0 * over_xy + side_z(over_xy)
            near = sides + side_y(centre, ends[x + 1]) + side_z(centre)
            here = pl.ds(pl.multiple_of(base + x * width_y, width_y), width_y)
            out_ref[here, :] = (
                (10.0 / 3.0) * centre
                + (1.0 / 3.0) * near
                - weight[x] * over_xyz
                - taken_ref[here, :]
            )
        return carry

    lax.fori_loop(0, comps, component, 0, unroll=4)


def swap_pairs(count, swap):
    pairs = []
    for low in range(swap, count - 1, 2):
        pairs += [(low, low + 1), (low + 1, low)]
    return pairs


def on_device(wave_field, medium_term, node_flux, node_cell, block_target, boundary_matrix):
    comps, width_x, width_y, depth = wave_field.shape
    rows, cols = lax.axis_size("row"), lax.axis_size("col")
    dims = (comps, width_x, width_y, depth, rows, cols)
    lines = width_x * width_y
    nodes = node_cell.shape[-1]
    slot_len = nodes // cols
    row_swaps = 1 if rows == 2 else 2
    slab_rows, span = boundary_matrix.shape[1:]
    own_rows = slab_rows // cols
    f32, bf16 = jnp.float32, jnp.bfloat16
    params = pltpu.CompilerParams(vmem_limit_bytes=SMALL)

    field = wave_field.reshape(comps * lines, depth)
    cells = node_cell.reshape(1, nodes)
    targets = block_target.reshape(1, cols)
    flux = node_flux.reshape(comps, nodes)
    medium = medium_term.reshape(lines, depth)

    tiles, *faces = pl.pallas_call(
        functools.partial(trace_kernel, dims),
        out_shape=[jax.ShapeDtypeStruct((rows * cols, TILE_ROWS, 2 * comps), bf16)]
        + [jax.ShapeDtypeStruct((comps * width_x, depth), f32)] * row_swaps,
        in_specs=[pl.BlockSpec(memory_space=pltpu.SMEM), vmem(), vmem()],
        out_specs=[vmem()] * (1 + row_swaps),
        scratch_shapes=[pltpu.VMEM((comps * lines, depth), bf16)],
        compiler_params=params,
        name="traces",
    )(targets, cells, field)

    row_sides = [
        lax.ppermute(face, "row", swap_pairs(rows, swap)) for swap, face in enumerate(faces)
    ]
    received = lax.all_to_all(tiles, ("row", "col"), 0, 0, tiled=True)

    col_faces = pl.pallas_call(
        functools.partial(face_kernel, dims),
        out_shape=[jax.ShapeDtypeStruct((comps * (width_y + row_swaps), depth), f32)] * 2,
        in_specs=[vmem()] * (1 + row_swaps),
        out_specs=[vmem()] * 2,
        compiler_params=params,
        name="faces",
    )(field, *row_sides)
    col_sides = [
        lax.ppermute(face, "col", swap_pairs(cols, swap)) for swap, face in enumerate(col_faces)
    ]

    if slot_len % 8:
        received = unpack_tiles(received, slot_len, comps)
    shares = pl.pallas_call(
        functools.partial(boundary_kernel, slot_len, own_rows),
        out_shape=jax.ShapeDtypeStruct((cols, own_rows // 2, 2 * comps), f32),
        in_specs=[vmem()] * 2,
        out_specs=vmem(),
        compiler_params=pltpu.CompilerParams(vmem_limit_bytes=2 * SMALL),
        name="boundary",
    )(received, boundary_matrix)
    shares = lax.all_to_all(shares, "col", 0, 0, tiled=True)

    volume = pl.pallas_call(
        functools.partial(volume_kernel, dims, row_swaps),
        out_shape=jax.ShapeDtypeStruct((comps * lines, depth), f32),
        in_specs=[vmem()] * (6 + row_swaps),
        out_specs=vmem(),
        scratch_shapes=[
            pltpu.VMEM((comps * lines, nodes), bf16),
            pltpu.VMEM((comps * lines, depth), f32),
        ],
        compiler_params=params,
        name="volume",
    )(field, medium, flux, cells, *row_sides, *col_sides)

    boundary_image = pl.pallas_call(
        sum_kernel,
        out_shape=jax.ShapeDtypeStruct((own_rows, comps), f32),
        in_specs=[vmem()],
        out_specs=vmem(),
        compiler_params=params,
        name="sum",
    )(shares)
    return (volume.reshape(comps, width_x, width_y, depth), boundary_image)


def solution(mesh):
    in_specs = (
        P(None, "col", "row", None),
        P("col", "row", None),
        P(None, "col", "row", None),
        P("col", "row", None),
        P("col", "row", None),
        P(None, "row", "col"),
    )
    out_specs = (P(None, "col", "row", None), P(("row", "col"), None))
    return jax.shard_map(
        on_device, mesh=mesh, in_specs=in_specs, out_specs=out_specs, check_vma=False
    )
```

time: 110 us -> 40.4 us (0.37)
  waiting for transfers between devices: 39.1 us -> 8.02 us
  other arithmetic: 15.5 us -> 0 us
  between operations: 14.3 us -> 0.75 us
  local copies, waits for them, and re-layouts: 16 us -> 3.99 us
  Pallas kernels: 0 us -> 10.2 us
  blocking collectives: 5.29 us -> 0 us
  starting transfers between devices: 19 us -> 17.1 us
    unnamed x2 -> x0, waiting for transfers between devices: 32.5 us -> none
    pallas_call x0 -> x5, Pallas kernels: none -> 10.2 us  [the longest x1 5.36 us: on_device(): pl.pallas_call(functools.partial(volume_kernel, dims, row_swaps), out_sha...]
    ppermute x4 -> x3, starting transfers between devices: 11.9 us -> 2.58 us  [the longest x1 1.83 us: on_device(): lax.ppermute(face, 'row', swap_pairs(rows, swap))]
    all_to_all x1 -> x2, starting transfers between devices: 7.09 us -> 14.5 us  [the longest x1 7.3 us: on_device(): received = lax.all_to_all(tiles, ('row', 'col'), 0, 0, tiled=True)]
    add x3 -> x0, other arithmetic: 6.45 us -> none  [three_tap(): return side_weight * (lower + upper) + centre_weight * middle]
    scatter-add x1 -> x0, other arithmetic: 5.32 us -> none  [on_device(): flat_image.at[:, node_cell.reshape(node_total)]]
    all_gather x1 -> x0, blocking collectives: 5.29 us -> none  [on_device(): column_traces = lax.all_gather(received, 'row', axis=1, tiled=True)]
    ppermute x4 -> x3, waiting for transfers between devices: 0.14 us -> 5.08 us  [the longest x1 5.08 us: on_device(): lax.ppermute(face, 'row', swap_pairs(rows, swap))]
  transfers between devices with their start and end apart: 6 -> 5, of which waited for: 3 -> 3; matrix products, arithmetic and copies ran while one was open for 25% -> 0% of each run, Pallas kernels for 0% -> 17%
where the time goes in v1:
time: 40.4 us; the launch traced here: 40 us
  starting transfers between devices  17.1 us (42%)
  Pallas kernels  10.2 us (25%)
  waiting for transfers between devices  8.02 us (20%)
  local copies, waits for them, and re-layouts  3.99 us (10%)
  between operations  0.75 us (2%)
    all_to_all x1, starting transfers between devices, on_device(): received = lax.all_to_all(tiles, ('row', 'col'), 0, 0, tiled=True)  7.3 us
    all_to_all x1, starting transfers between devices, on_device(): shares = lax.all_to_all(shares, 'col', 0, 0, tiled=True)  7.21 us
    pallas_call x1, Pallas kernels, on_device(): pl.pallas_call(functools.partial(volume_kernel, dims, row_swaps), out_sha...  5.36 us
    ppermute x1, waiting for transfers between devices, on_device(): lax.ppermute(face, 'row', swap_pairs(rows, swap))  5.08 us
    unnamed x17, local copies, waits for them, and re-layouts  3.99 us
    pallas_call x1, Pallas kernels, on_device(): pl.pallas_call(functools.partial(trace_kernel, dims), out_shape=[jax.Shap...  2.61 us
    all_to_all x1, waiting for transfers between devices, on_device(): shares = lax.all_to_all(shares, 'col', 0, 0, tiled=True)  2.51 us
    ppermute x1, starting transfers between devices, on_device(): lax.ppermute(face, 'row', swap_pairs(rows, swap))  1.83 us
  transfers between devices with their start and end apart: 5, of which 3 were waited for; matrix products, arithmetic and copies ran while one was open for 0% of the time, Pallas kernels for 17%

profile of v1, /device:TPU:0, one launch (start us, length us, event | category | flops | bytes accessed | tf_op | source)
XLA Modules:
  0.0 40.0 jit_solution(4094509824522881400)
XLA Ops:
  0.6 0.0 copy-start
  0.6 1.2 %copy-done = f32[64,4,8,128]{3,2,1,0:T(8,128)S(1)} copy-done((f32[64,4,8,128]{3,2,1,0:T(8,128)S(1)}, f32[64,4,8,128]{3,2,1,0:T(8,128)}, u32[]{:S(2)}) %copy-start) | copy-done | bytes 1048600
  1.9 0.0 copy-start.4
  1.9 0.7 %copy-done.4 = s32[1,1,384]{2,1,0:T(1,128)S(1)} copy-done((s32[1,1,384]{2,1,0:T(1,128)S(1)}, s32[1,1,384]{2,1,0:T(1,128)}, u32[]{:S(2)}) %copy-start.4) | copy-done | bytes 1560
  2.5 0.0 copy-start.6
  2.5 0.7 %copy-done.6 = s32[1,1,16]{2,1,0:T(1,128)S(1)} copy-done((s32[1,1,16]{2,1,0:T(1,128)S(1)}, s32[1,1,16]{2,1,0:T(1,128)}, u32[]{:S(2)}) %copy-start.6) | copy-done | bytes 88
  3.2 0.0 copy-start.1
  3.2 2.6 %traces.1 = (bf16[32,16,128]{2,1,0:T(8,128)(2,1)}, f32[256,128]{1,0:T(8,128)S(1)}) custom-call(s32[1,16]{1,0:T(1,128)S(1)} %bitcast.15, s32[1,384]{1,0:T(1,128)S(1)} %bitcast.13, f32[2048,128]{1,0:T(8,128)S(1)} %bitcast.8), custom_call_target="tpu_custom_call" | custom-call | tf_op jit(solution)/shard_map/traces/pallas_call | solution.py:253
  5.8 7.3 %all-to-all-start = ((bf16[32,16,128]{2,1,0:T(8,128)(2,1)}), bf16[32,16,128]{2,1,0:T(8,128)(2,1)S(1)}, u32[]{:S(2)}, u32[]{:S(2)}) async-start(bf16[32,16,128]{2,1,0:T(8,128)(2,1)} %get-tuple-element.9), calls=%async_computation | async-start | bytes 262144 | tf_op jit(solution)/shard_map/all_to_all | solution.py:267
  13.1 0.0 copy-start.7
  13.1 0.0 copy-start.3
  13.1 0.0 copy-start.5
  13.1 1.8 %collective-permute-start = (f32[256,128]{1,0:T(8,128)S(1)}, f32[256,128]{1,0:T(8,128)S(1)}, u32[]{:S(2)}, u32[]{:S(2)}) collective-permute-start(f32[256,128]{1,0:T(8,128)S(1)} %get-tuple-element.6), channel_id=1, source_target_pairs={{0,16},{16,0},{1,17},{17,1},{2,18},{18,2},{3,19},{19,3},{4,20},{20... | collective-permute-start | bytes 393224 | tf_op jit(solution)/shard_map/ppermute | solution.py:265
  15.0 5.1 %collective-permute-done.refs_1_.refs_4_ = f32[256,128]{1,0:T(8,128)S(1)} collective-permute-done((f32[256,128]{1,0:T(8,128)S(1)}, f32[256,128]{1,0:T(8,128)S(1)}, u32[]{:S(2)}, u32[]{:S(2)}) %collective-permute-start) | collective-permute-done | bytes 131104 | tf_op jit(solution)/shard_map/ppermute | solution.py:265
  20.1 0.0 copy-done.1
  20.1 0.1 faces.1
  20.1 0.1 collective-permute-start.1
  20.2 0.7 %collective-permute-start.2 = (f32[576,128]{1,0:T(8,128)S(1)}, f32[576,128]{1,0:T(8,128)S(1)}, u32[]{:S(2)}, u32[]{:S(2)}) collective-permute-start(f32[576,128]{1,0:T(8,128)S(1)} %get-tuple-element.8), channel_id=1, source_target_pairs={{1,2},{2,1},{3,4},{4,3},{5,6},{6,5},{7,8},{8,7},{9,10},{10,9},{11,... | collective-permute-start | bytes 884744 | tf_op jit(solution)/shard_map/ppermute | solution.py:278
  20.9 0.4 %all-to-all-done.trace_ref = bf16[32,16,128]{2,1,0:T(8,128)(2,1)S(1)} async-done(((bf16[32,16,128]{2,1,0:T(8,128)(2,1)}), bf16[32,16,128]{2,1,0:T(8,128)(2,1)S(1)}, u32[]{:S(2)}, u32[]{:S(2)}) %all-to-all-start) | async-done | bytes 131104 | tf_op jit(solution)/shard_map/all_to_all | solution.py:267
  21.3 0.0 copy-start.2
  21.3 1.4 %copy-done.2 = bf16[2,512,768]{2,1,0:T(8,128)(2,1)S(1)} copy-done((bf16[2,512,768]{2,1,0:T(8,128)(2,1)S(1)}, bf16[2,512,768]{2,1,0:T(8,128)(2,1)}, u32[]{:S(2)}) %copy-start.2) | copy-done | bytes 1572888
  22.7 1.4 %boundary.1 = f32[16,16,128]{2,1,0:T(8,128)} custom-call(bf16[32,16,128]{2,1,0:T(8,128)(2,1)S(1)} %all-to-all-done.trace_ref, bf16[2,512,768]{2,1,0:T(8,128)(2,1)S(1)} %copy-done.2), custom_call_target="tpu_custom_call" | custom-call | tf_op jit(solution)/shard_map/boundary/pallas_call | solution.py:283
  24.2 7.2 %all-to-all-start.1 = ((f32[16,16,128]{2,1,0:T(8,128)}), f32[16,16,128]{2,1,0:T(8,128)S(1)}, u32[]{:S(2)}, u32[]{:S(2)}) async-start(f32[16,16,128]{2,1,0:T(8,128)} %boundary.1), calls=%async_computation.1 | async-start | bytes 262144 | tf_op jit(solution)/shard_map/all_to_all | solution.py:291
  31.4 0.0 copy-done.7
  31.4 0.0 collective-permute-done.1.refs_5_
  31.4 0.0 collective-permute-done.2.refs_6_
  31.4 0.0 copy-done.3
  31.4 0.0 copy-done.5
  31.5 5.4 %volume.1 = f32[2048,128]{1,0:T(8,128)} custom-call(f32[2048,128]{1,0:T(8,128)S(1)} %bitcast.10, f32[32,128]{1,0:T(8,128)S(1)} %bitcast.12, f32[64,384]{1,0:T(8,128)S(1)} %bitcast.11, s32[1,384]{1,0:T(1,128)S(1)} %bitcast.14, f32[256,128]{1,0:T(8,128)S(1)} %collective-permute-done.refs_1_.refs_4_, f32[576,128]{1,0:T(8,128)S(1)} %collective-permute-done.1.refs_5_, ...), custom_call_target="tpu_custom_call" | custom-call | tf_op jit(solution)/shard_map/volume/pallas_call | solution.py:293
  36.8 2.5 %all-to-all-done.1.part_ref = f32[16,16,128]{2,1,0:T(8,128)S(1)} async-done(((f32[16,16,128]{2,1,0:T(8,128)}), f32[16,16,128]{2,1,0:T(8,128)S(1)}, u32[]{:S(2)}, u32[]{:S(2)}) %all-to-all-start.1) | async-done | bytes 131104 | tf_op jit(solution)/shard_map/all_to_all | solution.py:291
  39.3 0.7 %sum.1 = f32[32,64]{1,0:T(8,128)} custom-call(f32[16,16,128]{2,1,0:T(8,128)S(1)} %all-to-all-done.1.part_ref), custom_call_target="tpu_custom_call" | custom-call | tf_op jit(solution)/shard_map/sum/pallas_call | solution.py:306
  (1 shorter events, 0.0 us)
Async XLA Ops:
  0.6 1.2 %copy-start = (f32[64,4,8,128]{3,2,1,0:T(8,128)S(1)}, f32[64,4,8,128]{3,2,1,0:T(8,128)}, u32[]{:S(2)}) copy-start(f32[64,4,8,128]{3,2,1,0:T(8,128)} %param.6) | copy-start | bytes 3145732
  1.9 0.7 %copy-start.4 = (s32[1,1,384]{2,1,0:T(1,128)S(1)}, s32[1,1,384]{2,1,0:T(1,128)}, u32[]{:S(2)}) copy-start(s32[1,1,384]{2,1,0:T(1,128)} %param.9) | copy-start | bytes 4612
  2.5 0.7 %copy-start.6 = (s32[1,1,16]{2,1,0:T(1,128)S(1)}, s32[1,1,16]{2,1,0:T(1,128)}, u32[]{:S(2)}) copy-start(s32[1,1,16]{2,1,0:T(1,128)} %param.10) | copy-start | bytes 196
  3.2 16.9 %copy-start.1 = (f32[64,4,8,128]{3,2,1,0:T(8,128)S(1)}, f32[64,4,8,128]{3,2,1,0:T(8,128)}, u32[]{:S(2)}) copy-start(f32[64,4,8,128]{3,2,1,0:T(8,128)} %param.6) | copy-start | bytes 3145732
  5.8 15.5 %all-to-all-start = ((bf16[32,16,128]{2,1,0:T(8,128)(2,1)}), bf16[32,16,128]{2,1,0:T(8,128)(2,1)S(1)}, u32[]{:S(2)}, u32[]{:S(2)}) async-start(bf16[32,16,128]{2,1,0:T(8,128)(2,1)} %get-tuple-element.9), calls=%async_computation | async-start | bytes 262144 | tf_op jit(solution)/shard_map/all_to_all | solution.py:267
  13.1 18.3 %copy-start.7 = (f32[64,1,1,384]{3,2,1,0:T(1,128)S(1)}, f32[64,1,1,384]{3,2,1,0:T(1,128)}, u32[]{:S(2)}) copy-start(f32[64,1,1,384]{3,2,1,0:T(1,128)} %param.8) | copy-start | bytes 294916
  13.1 18.3 %copy-start.3 = (f32[4,8,128]{2,1,0:T(8,128)S(1)}, f32[4,8,128]{2,1,0:T(8,128)}, u32[]{:S(2)}) copy-start(f32[4,8,128]{2,1,0:T(8,128)} %param.7) | copy-start | bytes 49156
  13.1 18.3 %copy-start.5 = (s32[1,1,384]{2,1,0:T(1,128)S(1)}, s32[1,1,384]{2,1,0:T(1,128)}, u32[]{:S(2)}) copy-start(s32[1,1,384]{2,1,0:T(1,128)} %param.9) | copy-start | bytes 4612
  13.1 6.9 %collective-permute-start = (f32[256,128]{1,0:T(8,128)S(1)}, f32[256,128]{1,0:T(8,128)S(1)}, u32[]{:S(2)}, u32[]{:S(2)}) collective-permute-start(f32[256,128]{1,0:T(8,128)S(1)} %get-tuple-element.6), channel_id=1, source_target_pairs={{0,16},{16,0},{1,17},{17,1},{2,18},{18,2},{3,19},{19,3},{4,20},{20... | collective-permute-start | bytes 393224 | tf_op jit(solution)/shard_map/ppermute | solution.py:265
  20.1 11.3 %collective-permute-start.1 = (f32[576,128]{1,0:T(8,128)S(1)}, f32[576,128]{1,0:T(8,128)S(1)}, u32[]{:S(2)}, u32[]{:S(2)}) collective-permute-start(f32[576,128]{1,0:T(8,128)S(1)} %get-tuple-element.7), channel_id=1, source_target_pairs={{0,1},{1,0},{2,3},{3,2},{4,5},{5,4},{6,7},{7,6},{8,9},{9,8},{10,11... | collective-permute-start | bytes 884744 | tf_op jit(solution)/shard_map/ppermute | solution.py:278
  20.2 11.2 %collective-permute-start.2 = (f32[576,128]{1,0:T(8,128)S(1)}, f32[576,128]{1,0:T(8,128)S(1)}, u32[]{:S(2)}, u32[]{:S(2)}) collective-permute-start(f32[576,128]{1,0:T(8,128)S(1)} %get-tuple-element.8), channel_id=1, source_target_pairs={{1,2},{2,1},{3,4},{4,3},{5,6},{6,5},{7,8},{8,7},{9,10},{10,9},{11,... | collective-permute-start | bytes 884744 | tf_op jit(solution)/shard_map/ppermute | solution.py:278
  21.3 1.4 %copy-start.2 = (bf16[2,512,768]{2,1,0:T(8,128)(2,1)S(1)}, bf16[2,512,768]{2,1,0:T(8,128)(2,1)}, u32[]{:S(2)}) copy-start(bf16[2,512,768]{2,1,0:T(8,128)(2,1)} %matrix_ref.1) | copy-start | bytes 4718596
  24.2 15.2 %all-to-all-start.1 = ((f32[16,16,128]{2,1,0:T(8,128)}), f32[16,16,128]{2,1,0:T(8,128)S(1)}, u32[]{:S(2)}, u32[]{:S(2)}) async-start(f32[16,16,128]{2,1,0:T(8,128)} %boundary.1), calls=%async_computation.1 | async-start | bytes 262144 | tf_op jit(solution)/shard_map/all_to_all | solution.py:291

commit v2 on v1

v2 whole, which is shorter than its diff:
```python
import functools

import jax
import jax.numpy as jnp
from jax import lax
from jax.experimental import pallas as pl
from jax.experimental.pallas import tpu as pltpu
from jax.sharding import PartitionSpec as P

TILE_ROWS = 16
SMALL = 8 * 2**20
WHOLE = 64560 * 2**10


def vmem():
    return pl.BlockSpec(memory_space=pltpu.VMEM)


def hbm():
    return pl.BlockSpec(memory_space=pltpu.HBM)


def one_hot_depth(cells, depth):
    lanes = jnp.bitwise_and(cells, depth - 1)
    at = lax.broadcasted_iota(jnp.int32, (depth, cells.shape[1]), 0)
    return jnp.where(at == lanes, 1.0, 0.0).astype(jnp.bfloat16)


def line_of(cells, depth):
    return jnp.right_shift(cells, depth.bit_length() - 1)


def trace_kernel(dims, row_swaps, target_hbm, cell_hbm, field_hbm, tile_ref, *rest):
    comps, width_x, width_y, depth, rows, cols = dims
    row_faces, col_faces = rest[:row_swaps], rest[row_swaps : row_swaps + 2]
    target_ref, cell_ref, field_ref, lhs_ref, arrived, left_sem = rest[row_swaps + 2 :]
    lines = width_x * width_y
    nodes = cell_ref.shape[1]
    slot_len = nodes // cols
    copies = [
        pltpu.make_async_copy(source, target, arrived.at[index])
        for index, (source, target) in enumerate(
            [(cell_hbm, cell_ref), (field_hbm, field_ref), (target_hbm, target_ref)]
        )
    ]
    for copy in copies:
        copy.start()
    copies[0].wait()
    cells = cell_ref[...]
    hot = one_hot_depth(cells, depth)
    node_line = jnp.broadcast_to(line_of(cells, depth), (8, nodes))
    copies[1].wait()
    col_odd = lax.rem(lax.axis_index("col"), 2)
    sent = []
    for swap, face_ref in enumerate(col_faces):
        layer = jnp.where(col_odd == swap, width_x - 1, 0)
        start = pl.multiple_of(layer * width_y, width_y)
        sent.append(
            pltpu.make_async_copy(
                field_ref.at[:, pl.ds(start, width_y), :], face_ref, left_sem.at[swap]
            )
        )
        sent[-1].start()
    flat = field_ref.reshape(comps * lines, depth)
    for line in range(lines):
        lhs_ref[pl.ds(line * comps, comps), :] = flat[
            pl.ds(line, comps, stride=lines), :
        ].astype(jnp.bfloat16)
    total = jnp.zeros((comps // 8, 8, nodes), jnp.float32)
    group = 4
    for first in range(0, lines, group):
        block = jnp.dot(
            lhs_ref[pl.ds(first * comps, group * comps), :], hot, preferred_element_type=jnp.float32
        ).reshape(group, comps // 8, 8, nodes)
        for line in range(group):
            total = jnp.where((node_line == first + line)[None], block[line], total)
    by_node = total.reshape(comps, nodes).T
    copies[2].wait()
    left_len = min(slot_len, TILE_ROWS)
    for slot in range(cols):
        piece = by_node[slot * slot_len : (slot + 1) * slot_len]
        left = piece[:left_len]
        right = piece[left_len:]
        if left_len < TILE_ROWS:
            left = jnp.concatenate(
                [left, jnp.zeros((TILE_ROWS - left_len, comps), jnp.float32)], axis=0
            )
        gap = TILE_ROWS - (slot_len - left_len)
        if slot_len == left_len:
            right = jnp.zeros((TILE_ROWS, comps), jnp.float32)
        elif gap:
            right = jnp.concatenate([right, jnp.zeros((gap, comps), jnp.float32)], axis=0)
        tile = jnp.concatenate([left, right], axis=1).astype(jnp.bfloat16)
        for row in range(rows):
            tile_ref[row * cols + target_ref[0, slot]] = tile
    row_odd = lax.rem(lax.axis_index("row"), 2)
    for swap, face_ref in enumerate(row_faces):
        layer = jnp.where(row_odd == swap, width_y - 1, 0)
        face_ref[...] = flat[pl.ds(layer, comps * width_x, stride=width_y), :]
    for copy in sent:
        copy.wait()


def corner_kernel(dims, row_swaps, *refs):
    comps, width_x = dims[:2]
    odd = lax.rem(lax.axis_index("col"), 2)
    for swap, out_ref in enumerate(refs[row_swaps:]):
        layer = jnp.where(odd == swap, width_x - 1, 0)
        for index, row_ref in enumerate(refs[:row_swaps]):
            out_ref[pl.ds(index * comps, comps), :] = row_ref[
                pl.ds(layer, comps, stride=width_x), :
            ]


def unpack_tiles(tiles, slot_len, comps):
    left_len = min(slot_len, TILE_ROWS)
    parts = [tiles[:, :left_len, :comps]]
    if slot_len > left_len:
        parts.append(tiles[:, : slot_len - left_len, comps:])
    both = jnp.concatenate(parts, axis=1) if len(parts) > 1 else parts[0]
    return both.reshape(tiles.shape[0] * slot_len, comps)


def boundary_kernel(slot_len, own_rows, trace_ref, real_ref, imag_ref, corner_ref, out_ref):
    if len(trace_ref.shape) == 3:
        traces = unpack_tiles(
            trace_ref[...].astype(jnp.float32), slot_len, trace_ref.shape[2] // 2
        )
    else:
        traces = trace_ref[...].astype(jnp.float32)
    comps = traces.shape[1]
    angles = comps // 2
    turned = jnp.concatenate([-traces[:, angles:], traces[:, :angles]], axis=1)
    image = jnp.dot(
        real_ref[...], traces.astype(jnp.bfloat16), preferred_element_type=jnp.float32
    ) + jnp.dot(imag_ref[...], turned.astype(jnp.bfloat16), preferred_element_type=jnp.float32)
    image = image.reshape(image.shape[0] // own_rows, own_rows, comps)
    half = own_rows // 2
    out_ref[...] = jnp.concatenate([image[:, :half], image[:, half:]], axis=2)


def shifted_z(values, step):
    rows, depth = values.shape
    at_z = lax.broadcasted_iota(jnp.int32, (rows, depth), 1)
    outside = at_z == (0 if step == 1 else depth - 1)
    return jnp.where(outside, 0.0, pltpu.roll(values, step % depth, 1))


def side_z(values):
    return shifted_z(values, 1) + shifted_z(values, -1)


def volume_kernel(dims, row_swaps, *refs):
    comps, width_x, width_y, depth, rows, cols = dims
    field_ref, medium_ref, flux_ref, cell_ref = refs[:4]
    row_refs = refs[4 : 4 + row_swaps]
    first_ref, second_ref = refs[4 + row_swaps : 6 + row_swaps]
    out_ref, edge_ref, lhs_ref, taken_ref = refs[6 + row_swaps :]
    lines = width_x * width_y
    nodes = cell_ref.shape[1]
    cells = cell_ref[...]
    hot = one_hot_depth(cells, depth)
    at_line = lax.broadcasted_iota(jnp.int32, (lines, nodes), 0)
    line_hot = jnp.where(at_line == line_of(cells, depth), 1.0, 0.0)

    for comp in range(comps):
        lhs_ref[pl.ds(comp * lines, lines), :] = (
            line_hot * jnp.broadcast_to(flux_ref[pl.ds(comp, 1), :], (lines, nodes))
        ).astype(jnp.bfloat16)
    taken_ref[...] = lax.dot_general(
        lhs_ref[...], hot, (((1,), (1,)), ((), ())), preferred_element_type=jnp.float32
    )

    row_odd = lax.rem(lax.axis_index("row"), 2) == 1
    col_odd = lax.rem(lax.axis_index("col"), 2) == 1
    shape = (width_y, depth)
    at_y = lax.broadcasted_iota(jnp.int32, shape, 0)
    low_y, high_y = at_y == 0, at_y == width_y - 1
    weight = [1.0 / 12.0 + medium_ref[pl.ds(x * width_y, width_y), :] / 27.0 for x in range(width_x)]
    from_first = jnp.logical_or(
        jnp.logical_and(high_y, jnp.logical_not(row_odd)), jnp.logical_and(low_y, row_odd)
    )

    def side_y(values, ends):
        lower = jnp.where(low_y, ends, pltpu.roll(values, 1, 0))
        upper = jnp.where(high_y, ends, pltpu.roll(values, width_y - 1, 0))
        return lower + upper

    def wide(ref, index):
        return jnp.broadcast_to(ref[pl.ds(index, 1), :], shape)

    def component(comp):
        base = comp * lines
        planes = [
            field_ref[pl.ds(pl.multiple_of(base + x * width_y, width_y), width_y), :]
            for x in range(width_x)
        ]
        face = pl.ds(pl.multiple_of(comp * width_y, width_y), width_y)
        first, second = first_ref[face, :], second_ref[face, :]
        planes = (
            [jnp.where(col_odd, first, second)] + planes + [jnp.where(col_odd, second, first)]
        )
        ends = []
        for x in range(width_x):
            line = [wide(row_ref, comp * width_x + x) for row_ref in row_refs]
            ends.append(jnp.where(from_first, line[0], line[1] if row_swaps > 1 else 0.0))
        none = jnp.zeros(shape, jnp.float32)
        ends = [none] + ends + [none]
        for x in range(width_x):
            centre = planes[x + 1]
            sides = planes[x] + planes[x + 2]
            over_x = 2.0 * centre + sides
            ends_x = 2.0 * ends[x + 1] + (ends[x] + ends[x + 2])
            over_xy = 2.0 * over_x + side_y(over_x, ends_x)
            over_xyz = 2.0 * over_xy + side_z(over_xy)
            near = sides + side_y(centre, ends[x + 1]) + side_z(centre)
            here = pl.ds(pl.multiple_of(base + x * width_y, width_y), width_y)
            image = (
                (10.0 / 3.0) * centre
                + (1.0 / 3.0) * near
                - weight[x] * over_xyz
                - taken_ref[here, :]
            )
            out_ref[here, :] = image
            for side in range(2):
                if x == side * (width_x - 1):
                    edge_ref[side, face, :] = image

    together = 16

    def components(step, carry):
        for index in range(together):
            component(step * together + index)
        return carry

    lax.fori_loop(0, comps // together, components, 0)


def last_kernel(
    dims, row_swaps, part_ref, medium_ref, edge_ref, first_ref, second_ref, *refs
):
    comps, width_x, width_y, depth, rows, cols = dims
    image_ref, volume_ref, plane_ref, total_ref, sent = refs[1:]
    row_odd = lax.rem(lax.axis_index("row"), 2)
    col_odd = lax.rem(lax.axis_index("col"), 2) == 1
    copies = []
    for side in range(2):
        at_x = side * (width_x - 1)
        plane_ref[side] = edge_ref[side]
        for index in range(row_swaps):
            lines = pl.ds(index * comps, comps)
            first, second = first_ref[lines, :], second_ref[lines, :]
            if side:
                line = jnp.where(col_odd, second, first)
            else:
                line = jnp.where(col_odd, first, second)
            at_y = jnp.where(row_odd == index, width_y - 1, 0)
            weight = 1.0 / 12.0 + medium_ref[pl.ds(at_x * width_y + at_y, 1), :] / 27.0
            here = pl.ds(at_y, comps, stride=width_y)
            plane_ref[side, here, :] = plane_ref[side, here, :] - weight * (
                2.0 * line + side_z(line)
            )
        copies.append(
            pltpu.make_async_copy(
                plane_ref.at[side].reshape(comps, width_y, depth),
                volume_ref.at[:, pl.ds(at_x * width_y, width_y), :],
                sent.at[side],
            )
        )
        copies[-1].start()
    total = jnp.sum(part_ref[...], axis=0)
    half, lanes = total.shape
    total_ref[:half] = total[:, : lanes // 2]
    total_ref[half:] = total[:, lanes // 2 :]
    copies.append(pltpu.make_async_copy(total_ref, image_ref, sent.at[2]))
    copies[-1].start()
    for copy in copies:
        copy.wait()


def swap_pairs(count, swap):
    pairs = []
    for low in range(swap, count - 1, 2):
        pairs += [(low, low + 1), (low + 1, low)]
    return pairs


def on_device(wave_field, medium_term, node_flux, node_cell, block_target, boundary_matrix):
    comps, width_x, width_y, depth = wave_field.shape
    rows, cols = lax.axis_size("row"), lax.axis_size("col")
    dims = (comps, width_x, width_y, depth, rows, cols)
    lines = width_x * width_y
    nodes = node_cell.shape[-1]
    slot_len = nodes // cols
    row_swaps = 1 if rows == 2 else 2
    slab_rows, span = boundary_matrix.shape[1:]
    own_rows = slab_rows // cols
    f32, bf16 = jnp.float32, jnp.bfloat16
    params = pltpu.CompilerParams(vmem_limit_bytes=SMALL)
    whole_params = pltpu.CompilerParams(vmem_limit_bytes=WHOLE)

    field = wave_field.reshape(comps * lines, depth)
    cells = node_cell.reshape(1, nodes)
    targets = block_target.reshape(1, cols)
    flux = node_flux.reshape(comps, nodes)
    medium = medium_term.reshape(lines, depth)

    tiles, *faces = pl.pallas_call(
        functools.partial(trace_kernel, dims, row_swaps),
        out_shape=[jax.ShapeDtypeStruct((rows * cols, TILE_ROWS, 2 * comps), bf16)]
        + [jax.ShapeDtypeStruct((comps * width_x, depth), f32)] * row_swaps
        + [jax.ShapeDtypeStruct((comps, width_y, depth), f32)] * 2,
        in_specs=[hbm()] * 3,
        out_specs=[vmem()] * (1 + row_swaps) + [hbm()] * 2,
        scratch_shapes=[
            pltpu.SMEM((1, cols), jnp.int32),
            pltpu.VMEM((1, nodes), jnp.int32),
            pltpu.VMEM((comps, lines, depth), f32),
            pltpu.VMEM((comps * lines, depth), bf16),
            pltpu.SemaphoreType.DMA((3,)),
            pltpu.SemaphoreType.DMA((2,)),
        ],
        compiler_params=whole_params,
        name="traces",
    )(targets, cells, field.reshape(comps, lines, depth))
    col_sides = [
        lax.ppermute(face, "col", swap_pairs(cols, swap)).reshape(comps * width_y, depth)
        for swap, face in enumerate(faces[row_swaps:])
    ]
    row_sides = [
        lax.ppermute(face, "row", swap_pairs(rows, swap))
        for swap, face in enumerate(faces[:row_swaps])
    ]
    received = lax.all_to_all(tiles, ("row", "col"), 0, 0, tiled=True)

    if slot_len % 8:
        received = unpack_tiles(received, slot_len, comps)
    corners = pl.pallas_call(
        functools.partial(corner_kernel, dims, row_swaps),
        out_shape=[jax.ShapeDtypeStruct((row_swaps * comps, depth), f32)] * 2,
        in_specs=[vmem()] * row_swaps,
        out_specs=[vmem()] * 2,
        compiler_params=params,
        name="corners",
    )(*row_sides)
    shares = pl.pallas_call(
        functools.partial(boundary_kernel, slot_len, own_rows),
        out_shape=jax.ShapeDtypeStruct((cols, own_rows // 2, 2 * comps), f32),
        in_specs=[vmem()] * 4,
        out_specs=vmem(),
        compiler_params=params,
        name="boundary",
    )(received, boundary_matrix[0], boundary_matrix[1], corners[0])
    corner_sides = [
        lax.ppermute(lines_of, "col", swap_pairs(cols, swap))
        for swap, lines_of in enumerate(corners)
    ]
    shares = lax.all_to_all(shares, "col", 0, 0, tiled=True)

    volume, edges = pl.pallas_call(
        functools.partial(volume_kernel, dims, row_swaps),
        out_shape=[
            jax.ShapeDtypeStruct((comps * lines, depth), f32),
            jax.ShapeDtypeStruct((2, comps * width_y, depth), f32),
        ],
        in_specs=[vmem()] * (6 + row_swaps),
        out_specs=[vmem()] * 2,
        scratch_shapes=[
            pltpu.VMEM((comps * lines, nodes), bf16),
            pltpu.VMEM((comps * lines, depth), f32),
        ],
        compiler_params=params,
        name="volume",
    )(field, medium, flux, cells, *row_sides, *col_sides)

    boundary_image, volume = pl.pallas_call(
        functools.partial(last_kernel, dims, row_swaps),
        out_shape=[
            jax.ShapeDtypeStruct((own_rows, comps), f32),
            jax.ShapeDtypeStruct((comps, lines, depth), f32),
        ],
        in_specs=[vmem()] * 5 + [hbm()],
        out_specs=[hbm(), hbm()],
        scratch_shapes=[
            pltpu.VMEM((2, comps * width_y, depth), f32),
            pltpu.VMEM((own_rows, comps), f32),
            pltpu.SemaphoreType.DMA((3,)),
        ],
        input_output_aliases={5: 1},
        compiler_params=params,
        name="last",
    )(shares, medium, edges, *corner_sides, volume.reshape(comps, lines, depth))
    return (volume.reshape(comps, width_x, width_y, depth), boundary_image)


def solution(mesh):
    in_specs = (
        P(None, "col", "row", None),
        P("col", "row", None),
        P(None, "col", "row", None),
        P("col", "row", None),
        P("col", "row", None),
        P(None, "row", "col"),
    )
    out_specs = (P(None, "col", "row", None), P(("row", "col"), None))
    return jax.shard_map(
        on_device, mesh=mesh, in_specs=in_specs, out_specs=out_specs, check_vma=False
    )
```

time: 40.4 us -> 34.7 us (0.86)
  starting transfers between devices: 17.1 us -> 15.3 us
  local copies, waits for them, and re-layouts: 3.99 us -> 2.4 us
  Pallas kernels: 10.2 us -> 8.71 us
  waiting for transfers between devices: 8.02 us -> 7.24 us
    unnamed x17 -> x7, local copies, waits for them, and re-layouts: 3.99 us -> 0.92 us
    all_to_all x1, starting transfers between devices: 7.21 us -> 4.42 us  [on_device(): shares = lax.all_to_all(shares, 'col', 0, 0, tiled=True)]
    pallas_call x1, Pallas kernels: 5.36 us -> 2.97 us  [on_device(): pl.pallas_call(functools.partial(volume_kernel, dims, row_swaps), out_sha...]
    ppermute x1, waiting for transfers between devices: 5.08 us -> 3 us  [on_device(): lax.ppermute(face, 'row', swap_pairs(rows, swap))]
    squeeze x0 -> x1, local copies, waits for them, and re-layouts: none -> 1.48 us  [on_device(): boundary_matrix[1]]
    ppermute x0 -> x2, starting transfers between devices: none -> 1.06 us  [on_device(): lax.ppermute(lines_of, 'col', swap_pairs(cols, swap))]
    pallas_call x3, Pallas kernels: 3.37 us -> 4.32 us  [the longest x1 3.39 us: on_device(): pl.pallas_call(functools.partial(trace_kernel, dims, row_swaps), out_shap...]
    all_to_all x1, waiting for transfers between devices: 0.43 us -> 1.29 us  [on_device(): received = lax.all_to_all(tiles, ('row', 'col'), 0, 0, tiled=True)]
  transfers between devices with their start and end apart: 5 -> 7, of which waited for: 3 -> 3; matrix products, arithmetic and copies ran while one was open for 0% -> 7% of each run, Pallas kernels for 17% -> 13%
where the time goes in v2:
time: 34.7 us; the launch traced here: 34.4 us
  starting transfers between devices  15.3 us (44%)
  Pallas kernels  8.71 us (25%)
  waiting for transfers between devices  7.24 us (21%)
  local copies, waits for them, and re-layouts  2.4 us (7%)
  between operations  0.74 us (2%)
    all_to_all x1, starting transfers between devices, on_device(): received = lax.all_to_all(tiles, ('row', 'col'), 0, 0, tiled=True)  7.3 us
    all_to_all x1, starting transfers between devices, on_device(): shares = lax.all_to_all(shares, 'col', 0, 0, tiled=True)  4.42 us
    pallas_call x1, Pallas kernels, on_device(): pl.pallas_call(functools.partial(trace_kernel, dims, row_swaps), out_shap...  3.39 us
    ppermute x1, waiting for transfers between devices, on_device(): lax.ppermute(face, 'row', swap_pairs(rows, swap))  3 us
    pallas_call x1, Pallas kernels, on_device(): pl.pallas_call(functools.partial(volume_kernel, dims, row_swaps), out_sha...  2.97 us
    all_to_all x1, waiting for transfers between devices, on_device(): shares = lax.all_to_all(shares, 'col', 0, 0, tiled=True)  2.94 us
    ppermute x1, starting transfers between devices, on_device(): lax.ppermute(face, 'row', swap_pairs(rows, swap))  1.83 us
    squeeze x1, local copies, waits for them, and re-layouts, on_device(): boundary_matrix[1]  1.48 us
  transfers between devices with their start and end apart: 7, of which 3 were waited for; matrix products, arithmetic and copies ran while one was open for 7% of the time, Pallas kernels for 13%

profile of v2, /device:TPU:0, one launch (start us, length us, event | category | flops | bytes accessed | tf_op | source)
XLA Modules:
  0.0 34.4 jit_solution(15745276713153770934)
XLA Ops:
  0.6 3.4 %traces.1 = (bf16[32,16,128]{2,1,0:T(8,128)(2,1)}, f32[256,128]{1,0:T(8,128)}, f32[64,8,128]{2,1,0:T(8,128)}, f32[64,8,128]{2,1,0:T(8,128)}) custom-call(s32[1,16]{1,0:T(1,128)} %bitcast.27, s32[1,384]{1,0:T(1,128)} %bitcast.23, f32[64,32,128]{2,1,0:T(8,128)} %bitcast.16), custom_call_target="tpu_custom_call" | custom-call | tf_op jit(solution)/shard_map/traces/pallas_call | solution.py:308
  4.0 7.3 %all-to-all-start = ((bf16[32,16,128]{2,1,0:T(8,128)(2,1)}), bf16[32,16,128]{2,1,0:T(8,128)(2,1)S(1)}, u32[]{:S(2)}, u32[]{:S(2)}) async-start(bf16[32,16,128]{2,1,0:T(8,128)(2,1)} %get-tuple-element.12), calls=%async_computation | async-start | bytes 262144 | tf_op jit(solution)/shard_map/all_to_all | solution.py:334
  11.3 1.8 %collective-permute-start = (f32[256,128]{1,0:T(8,128)}, f32[256,128]{1,0:T(8,128)S(1)}, u32[]{:S(2)}, u32[]{:S(2)}) collective-permute-start(f32[256,128]{1,0:T(8,128)} %get-tuple-element.13), channel_id=1, source_target_pairs={{0,16},{16,0},{1,17},{17,1},{2,18},{18,2},{3,19},{19,3},{4,20},{20... | collective-permute-start | bytes 393224 | tf_op jit(solution)/shard_map/ppermute | solution.py:331
  13.2 0.0 collective-permute-start.1
  13.2 0.7 %collective-permute-start.2 = (f32[64,8,128]{2,1,0:T(8,128)}, f32[64,8,128]{2,1,0:T(8,128)S(1)}, u32[]{:S(2)}, u32[]{:S(2)}) collective-permute-start(f32[64,8,128]{2,1,0:T(8,128)} %get-tuple-element.16), channel_id=1, source_target_pairs={{1,2},{2,1},{3,4},{4,3},{5,6},{6,5},{7,8},{8,7},{9,10},{10,9},{11,... | collective-permute-start | bytes 786440 | tf_op jit(solution)/shard_map/ppermute | solution.py:327
  13.8 1.5 %slice_bitcast_fusion = (bf16[512,768]{1,0:T(8,128)(2,1)S(1)}, bf16[512,768]{1,0:T(8,128)(2,1)S(1)}) fusion(bf16[2,512,768]{2,1,0:T(8,128)(2,1)} %param.11), kind=kLoop, calls=%fused_computation | loop fusion | bytes 3145728 | tf_op jit(solution)/shard_map/squeeze | solution.py:353
  15.3 0.0 copy-start
  15.3 0.0 copy-start.1
  15.3 0.0 copy-start.2
  15.4 3.0 %collective-permute-done.refs_0_.refs_4_ = f32[256,128]{1,0:T(8,128)S(1)} collective-permute-done((f32[256,128]{1,0:T(8,128)}, f32[256,128]{1,0:T(8,128)S(1)}, u32[]{:S(2)}, u32[]{:S(2)}) %collective-permute-start) | collective-permute-done | bytes 131104 | tf_op jit(solution)/shard_map/ppermute | solution.py:331
  18.4 1.3 %all-to-all-done.trace_ref = bf16[32,16,128]{2,1,0:T(8,128)(2,1)S(1)} async-done(((bf16[32,16,128]{2,1,0:T(8,128)(2,1)}), bf16[32,16,128]{2,1,0:T(8,128)(2,1)S(1)}, u32[]{:S(2)}, u32[]{:S(2)}) %all-to-all-start) | async-done | bytes 131104 | tf_op jit(solution)/shard_map/all_to_all | solution.py:334
  19.7 1.4 %boundary.1 = f32[16,16,128]{2,1,0:T(8,128)} custom-call(bf16[32,16,128]{2,1,0:T(8,128)(2,1)S(1)} %all-to-all-done.trace_ref, bf16[512,768]{1,0:T(8,128)(2,1)S(1)} %get-tuple-element.23.real_ref, bf16[512,768]{1,0:T(8,128)(2,1)S(1)} %get-tuple-element.22.imag_ref, f32[64,128]{1,0:T(8,128)S(1)} %get-tuple-element.14.corner_ref), custom_call_target="tpu_custom_call" | custom-call | tf_op jit(solution)/shard_map/boundary/pallas_call | solution.py:346
  21.1 4.4 %all-to-all-start.1 = ((f32[16,16,128]{2,1,0:T(8,128)}), f32[16,16,128]{2,1,0:T(8,128)S(1)}, u32[]{:S(2)}, u32[]{:S(2)}) async-start(f32[16,16,128]{2,1,0:T(8,128)} %boundary.1), calls=%async_computation.1 | async-start | bytes 262144 | tf_op jit(solution)/shard_map/all_to_all | solution.py:358
  25.5 0.4 %collective-permute-start.3 = (f32[64,128]{1,0:T(8,128)S(1)}, f32[64,128]{1,0:T(8,128)S(1)}, u32[]{:S(2)}, u32[]{:S(2)}) collective-permute-start(f32[64,128]{1,0:T(8,128)S(1)} %get-tuple-element.14.corner_ref), channel_id=1, source_target_pairs={{0,1},{1,0},{2,3},{3,2},{4,5},{5,4},{6,7},{7,6},{8,9},{9,8},{10,11... | collective-permute-start | bytes 98312 | tf_op jit(solution)/shard_map/ppermute | solution.py:355
  25.9 0.7 %collective-permute-start.4 = (f32[64,128]{1,0:T(8,128)S(1)}, f32[64,128]{1,0:T(8,128)S(1)}, u32[]{:S(2)}, u32[]{:S(2)}) collective-permute-start(f32[64,128]{1,0:T(8,128)S(1)} %get-tuple-element.18), channel_id=1, source_target_pairs={{1,2},{2,1},{3,4},{4,3},{5,6},{6,5},{7,8},{8,7},{9,10},{10,9},{11,... | collective-permute-start | bytes 98312 | tf_op jit(solution)/shard_map/ppermute | solution.py:355
  26.6 0.9 %copy.11 = f32[64,1,1,384]{3,0,1,2:T(8,128)S(1)} copy(f32[64,1,1,384]{3,2,1,0:T(1,128)} %param.8) | data formatting | bytes 196608
  27.5 0.0 collective-permute-done.1
  27.5 0.0 collective-permute-done.2
  27.5 0.0 copy-done
  27.5 0.0 copy-done.1
  27.5 0.0 copy-done.2
  27.5 3.0 %volume.1 = (f32[2048,128]{1,0:T(8,128)}, f32[2,512,128]{2,1,0:T(8,128)S(1)}) custom-call(f32[2048,128]{1,0:T(8,128)S(1)} %bitcast.17, f32[32,128]{1,0:T(8,128)S(1)} %bitcast.21, f32[64,384]{1,0:T(8,128)S(1)} %bitcast.18, s32[1,384]{1,0:T(1,128)S(1)} %bitcast.24, f32[256,128]{1,0:T(8,128)S(1)} %collective-permute-done.refs_0_.refs_4_, ...), custom_call_target="tpu_custom_call" | custom-call | tf_op jit(solution)/shard_map/volume/pallas_call | solution.py:360
  30.5 0.0 collective-permute-done.3.first_ref
  30.5 0.0 collective-permute-done.4.second_ref
  30.5 2.9 %all-to-all-done.1.part_ref = f32[16,16,128]{2,1,0:T(8,128)S(1)} async-done(((f32[16,16,128]{2,1,0:T(8,128)}), f32[16,16,128]{2,1,0:T(8,128)S(1)}, u32[]{:S(2)}, u32[]{:S(2)}) %all-to-all-start.1) | async-done | bytes 131104 | tf_op jit(solution)/shard_map/all_to_all | solution.py:358
  33.4 0.9 %last.1 = (f32[32,64]{1,0:T(8,128)}, f32[64,32,128]{2,1,0:T(8,128)}) custom-call(f32[16,16,128]{2,1,0:T(8,128)S(1)} %all-to-all-done.1.part_ref, f32[32,128]{1,0:T(8,128)S(1)} %bitcast.22, f32[2,512,128]{2,1,0:T(8,128)S(1)} %get-tuple-element.17.edge_ref, f32[64,128]{1,0:T(8,128)S(1)} %collective-permute-done.3.first_ref, ...), custom_call_target="tpu_custom_call", output_to_operand_aliasing={{1}: (5, {})} | custom-call | tf_op jit(solution)/shard_map/last/pallas_call | solution.py:376
  (1 shorter events, 0.0 us)
Async XLA Ops:
  4.0 15.6 %all-to-all-start = ((bf16[32,16,128]{2,1,0:T(8,128)(2,1)}), bf16[32,16,128]{2,1,0:T(8,128)(2,1)S(1)}, u32[]{:S(2)}, u32[]{:S(2)}) async-start(bf16[32,16,128]{2,1,0:T(8,128)(2,1)} %get-tuple-element.12), calls=%async_computation | async-start | bytes 262144 | tf_op jit(solution)/shard_map/all_to_all | solution.py:334
  11.3 7.0 %collective-permute-start = (f32[256,128]{1,0:T(8,128)}, f32[256,128]{1,0:T(8,128)S(1)}, u32[]{:S(2)}, u32[]{:S(2)}) collective-permute-start(f32[256,128]{1,0:T(8,128)} %get-tuple-element.13), channel_id=1, source_target_pairs={{0,16},{16,0},{1,17},{17,1},{2,18},{18,2},{3,19},{19,3},{4,20},{20... | collective-permute-start | bytes 393224 | tf_op jit(solution)/shard_map/ppermute | solution.py:331
  13.2 14.3 %collective-permute-start.1 = (f32[64,8,128]{2,1,0:T(8,128)}, f32[64,8,128]{2,1,0:T(8,128)S(1)}, u32[]{:S(2)}, u32[]{:S(2)}) collective-permute-start(f32[64,8,128]{2,1,0:T(8,128)} %get-tuple-element.15), channel_id=1, source_target_pairs={{0,1},{1,0},{2,3},{3,2},{4,5},{5,4},{6,7},{7,6},{8,9},{9,8},{10,11... | collective-permute-start | bytes 786440 | tf_op jit(solution)/shard_map/ppermute | solution.py:327
  13.2 14.3 %collective-permute-start.2 = (f32[64,8,128]{2,1,0:T(8,128)}, f32[64,8,128]{2,1,0:T(8,128)S(1)}, u32[]{:S(2)}, u32[]{:S(2)}) collective-permute-start(f32[64,8,128]{2,1,0:T(8,128)} %get-tuple-element.16), channel_id=1, source_target_pairs={{1,2},{2,1},{3,4},{4,3},{5,6},{6,5},{7,8},{8,7},{9,10},{10,9},{11,... | collective-permute-start | bytes 786440 | tf_op jit(solution)/shard_map/ppermute | solution.py:327
  15.3 12.2 %copy-start = (f32[64,4,8,128]{3,2,1,0:T(8,128)S(1)}, f32[64,4,8,128]{3,2,1,0:T(8,128)}, u32[]{:S(2)}) copy-start(f32[64,4,8,128]{3,2,1,0:T(8,128)} %param.6) | copy-start | bytes 3145732
  15.3 12.2 %copy-start.1 = (f32[4,8,128]{2,1,0:T(8,128)S(1)}, f32[4,8,128]{2,1,0:T(8,128)}, u32[]{:S(2)}) copy-start(f32[4,8,128]{2,1,0:T(8,128)} %param.7) | copy-start | bytes 49156
  15.3 12.2 %copy-start.2 = (s32[1,1,384]{2,1,0:T(1,128)S(1)}, s32[1,1,384]{2,1,0:T(1,128)}, u32[]{:S(2)}) copy-start(s32[1,1,384]{2,1,0:T(1,128)} %param.9) | copy-start | bytes 4612
  21.1 12.4 %all-to-all-start.1 = ((f32[16,16,128]{2,1,0:T(8,128)}), f32[16,16,128]{2,1,0:T(8,128)S(1)}, u32[]{:S(2)}, u32[]{:S(2)}) async-start(f32[16,16,128]{2,1,0:T(8,128)} %boundary.1), calls=%async_computation.1 | async-start | bytes 262144 | tf_op jit(solution)/shard_map/all_to_all | solution.py:358
  25.5 5.0 %collective-permute-start.3 = (f32[64,128]{1,0:T(8,128)S(1)}, f32[64,128]{1,0:T(8,128)S(1)}, u32[]{:S(2)}, u32[]{:S(2)}) collective-permute-start(f32[64,128]{1,0:T(8,128)S(1)} %get-tuple-element.14.corner_ref), channel_id=1, source_target_pairs={{0,1},{1,0},{2,3},{3,2},{4,5},{5,4},{6,7},{7,6},{8,9},{9,8},{10,11... | collective-permute-start | bytes 98312 | tf_op jit(solution)/shard_map/ppermute | solution.py:355
  25.9 4.6 %collective-permute-start.4 = (f32[64,128]{1,0:T(8,128)S(1)}, f32[64,128]{1,0:T(8,128)S(1)}, u32[]{:S(2)}, u32[]{:S(2)}) collective-permute-start(f32[64,128]{1,0:T(8,128)S(1)} %get-tuple-element.18), channel_id=1, source_target_pairs={{1,2},{2,1},{3,4},{4,3},{5,6},{6,5},{7,8},{8,7},{9,10},{10,9},{11,... | collective-permute-start | bytes 98312 | tf_op jit(solution)/shard_map/ppermute | solution.py:355

commit v3 on v2

--- a/solution.py
+++ b/solution.py
@@ -20,38 +20,65 @@
     return pl.BlockSpec(memory_space=pltpu.HBM)
 
 
-def one_hot_depth(cells, depth):
-    lanes = jnp.bitwise_and(cells, depth - 1)
-    at = lax.broadcasted_iota(jnp.int32, (depth, cells.shape[1]), 0)
-    return jnp.where(at == lanes, 1.0, 0.0).astype(jnp.bfloat16)
-
-
-def line_of(cells, depth):
-    return jnp.right_shift(cells, depth.bit_length() - 1)
-
-
-def trace_kernel(dims, row_swaps, target_hbm, cell_hbm, field_hbm, tile_ref, *rest):
+def folded_hot(cells, depth, lines, fold):
+    few = lines // fold
+    line = jnp.right_shift(cells, depth.bit_length() - 1)
+    own = jnp.bitwise_and(line, few - 1)
+    key = jnp.right_shift(line, few.bit_length() - 1) * depth + jnp.bitwise_and(cells, depth - 1)
+    at = lax.broadcasted_iota(jnp.int32, (fold * depth, cells.shape[1]), 0)
+    return jnp.where(at == key, 1.0, 0.0).astype(jnp.bfloat16), own
+
+
+def root_first(count):
+    root = count * 11 // 16
+    return [root] + [index for index in range(count) if index != root]
+
+
+def trace_kernel(dims, row_swaps, target_hbm, cell_hbm, field_hbm, tile_hbm, *rest):
     comps, width_x, width_y, depth, rows, cols = dims
     row_faces, col_faces = rest[:row_swaps], rest[row_swaps : row_swaps + 2]
-    target_ref, cell_ref, field_ref, lhs_ref, arrived, left_sem = rest[row_swaps + 2 :]
+    target_ref, cell_ref, field_ref, lhs_ref, tile_ref, side_ref, arrived, left_sem = rest[
+        row_swaps + 2 :
+    ]
     lines = width_x * width_y
     nodes = cell_ref.shape[1]
     slot_len = nodes // cols
-    copies = [
-        pltpu.make_async_copy(source, target, arrived.at[index])
-        for index, (source, target) in enumerate(
-            [(cell_hbm, cell_ref), (field_hbm, field_ref), (target_hbm, target_ref)]
+    chunks, few = lhs_ref.shape[:2]
+    fold = lines // few
+    span = comps // chunks
+    copies = [pltpu.make_async_copy(cell_hbm, cell_ref, arrived.at[chunks])]
+    for chunk in range(chunks):
+        part = pl.ds(chunk * span, span)
+        copies.append(
+            pltpu.make_async_copy(field_hbm.at[part], field_ref.at[part], arrived.at[chunk])
         )
-    ]
+    copies.append(pltpu.make_async_copy(target_hbm, target_ref, arrived.at[chunks + 1]))
     for copy in copies:
         copy.start()
+    sent = []
     copies[0].wait()
-    cells = cell_ref[...]
-    hot = one_hot_depth(cells, depth)
-    node_line = jnp.broadcast_to(line_of(cells, depth), (8, nodes))
-    copies[1].wait()
+    hot, own = folded_hot(cell_ref[...], depth, lines, fold)
+    own = jnp.broadcast_to(own, (8, nodes))
+    flat = field_ref.reshape(comps * lines, depth)
+    found = []
+    for chunk in range(chunks):
+        copies[1 + chunk].wait()
+        for line in range(lines):
+            lhs_ref[chunk, line % few, :, pl.ds(line // few * depth, depth)] = flat[
+                pl.ds(chunk * span * lines + line, span, stride=lines), :
+            ].astype(jnp.bfloat16)
+        total = jnp.zeros((span // 8, 8, nodes), jnp.float32)
+        group = min(4, few)
+        for first in range(0, few, group):
+            block = jnp.dot(
+                lhs_ref[chunk, first : first + group].reshape(group * span, fold * depth),
+                hot,
+                preferred_element_type=jnp.float32,
+            ).reshape(group, span // 8, 8, nodes)
+            for line in range(group):
+                total = jnp.where((own == first + line)[None], block[line], total)
+        found.append(total.reshape(span, nodes))
     col_odd = lax.rem(lax.axis_index("col"), 2)
-    sent = []
     for swap, face_ref in enumerate(col_faces):
         layer = jnp.where(col_odd == swap, width_x - 1, 0)
         start = pl.multiple_of(layer * width_y, width_y)
@@ -61,21 +88,14 @@
             )
         )
         sent[-1].start()
-    flat = field_ref.reshape(comps * lines, depth)
-    for line in range(lines):
-        lhs_ref[pl.ds(line * comps, comps), :] = flat[
-            pl.ds(line, comps, stride=lines), :
-        ].astype(jnp.bfloat16)
-    total = jnp.zeros((comps // 8, 8, nodes), jnp.float32)
-    group = 4
-    for first in range(0, lines, group):
-        block = jnp.dot(
-            lhs_ref[pl.ds(first * comps, group * comps), :], hot, preferred_element_type=jnp.float32
-        ).reshape(group, comps // 8, 8, nodes)
-        for line in range(group):
-            total = jnp.where((node_line == first + line)[None], block[line], total)
-    by_node = total.reshape(comps, nodes).T
-    copies[2].wait()
+    row_odd = lax.rem(lax.axis_index("row"), 2)
+    for swap, face_ref in enumerate(row_faces):
+        layer = jnp.where(row_odd == swap, width_y - 1, 0)
+        side_ref[swap] = flat[pl.ds(layer, comps * width_x, stride=width_y), :]
+        sent.append(pltpu.make_async_copy(side_ref.at[swap], face_ref, left_sem.at[2 + swap]))
+        sent[-1].start()
+    by_node = jnp.concatenate(found, axis=0).T
+    copies[-1].wait()
     left_len = min(slot_len, TILE_ROWS)
     for slot in range(cols):
         piece = by_node[slot * slot_len : (slot + 1) * slot_len]
@@ -93,23 +113,19 @@
         tile = jnp.concatenate([left, right], axis=1).astype(jnp.bfloat16)
         for row in range(rows):
             tile_ref[row * cols + target_ref[0, slot]] = tile
-    row_odd = lax.rem(lax.axis_index("row"), 2)
-    for swap, face_ref in enumerate(row_faces):
-        layer = jnp.where(row_odd == swap, width_y - 1, 0)
-        face_ref[...] = flat[pl.ds(layer, comps * width_x, stride=width_y), :]
+    sent.append(pltpu.make_async_copy(tile_ref, tile_hbm, left_sem.at[2 + row_swaps]))
+    sent[-1].start()
     for copy in sent:
         copy.wait()
 
 
-def corner_kernel(dims, row_swaps, *refs):
-    comps, width_x = dims[:2]
-    odd = lax.rem(lax.axis_index("col"), 2)
-    for swap, out_ref in enumerate(refs[row_swaps:]):
-        layer = jnp.where(odd == swap, width_x - 1, 0)
-        for index, row_ref in enumerate(refs[:row_swaps]):
-            out_ref[pl.ds(index * comps, comps), :] = row_ref[
-                pl.ds(layer, comps, stride=width_x), :
-            ]
+def corner_kernel(dims, first_ref, second_ref, *out_refs):
+    comps, width_x, width_y = dims[:3]
+    odd = lax.rem(lax.axis_index("row"), 2)
+    for swap, out_ref in enumerate(out_refs):
+        layer = jnp.where(odd == swap, width_y - 1, 0)
+        for index, ref in enumerate((first_ref, second_ref)):
+            out_ref[pl.ds(index * comps, comps), :] = ref[pl.ds(layer, comps, stride=width_y), :]
 
 
 def unpack_tiles(tiles, slot_len, comps):
@@ -121,7 +137,7 @@
     return both.reshape(tiles.shape[0] * slot_len, comps)
 
 
-def boundary_kernel(slot_len, own_rows, trace_ref, real_ref, imag_ref, corner_ref, out_ref):
+def boundary_kernel(slot_len, own_rows, trace_ref, real_ref, imag_ref, row_ref, out_ref):
     if len(trace_ref.shape) == 3:
         traces = unpack_tiles(
             trace_ref[...].astype(jnp.float32), slot_len, trace_ref.shape[2] // 2
@@ -136,7 +152,9 @@
     ) + jnp.dot(imag_ref[...], turned.astype(jnp.bfloat16), preferred_element_type=jnp.float32)
     image = image.reshape(image.shape[0] // own_rows, own_rows, comps)
     half = own_rows // 2
-    out_ref[...] = jnp.concatenate([image[:, :half], image[:, half:]], axis=2)
+    packed = jnp.concatenate([image[:, :half], image[:, half:]], axis=2)
+    for place, col in enumerate(root_first(packed.shape[0])):
+        out_ref[place] = packed[col]
 
 
 def shifted_z(values, step):
@@ -158,14 +176,14 @@
     out_ref, edge_ref, lhs_ref, taken_ref = refs[6 + row_swaps :]
     lines = width_x * width_y
     nodes = cell_ref.shape[1]
-    cells = cell_ref[...]
-    hot = one_hot_depth(cells, depth)
-    at_line = lax.broadcasted_iota(jnp.int32, (lines, nodes), 0)
-    line_hot = jnp.where(at_line == line_of(cells, depth), 1.0, 0.0)
-
+    fold = 2
+    few = lines // fold
+    hot, own = folded_hot(cell_ref[...], depth, lines, fold)
+    at_line = lax.broadcasted_iota(jnp.int32, (few, nodes), 0)
+    line_hot = jnp.where(at_line == own, 1.0, 0.0)
     for comp in range(comps):
-        lhs_ref[pl.ds(comp * lines, lines), :] = (
-            line_hot * jnp.broadcast_to(flux_ref[pl.ds(comp, 1), :], (lines, nodes))
+        lhs_ref[pl.ds(comp * few, few), :] = (
+            line_hot * jnp.broadcast_to(flux_ref[comp], (few, nodes))
         ).astype(jnp.bfloat16)
     taken_ref[...] = lax.dot_general(
         lhs_ref[...], hot, (((1,), (1,)), ((), ())), preferred_element_type=jnp.float32
@@ -219,7 +237,12 @@
                 (10.0 / 3.0) * centre
                 + (1.0 / 3.0) * near
                 - weight[x] * over_xyz
-                - taken_ref[here, :]
+                - taken_ref[
+                    pl.ds(
+                        pl.multiple_of(comp * few + x * width_y % few, width_y), width_y
+                    ),
+                    pl.ds(x * width_y // few * depth, depth),
+                ]
             )
             out_ref[here, :] = image
             for side in range(2):
@@ -237,10 +260,11 @@
 
 
 def last_kernel(
-    dims, row_swaps, part_ref, medium_ref, edge_ref, first_ref, second_ref, *refs
+    dims, row_swaps, part_ref, medium_ref, edge_ref, *refs
 ):
     comps, width_x, width_y, depth, rows, cols = dims
-    image_ref, volume_ref, plane_ref, total_ref, sent = refs[1:]
+    corner_refs = refs[:row_swaps]
+    image_ref, volume_ref, plane_ref, total_ref, sent = refs[row_swaps + 1 :]
     row_odd = lax.rem(lax.axis_index("row"), 2)
     col_odd = lax.rem(lax.axis_index("col"), 2) == 1
     copies = []
@@ -248,8 +272,8 @@
         at_x = side * (width_x - 1)
         plane_ref[side] = edge_ref[side]
         for index in range(row_swaps):
-            lines = pl.ds(index * comps, comps)
-            first, second = first_ref[lines, :], second_ref[lines, :]
+            first = corner_refs[index][pl.ds(0, comps), :]
+            second = corner_refs[index][pl.ds(comps, comps), :]
             if side:
                 line = jnp.where(col_odd, second, first)
             else:
@@ -297,12 +321,12 @@
     own_rows = slab_rows // cols
     f32, bf16 = jnp.float32, jnp.bfloat16
     params = pltpu.CompilerParams(vmem_limit_bytes=SMALL)
-    whole_params = pltpu.CompilerParams(vmem_limit_bytes=WHOLE)
-
+
+    chunks, fold = 2, 4
     field = wave_field.reshape(comps * lines, depth)
     cells = node_cell.reshape(1, nodes)
     targets = block_target.reshape(1, cols)
-    flux = node_flux.reshape(comps, nodes)
+    flux = node_flux.reshape(comps, 1, nodes)
     medium = medium_term.reshape(lines, depth)
 
     tiles, *faces = pl.pallas_call(
@@ -311,21 +335,23 @@
         + [jax.ShapeDtypeStruct((comps * width_x, depth), f32)] * row_swaps
         + [jax.ShapeDtypeStruct((comps, width_y, depth), f32)] * 2,
         in_specs=[hbm()] * 3,
-        out_specs=[vmem()] * (1 + row_swaps) + [hbm()] * 2,
+        out_specs=[hbm()] * (3 + row_swaps),
         scratch_shapes=[
             pltpu.SMEM((1, cols), jnp.int32),
             pltpu.VMEM((1, nodes), jnp.int32),
             pltpu.VMEM((comps, lines, depth), f32),
-            pltpu.VMEM((comps * lines, depth), bf16),
-            pltpu.SemaphoreType.DMA((3,)),
-            pltpu.SemaphoreType.DMA((2,)),
+            pltpu.VMEM((chunks, lines // fold, comps // chunks, fold * depth), bf16),
+            pltpu.VMEM((rows * cols, TILE_ROWS, 2 * comps), bf16),
+            pltpu.VMEM((row_swaps, comps * width_x, depth), f32),
+            pltpu.SemaphoreType.DMA((chunks + 2,)),
+            pltpu.SemaphoreType.DMA((3 + row_swaps,)),
         ],
-        compiler_params=whole_params,
+        compiler_params=pltpu.CompilerParams(vmem_limit_bytes=WHOLE),
         name="traces",
     )(targets, cells, field.reshape(comps, lines, depth))
     col_sides = [
         lax.ppermute(face, "col", swap_pairs(cols, swap)).reshape(comps * width_y, depth)
-        for swap, face in enumerate(faces[row_swaps:])
+        for swap, face in enumerate(faces[row_swaps : row_swaps + 2])
     ]
     row_sides = [
         lax.ppermute(face, "row", swap_pairs(rows, swap))
@@ -335,14 +361,6 @@
 
     if slot_len % 8:
         received = unpack_tiles(received, slot_len, comps)
-    corners = pl.pallas_call(
-        functools.partial(corner_kernel, dims, row_swaps),
-        out_shape=[jax.ShapeDtypeStruct((row_swaps * comps, depth), f32)] * 2,
-        in_specs=[vmem()] * row_swaps,
-        out_specs=[vmem()] * 2,
-        compiler_params=params,
-        name="corners",
-    )(*row_sides)
     shares = pl.pallas_call(
         functools.partial(boundary_kernel, slot_len, own_rows),
         out_shape=jax.ShapeDtypeStruct((cols, own_rows // 2, 2 * comps), f32),
@@ -350,12 +368,23 @@
         out_specs=vmem(),
         compiler_params=params,
         name="boundary",
-    )(received, boundary_matrix[0], boundary_matrix[1], corners[0])
+    )(received, boundary_matrix[0], boundary_matrix[1], row_sides[0])
+    shares = lax.all_to_all(
+        shares, "col", 0, 0, tiled=True, axis_index_groups=[root_first(cols)]
+    )
+
+    corners = pl.pallas_call(
+        functools.partial(corner_kernel, dims),
+        out_shape=[jax.ShapeDtypeStruct((2 * comps, depth), f32)] * row_swaps,
+        in_specs=[vmem()] * 2,
+        out_specs=[vmem()] * row_swaps,
+        compiler_params=params,
+        name="corners",
+    )(*col_sides)
     corner_sides = [
-        lax.ppermute(lines_of, "col", swap_pairs(cols, swap))
+        lax.ppermute(lines_of, "row", swap_pairs(rows, swap))
         for swap, lines_of in enumerate(corners)
     ]
-    shares = lax.all_to_all(shares, "col", 0, 0, tiled=True)
 
     volume, edges = pl.pallas_call(
         functools.partial(volume_kernel, dims, row_swaps),
@@ -366,8 +395,8 @@
         in_specs=[vmem()] * (6 + row_swaps),
         out_specs=[vmem()] * 2,
         scratch_shapes=[
-            pltpu.VMEM((comps * lines, nodes), bf16),
-            pltpu.VMEM((comps * lines, depth), f32),
+            pltpu.VMEM((comps * lines // 2, nodes), bf16),
+            pltpu.VMEM((comps * lines // 2, 2 * depth), f32),
         ],
         compiler_params=params,
         name="volume",
@@ -379,14 +408,14 @@
             jax.ShapeDtypeStruct((own_rows, comps), f32),
             jax.ShapeDtypeStruct((comps, lines, depth), f32),
         ],
-        in_specs=[vmem()] * 5 + [hbm()],
+        in_specs=[vmem()] * (3 + row_swaps) + [hbm()],
         out_specs=[hbm(), hbm()],
         scratch_shapes=[
             pltpu.VMEM((2, comps * width_y, depth), f32),
             pltpu.VMEM((own_rows, comps), f32),
             pltpu.SemaphoreType.DMA((3,)),
         ],
-        input_output_aliases={5: 1},
+        input_output_aliases={3 + row_swaps: 1},
         compiler_params=params,
         name="last",
     )(shares, medium, edges, *corner_sides, volume.reshape(comps, lines, depth))

time: 34.7 us -> 31.1 us (0.90)
  waiting for transfers between devices: 7.24 us -> 4.78 us
  local copies, waits for them, and re-layouts: 2.4 us -> 1.5 us
  Pallas kernels: 8.71 us -> 8.2 us
    all_to_all x1, waiting for transfers between devices: 2.94 us -> 0.01 us  [on_device(): lax.all_to_all(shares, 'col', 0, 0, tiled=True, axis_index_groups=[root_f...]
    unnamed x7 -> x8, local copies, waits for them, and re-layouts: 0.92 us -> 0.03 us
    ppermute x2 -> x1, waiting for transfers between devices: 0.01 us -> 0.47 us  [on_device(): lax.ppermute(lines_of, 'row', swap_pairs(rows, swap))]
    all_to_all x1, starting transfers between devices: 4.42 us -> 4.83 us  [on_device(): lax.all_to_all(shares, 'col', 0, 0, tiled=True, axis_index_groups=[root_f...]
    pallas_call x1, Pallas kernels: 3.39 us -> 2.97 us  [on_device(): pl.pallas_call(functools.partial(trace_kernel, dims, row_swaps), out_shap...]
    ppermute x2 -> x1, starting transfers between devices: 1.06 us -> 0.99 us  [on_device(): lax.ppermute(lines_of, 'row', swap_pairs(rows, swap))]
  transfers between devices with their start and end apart: 7 -> 6, of which waited for: 3 -> 3; matrix products, arithmetic and copies ran while one was open for 7% -> 5% of each run, Pallas kernels for 13% -> 14%
where the time goes in v3:
time: 31.1 us; the launch traced here: 30.8 us
  starting transfers between devices  15.6 us (50%)
  Pallas kernels  8.2 us (26%)
  waiting for transfers between devices  4.78 us (15%)
  local copies, waits for them, and re-layouts  1.5 us (5%)
  between operations  0.72 us (2%)
    all_to_all x1, starting transfers between devices, on_device(): received = lax.all_to_all(tiles, ('row', 'col'), 0, 0, tiled=True)  7.3 us
    all_to_all x1, starting transfers between devices, on_device(): lax.all_to_all(shares, 'col', 0, 0, tiled=True, axis_index_groups=[root_f...  4.83 us
    ppermute x1, waiting for transfers between devices, on_device(): lax.ppermute(face, 'row', swap_pairs(rows, swap))  2.99 us
    pallas_call x1, Pallas kernels, on_device(): pl.pallas_call(functools.partial(trace_kernel, dims, row_swaps), out_shap...  2.97 us
    pallas_call x1, Pallas kernels, on_device(): pl.pallas_call(functools.partial(volume_kernel, dims, row_swaps), out_sha...  2.85 us
    ppermute x1, starting transfers between devices, on_device(): lax.ppermute(face, 'row', swap_pairs(rows, swap))  1.83 us
    squeeze x1, local copies, waits for them, and re-layouts, on_device(): boundary_matrix[1]  1.48 us
    pallas_call x1, Pallas kernels, on_device(): pl.pallas_call(functools.partial(boundary_kernel, slot_len, own_rows), ou...  1.42 us
  transfers between devices with their start and end apart: 6, of which 3 were waited for; matrix products, arithmetic and copies ran while one was open for 5% of the time, Pallas kernels for 14%

profile of v3, /device:TPU:0, one launch (start us, length us, event | category | flops | bytes accessed | tf_op | source)
XLA Modules:
  0.0 30.8 jit_solution(15612985241137100938)
XLA Ops:
  0.6 3.0 %traces.1 = (bf16[32,16,128]{2,1,0:T(8,128)(2,1)}, f32[256,128]{1,0:T(8,128)}, f32[64,8,128]{2,1,0:T(8,128)}, f32[64,8,128]{2,1,0:T(8,128)}) custom-call(s32[1,16]{1,0:T(1,128)} %bitcast.27, s32[1,384]{1,0:T(1,128)} %bitcast.23, f32[64,32,128]{2,1,0:T(8,128)} %bitcast.14), custom_call_target="tpu_custom_call" | custom-call | tf_op jit(solution)/shard_map/traces/pallas_call | solution.py:332
  3.6 7.3 %all-to-all-start = ((bf16[32,16,128]{2,1,0:T(8,128)(2,1)}), bf16[32,16,128]{2,1,0:T(8,128)(2,1)S(1)}, u32[]{:S(2)}, u32[]{:S(2)}) async-start(bf16[32,16,128]{2,1,0:T(8,128)(2,1)} %get-tuple-element.10), calls=%async_computation | async-start | bytes 262144 | tf_op jit(solution)/shard_map/all_to_all | solution.py:360
  10.9 1.8 %collective-permute-start = (f32[256,128]{1,0:T(8,128)}, f32[256,128]{1,0:T(8,128)S(1)}, u32[]{:S(2)}, u32[]{:S(2)}) collective-permute-start(f32[256,128]{1,0:T(8,128)} %get-tuple-element.11), channel_id=1, source_target_pairs={{0,16},{16,0},{1,17},{17,1},{2,18},{18,2},{3,19},{19,3},{4,20},{20... | collective-permute-start | bytes 393224 | tf_op jit(solution)/shard_map/ppermute | solution.py:357
  12.8 0.0 collective-permute-start.1
  12.8 0.7 %collective-permute-start.2 = (f32[64,8,128]{2,1,0:T(8,128)}, f32[64,8,128]{2,1,0:T(8,128)S(1)}, u32[]{:S(2)}, u32[]{:S(2)}) collective-permute-start(f32[64,8,128]{2,1,0:T(8,128)} %get-tuple-element.13), channel_id=1, source_target_pairs={{1,2},{2,1},{3,4},{4,3},{5,6},{6,5},{7,8},{8,7},{9,10},{10,9},{11,... | collective-permute-start | bytes 786440 | tf_op jit(solution)/shard_map/ppermute | solution.py:353
  13.4 1.5 %slice_bitcast_fusion = (bf16[512,768]{1,0:T(8,128)(2,1)S(1)}, bf16[512,768]{1,0:T(8,128)(2,1)S(1)}) fusion(bf16[2,512,768]{2,1,0:T(8,128)(2,1)} %param.11), kind=kLoop, calls=%fused_computation | loop fusion | bytes 3145728 | tf_op jit(solution)/shard_map/squeeze | solution.py:371
  14.9 0.0 copy-start
  14.9 0.0 copy-start.1
  14.9 0.0 copy-start.2
  14.9 0.0 copy-start.3
  15.0 3.0 %collective-permute-done.row_ref.refs_4_ = f32[256,128]{1,0:T(8,128)S(1)} collective-permute-done((f32[256,128]{1,0:T(8,128)}, f32[256,128]{1,0:T(8,128)S(1)}, u32[]{:S(2)}, u32[]{:S(2)}) %collective-permute-start) | collective-permute-done | bytes 131104 | tf_op jit(solution)/shard_map/ppermute | solution.py:357
  17.9 1.3 %all-to-all-done.trace_ref = bf16[32,16,128]{2,1,0:T(8,128)(2,1)S(1)} async-done(((bf16[32,16,128]{2,1,0:T(8,128)(2,1)}), bf16[32,16,128]{2,1,0:T(8,128)(2,1)S(1)}, u32[]{:S(2)}, u32[]{:S(2)}) %all-to-all-start) | async-done | bytes 131104 | tf_op jit(solution)/shard_map/all_to_all | solution.py:360
  19.2 1.4 %boundary.1 = f32[16,16,128]{2,1,0:T(8,128)} custom-call(bf16[32,16,128]{2,1,0:T(8,128)(2,1)S(1)} %all-to-all-done.trace_ref, bf16[512,768]{1,0:T(8,128)(2,1)S(1)} %get-tuple-element.19.real_ref, bf16[512,768]{1,0:T(8,128)(2,1)S(1)} %get-tuple-element.18.imag_ref, f32[256,128]{1,0:T(8,128)S(1)} %collective-permute-done.row_ref.refs_4_), custom_call_target="tpu_custom_call" | custom-call | tf_op jit(solution)/shard_map/boundary/pallas_call | solution.py:364
  20.7 4.8 %all-to-all-start.1 = ((f32[16,16,128]{2,1,0:T(8,128)}), f32[16,16,128]{2,1,0:T(8,128)S(1)}, u32[]{:S(2)}, u32[]{:S(2)}) async-start(f32[16,16,128]{2,1,0:T(8,128)} %boundary.1), calls=%async_computation.1 | async-start | bytes 262144 | tf_op jit(solution)/shard_map/all_to_all | solution.py:372
  25.5 0.0 collective-permute-done.1
  25.5 0.0 collective-permute-done.2
  25.6 1.0 %collective-permute-start.3 = (f32[128,128]{1,0:T(8,128)S(1)}, f32[128,128]{1,0:T(8,128)S(1)}, u32[]{:S(2)}, u32[]{:S(2)}) collective-permute-start(f32[128,128]{1,0:T(8,128)S(1)} %corners.1), channel_id=1, source_target_pairs={{0,16},{16,0},{1,17},{17,1},{2,18},{18,2},{3,19},{19,3},{4,20},{20... | collective-permute-start | bytes 196616 | tf_op jit(solution)/shard_map/ppermute | solution.py:385
  26.5 0.0 copy-done
  26.5 0.0 copy-done.1
  26.6 0.0 copy-done.2
  26.6 0.0 copy-done.3
  26.6 2.9 %volume.1 = (f32[2048,128]{1,0:T(8,128)}, f32[2,512,128]{2,1,0:T(8,128)S(1)}) custom-call(f32[2048,128]{1,0:T(8,128)S(1)} %bitcast.15, f32[32,128]{1,0:T(8,128)S(1)} %bitcast.21, f32[64,1,384]{2,1,0:T(1,128)S(1)} %bitcast.20, s32[1,384]{1,0:T(1,128)S(1)} %bitcast.24, f32[256,128]{1,0:T(8,128)S(1)} %collective-permute-done.row_ref.refs_4_, ...), custom_call_target="tpu_custom_call" | custom-call | tf_op jit(solution)/shard_map/volume/pallas_call | solution.py:389
  29.4 0.5 %collective-permute-done.3.refs_0_ = f32[128,128]{1,0:T(8,128)S(1)} collective-permute-done((f32[128,128]{1,0:T(8,128)S(1)}, f32[128,128]{1,0:T(8,128)S(1)}, u32[]{:S(2)}, u32[]{:S(2)}) %collective-permute-start.3) | collective-permute-done | bytes 65568 | tf_op jit(solution)/shard_map/ppermute | solution.py:385
  29.9 0.0 all-to-all-done.1.part_ref
  29.9 0.9 %last.1 = (f32[32,64]{1,0:T(8,128)}, f32[64,32,128]{2,1,0:T(8,128)}) custom-call(f32[16,16,128]{2,1,0:T(8,128)S(1)} %all-to-all-done.1.part_ref, f32[32,128]{1,0:T(8,128)S(1)} %bitcast.22, f32[2,512,128]{2,1,0:T(8,128)S(1)} %get-tuple-element.14.edge_ref, f32[128,128]{1,0:T(8,128)S(1)} %collective-permute-done.3.refs_0_, ...), custom_call_target="tpu_custom_call", output_to_operand_aliasing={{1}: (4, {})} | custom-call | tf_op jit(solution)/shard_map/last/pallas_call | solution.py:405
  (1 shorter events, 0.0 us)
Async XLA Ops:
  3.6 15.6 %all-to-all-start = ((bf16[32,16,128]{2,1,0:T(8,128)(2,1)}), bf16[32,16,128]{2,1,0:T(8,128)(2,1)S(1)}, u32[]{:S(2)}, u32[]{:S(2)}) async-start(bf16[32,16,128]{2,1,0:T(8,128)(2,1)} %get-tuple-element.10), calls=%async_computation | async-start | bytes 262144 | tf_op jit(solution)/shard_map/all_to_all | solution.py:360
  10.9 7.0 %collective-permute-start = (f32[256,128]{1,0:T(8,128)}, f32[256,128]{1,0:T(8,128)S(1)}, u32[]{:S(2)}, u32[]{:S(2)}) collective-permute-start(f32[256,128]{1,0:T(8,128)} %get-tuple-element.11), channel_id=1, source_target_pairs={{0,16},{16,0},{1,17},{17,1},{2,18},{18,2},{3,19},{19,3},{4,20},{20... | collective-permute-start | bytes 393224 | tf_op jit(solution)/shard_map/ppermute | solution.py:357
  12.8 12.7 %collective-permute-start.1 = (f32[64,8,128]{2,1,0:T(8,128)}, f32[64,8,128]{2,1,0:T(8,128)S(1)}, u32[]{:S(2)}, u32[]{:S(2)}) collective-permute-start(f32[64,8,128]{2,1,0:T(8,128)} %get-tuple-element.12), channel_id=1, source_target_pairs={{0,1},{1,0},{2,3},{3,2},{4,5},{5,4},{6,7},{7,6},{8,9},{9,8},{10,11... | collective-permute-start | bytes 786440 | tf_op jit(solution)/shard_map/ppermute | solution.py:353
  12.8 12.8 %collective-permute-start.2 = (f32[64,8,128]{2,1,0:T(8,128)}, f32[64,8,128]{2,1,0:T(8,128)S(1)}, u32[]{:S(2)}, u32[]{:S(2)}) collective-permute-start(f32[64,8,128]{2,1,0:T(8,128)} %get-tuple-element.13), channel_id=1, source_target_pairs={{1,2},{2,1},{3,4},{4,3},{5,6},{6,5},{7,8},{8,7},{9,10},{10,9},{11,... | collective-permute-start | bytes 786440 | tf_op jit(solution)/shard_map/ppermute | solution.py:353
  14.9 11.6 %copy-start = (f32[64,4,8,128]{3,2,1,0:T(8,128)S(1)}, f32[64,4,8,128]{3,2,1,0:T(8,128)}, u32[]{:S(2)}) copy-start(f32[64,4,8,128]{3,2,1,0:T(8,128)} %param.6) | copy-start | bytes 3145732
  14.9 11.6 %copy-start.1 = (f32[64,1,1,384]{3,2,1,0:T(1,128)S(1)}, f32[64,1,1,384]{3,2,1,0:T(1,128)}, u32[]{:S(2)}) copy-start(f32[64,1,1,384]{3,2,1,0:T(1,128)} %param.8) | copy-start | bytes 294916
  14.9 11.6 %copy-start.2 = (f32[4,8,128]{2,1,0:T(8,128)S(1)}, f32[4,8,128]{2,1,0:T(8,128)}, u32[]{:S(2)}) copy-start(f32[4,8,128]{2,1,0:T(8,128)} %param.7) | copy-start | bytes 49156
  14.9 11.6 %copy-start.3 = (s32[1,1,384]{2,1,0:T(1,128)S(1)}, s32[1,1,384]{2,1,0:T(1,128)}, u32[]{:S(2)}) copy-start(s32[1,1,384]{2,1,0:T(1,128)} %param.9) | copy-start | bytes 4612
  20.7 9.2 %all-to-all-start.1 = ((f32[16,16,128]{2,1,0:T(8,128)}), f32[16,16,128]{2,1,0:T(8,128)S(1)}, u32[]{:S(2)}, u32[]{:S(2)}) async-start(f32[16,16,128]{2,1,0:T(8,128)} %boundary.1), calls=%async_computation.1 | async-start | bytes 262144 | tf_op jit(solution)/shard_map/all_to_all | solution.py:372
  25.6 4.3 %collective-permute-start.3 = (f32[128,128]{1,0:T(8,128)S(1)}, f32[128,128]{1,0:T(8,128)S(1)}, u32[]{:S(2)}, u32[]{:S(2)}) collective-permute-start(f32[128,128]{1,0:T(8,128)S(1)} %corners.1), channel_id=1, source_target_pairs={{0,16},{16,0},{1,17},{17,1},{2,18},{18,2},{3,19},{19,3},{4,20},{20... | collective-permute-start | bytes 196616 | tf_op jit(solution)/shard_map/ppermute | solution.py:385

commit v4 on v3

--- a/solution.py
+++ b/solution.py
@@ -125,7 +125,9 @@
     for swap, out_ref in enumerate(out_refs):
         layer = jnp.where(odd == swap, width_y - 1, 0)
         for index, ref in enumerate((first_ref, second_ref)):
-            out_ref[pl.ds(index * comps, comps), :] = ref[pl.ds(layer, comps, stride=width_y), :]
+            out_ref[pl.ds(index * comps, comps), :] = ref[
+                pl.ds(layer, comps, stride=width_y), :
+            ].astype(out_ref.dtype)
 
 
 def unpack_tiles(tiles, slot_len, comps):
@@ -152,7 +154,7 @@
     ) + jnp.dot(imag_ref[...], turned.astype(jnp.bfloat16), preferred_element_type=jnp.float32)
     image = image.reshape(image.shape[0] // own_rows, own_rows, comps)
     half = own_rows // 2
-    packed = jnp.concatenate([image[:, :half], image[:, half:]], axis=2)
+    packed = jnp.concatenate([image[:, :half], image[:, half:]], axis=2).astype(out_ref.dtype)
     for place, col in enumerate(root_first(packed.shape[0])):
         out_ref[place] = packed[col]
 
@@ -210,10 +212,10 @@
     def component(comp):
         base = comp * lines
         planes = [
-            field_ref[pl.ds(pl.multiple_of(base + x * width_y, width_y), width_y), :]
+            field_ref[pl.ds(base + x * width_y, width_y), :]
             for x in range(width_x)
         ]
-        face = pl.ds(pl.multiple_of(comp * width_y, width_y), width_y)
+        face = pl.ds(comp * width_y, width_y)
         first, second = first_ref[face, :], second_ref[face, :]
         planes = (
             [jnp.where(col_odd, first, second)] + planes + [jnp.where(col_odd, second, first)]
@@ -232,7 +234,7 @@
             over_xy = 2.0 * over_x + side_y(over_x, ends_x)
             over_xyz = 2.0 * over_xy + side_z(over_xy)
             near = sides + side_y(centre, ends[x + 1]) + side_z(centre)
-            here = pl.ds(pl.multiple_of(base + x * width_y, width_y), width_y)
+            here = pl.ds(base + x * width_y, width_y)
             image = (
                 (10.0 / 3.0) * centre
                 + (1.0 / 3.0) * near
@@ -249,14 +251,8 @@
                 if x == side * (width_x - 1):
                     edge_ref[side, face, :] = image
 
-    together = 16
-
-    def components(step, carry):
-        for index in range(together):
-            component(step * together + index)
-        return carry
-
-    lax.fori_loop(0, comps // together, components, 0)
+    for comp in range(comps):
+        component(comp)
 
 
 def last_kernel(
@@ -267,13 +263,18 @@
     image_ref, volume_ref, plane_ref, total_ref, sent = refs[row_swaps + 1 :]
     row_odd = lax.rem(lax.axis_index("row"), 2)
     col_odd = lax.rem(lax.axis_index("col"), 2) == 1
-    copies = []
+    total = jnp.sum(part_ref[...].astype(jnp.float32), axis=0)
+    half, lanes = total.shape
+    total_ref[:half] = total[:, : lanes // 2]
+    total_ref[half:] = total[:, lanes // 2 :]
+    copies = [pltpu.make_async_copy(total_ref, image_ref, sent.at[2])]
+    copies[-1].start()
     for side in range(2):
         at_x = side * (width_x - 1)
         plane_ref[side] = edge_ref[side]
         for index in range(row_swaps):
-            first = corner_refs[index][pl.ds(0, comps), :]
-            second = corner_refs[index][pl.ds(comps, comps), :]
+            first = corner_refs[index][pl.ds(0, comps), :].astype(jnp.float32)
+            second = corner_refs[index][pl.ds(comps, comps), :].astype(jnp.float32)
             if side:
                 line = jnp.where(col_odd, second, first)
             else:
@@ -292,12 +293,6 @@
             )
         )
         copies[-1].start()
-    total = jnp.sum(part_ref[...], axis=0)
-    half, lanes = total.shape
-    total_ref[:half] = total[:, : lanes // 2]
-    total_ref[half:] = total[:, lanes // 2 :]
-    copies.append(pltpu.make_async_copy(total_ref, image_ref, sent.at[2]))
-    copies[-1].start()
     for copy in copies:
         copy.wait()
 
@@ -363,7 +358,7 @@
         received = unpack_tiles(received, slot_len, comps)
     shares = pl.pallas_call(
         functools.partial(boundary_kernel, slot_len, own_rows),
-        out_shape=jax.ShapeDtypeStruct((cols, own_rows // 2, 2 * comps), f32),
+        out_shape=jax.ShapeDtypeStruct((cols, own_rows // 2, 2 * comps), bf16),
         in_specs=[vmem()] * 4,
         out_specs=vmem(),
         compiler_params=params,
@@ -375,7 +370,7 @@
 
     corners = pl.pallas_call(
         functools.partial(corner_kernel, dims),
-        out_shape=[jax.ShapeDtypeStruct((2 * comps, depth), f32)] * row_swaps,
+        out_shape=[jax.ShapeDtypeStruct((2 * comps, depth), bf16)] * row_swaps,
         in_specs=[vmem()] * 2,
         out_specs=[vmem()] * row_swaps,
         compiler_params=params,

time: 31.1 us -> 30.7 us (0.987)
  Pallas kernels: 8.2 us -> 7.79 us
    pallas_call x1, Pallas kernels: 2.85 us -> 2.47 us  [on_device(): pl.pallas_call(functools.partial(volume_kernel, dims, row_swaps), out_sha...]
  transfers between devices with their start and end apart: 6 -> 6, of which waited for: 3 -> 3; matrix products, arithmetic and copies ran while one was open for 5% -> 5% of each run, Pallas kernels for 14% -> 13%
where the time goes in v4:
time: 30.7 us; the launch traced here: 30.4 us
  starting transfers between devices  15.6 us (51%)
  Pallas kernels  7.79 us (25%)
  waiting for transfers between devices  4.82 us (16%)
  local copies, waits for them, and re-layouts  1.5 us (5%)
  between operations  0.72 us (2%)
    all_to_all x1, starting transfers between devices, on_device(): received = lax.all_to_all(tiles, ('row', 'col'), 0, 0, tiled=True)  7.3 us
    all_to_all x1, starting transfers between devices, on_device(): lax.all_to_all(shares, 'col', 0, 0, tiled=True, axis_index_groups=[root_f...  4.83 us
    ppermute x1, waiting for transfers between devices, on_device(): lax.ppermute(face, 'row', swap_pairs(rows, swap))  2.99 us
    pallas_call x1, Pallas kernels, on_device(): pl.pallas_call(functools.partial(trace_kernel, dims, row_swaps), out_shap...  2.97 us
    pallas_call x1, Pallas kernels, on_device(): pl.pallas_call(functools.partial(volume_kernel, dims, row_swaps), out_sha...  2.47 us
    ppermute x1, starting transfers between devices, on_device(): lax.ppermute(face, 'row', swap_pairs(rows, swap))  1.83 us
    squeeze x1, local copies, waits for them, and re-layouts, on_device(): boundary_matrix[1]  1.48 us
    pallas_call x1, Pallas kernels, on_device(): pl.pallas_call(functools.partial(boundary_kernel, slot_len, own_rows), ou...  1.39 us
  transfers between devices with their start and end apart: 6, of which 3 were waited for; matrix products, arithmetic and copies ran while one was open for 5% of the time, Pallas kernels for 13%

profile of v4, /device:TPU:0, one launch (start us, length us, event | category | flops | bytes accessed | tf_op | source)
XLA Modules:
  0.0 30.4 jit_solution(2233040229434932929)
XLA Ops:
  0.6 3.0 %traces.1 = (bf16[32,16,128]{2,1,0:T(8,128)(2,1)}, f32[256,128]{1,0:T(8,128)}, f32[64,8,128]{2,1,0:T(8,128)}, f32[64,8,128]{2,1,0:T(8,128)}) custom-call(s32[1,16]{1,0:T(1,128)} %bitcast.27, s32[1,384]{1,0:T(1,128)} %bitcast.23, f32[64,32,128]{2,1,0:T(8,128)} %bitcast.14), custom_call_target="tpu_custom_call" | custom-call | tf_op jit(solution)/shard_map/traces/pallas_call | solution.py:327
  3.6 7.3 %all-to-all-start = ((bf16[32,16,128]{2,1,0:T(8,128)(2,1)}), bf16[32,16,128]{2,1,0:T(8,128)(2,1)S(1)}, u32[]{:S(2)}, u32[]{:S(2)}) async-start(bf16[32,16,128]{2,1,0:T(8,128)(2,1)} %get-tuple-element.10), calls=%async_computation | async-start | bytes 262144 | tf_op jit(solution)/shard_map/all_to_all | solution.py:355
  10.9 1.8 %collective-permute-start = (f32[256,128]{1,0:T(8,128)}, f32[256,128]{1,0:T(8,128)S(1)}, u32[]{:S(2)}, u32[]{:S(2)}) collective-permute-start(f32[256,128]{1,0:T(8,128)} %get-tuple-element.11), channel_id=1, source_target_pairs={{0,16},{16,0},{1,17},{17,1},{2,18},{18,2},{3,19},{19,3},{4,20},{20... | collective-permute-start | bytes 393224 | tf_op jit(solution)/shard_map/ppermute | solution.py:352
  12.8 0.0 collective-permute-start.1
  12.8 0.7 %collective-permute-start.2 = (f32[64,8,128]{2,1,0:T(8,128)}, f32[64,8,128]{2,1,0:T(8,128)S(1)}, u32[]{:S(2)}, u32[]{:S(2)}) collective-permute-start(f32[64,8,128]{2,1,0:T(8,128)} %get-tuple-element.13), channel_id=1, source_target_pairs={{1,2},{2,1},{3,4},{4,3},{5,6},{6,5},{7,8},{8,7},{9,10},{10,9},{11,... | collective-permute-start | bytes 786440 | tf_op jit(solution)/shard_map/ppermute | solution.py:348
  13.4 1.5 %slice_bitcast_fusion = (bf16[512,768]{1,0:T(8,128)(2,1)S(1)}, bf16[512,768]{1,0:T(8,128)(2,1)S(1)}) fusion(bf16[2,512,768]{2,1,0:T(8,128)(2,1)} %param.11), kind=kLoop, calls=%fused_computation | loop fusion | bytes 3145728 | tf_op jit(solution)/shard_map/squeeze | solution.py:366
  14.9 0.0 copy-start
  14.9 0.0 copy-start.1
  14.9 0.0 copy-start.2
  14.9 0.0 copy-start.3
  15.0 3.0 %collective-permute-done.row_ref.refs_4_ = f32[256,128]{1,0:T(8,128)S(1)} collective-permute-done((f32[256,128]{1,0:T(8,128)}, f32[256,128]{1,0:T(8,128)S(1)}, u32[]{:S(2)}, u32[]{:S(2)}) %collective-permute-start) | collective-permute-done | bytes 131104 | tf_op jit(solution)/shard_map/ppermute | solution.py:352
  17.9 1.3 %all-to-all-done.trace_ref = bf16[32,16,128]{2,1,0:T(8,128)(2,1)S(1)} async-done(((bf16[32,16,128]{2,1,0:T(8,128)(2,1)}), bf16[32,16,128]{2,1,0:T(8,128)(2,1)S(1)}, u32[]{:S(2)}, u32[]{:S(2)}) %all-to-all-start) | async-done | bytes 131104 | tf_op jit(solution)/shard_map/all_to_all | solution.py:355
  19.2 1.4 %boundary.1 = bf16[16,16,128]{2,1,0:T(8,128)(2,1)} custom-call(bf16[32,16,128]{2,1,0:T(8,128)(2,1)S(1)} %all-to-all-done.trace_ref, bf16[512,768]{1,0:T(8,128)(2,1)S(1)} %get-tuple-element.19.real_ref, bf16[512,768]{1,0:T(8,128)(2,1)S(1)} %get-tuple-element.18.imag_ref, f32[256,128]{1,0:T(8,128)S(1)} %collective-permute-done.row_ref.refs_4_), custom_call_target="tpu_custom_call" | custom-call | tf_op jit(solution)/shard_map/boundary/pallas_call | solution.py:359
  20.6 4.8 %all-to-all-start.1 = ((bf16[16,16,128]{2,1,0:T(8,128)(2,1)}), bf16[16,16,128]{2,1,0:T(8,128)(2,1)S(1)}, u32[]{:S(2)}, u32[]{:S(2)}) async-start(bf16[16,16,128]{2,1,0:T(8,128)(2,1)} %boundary.1), calls=%async_computation.1 | async-start | bytes 131072 | tf_op jit(solution)/shard_map/all_to_all | solution.py:367
  25.5 0.0 collective-permute-done.1
  25.5 0.0 collective-permute-done.2
  25.5 1.0 %collective-permute-start.3 = (bf16[128,128]{1,0:T(8,128)(2,1)S(1)}, bf16[128,128]{1,0:T(8,128)(2,1)S(1)}, u32[]{:S(2)}, u32[]{:S(2)}) collective-permute-start(bf16[128,128]{1,0:T(8,128)(2,1)S(1)} %corners.1), channel_id=1, source_target_pairs={{0,16},{16,0},{1,17},{17,1},{2,18},{18,2},{3,19},{19,3},{4,20},{20... | collective-permute-start | bytes 98312 | tf_op jit(solution)/shard_map/ppermute | solution.py:380
  26.5 0.0 copy-done
  26.5 0.0 copy-done.1
  26.5 0.0 copy-done.2
  26.5 0.0 copy-done.3
  26.5 2.5 %volume.1 = (f32[2048,128]{1,0:T(8,128)}, f32[2,512,128]{2,1,0:T(8,128)S(1)}) custom-call(f32[2048,128]{1,0:T(8,128)S(1)} %bitcast.15, f32[32,128]{1,0:T(8,128)S(1)} %bitcast.21, f32[64,1,384]{2,1,0:T(1,128)S(1)} %bitcast.20, s32[1,384]{1,0:T(1,128)S(1)} %bitcast.24, f32[256,128]{1,0:T(8,128)S(1)} %collective-permute-done.row_ref.refs_4_, ...), custom_call_target="tpu_custom_call" | custom-call | tf_op jit(solution)/shard_map/volume/pallas_call | solution.py:384
  29.0 0.5 %collective-permute-done.3.refs_0_ = bf16[128,128]{1,0:T(8,128)(2,1)S(1)} collective-permute-done((bf16[128,128]{1,0:T(8,128)(2,1)S(1)}, bf16[128,128]{1,0:T(8,128)(2,1)S(1)}, u32[]{:S(2)}, u32[]{:S(2)}) %collective-permute-start.3) | collective-permute-done | bytes 32800 | tf_op jit(solution)/shard_map/ppermute | solution.py:380
  29.5 0.0 all-to-all-done.1.part_ref
  29.5 0.9 %last.1 = (f32[32,64]{1,0:T(8,128)}, f32[64,32,128]{2,1,0:T(8,128)}) custom-call(bf16[16,16,128]{2,1,0:T(8,128)(2,1)S(1)} %all-to-all-done.1.part_ref, f32[32,128]{1,0:T(8,128)S(1)} %bitcast.22, f32[2,512,128]{2,1,0:T(8,128)S(1)} %get-tuple-element.14.edge_ref, bf16[128,128]{1,0:T(8,128)(2,1)S(1)} %collective-permute-done.3.refs_0_, ...), custom_call_target="tpu_custom_call", output_to_operand_aliasing={{1}: (4, {})} | custom-call | tf_op jit(solution)/shard_map/last/pallas_call | solution.py:400
  (1 shorter events, 0.0 us)
Async XLA Ops:
  3.6 15.6 %all-to-all-start = ((bf16[32,16,128]{2,1,0:T(8,128)(2,1)}), bf16[32,16,128]{2,1,0:T(8,128)(2,1)S(1)}, u32[]{:S(2)}, u32[]{:S(2)}) async-start(bf16[32,16,128]{2,1,0:T(8,128)(2,1)} %get-tuple-element.10), calls=%async_computation | async-start | bytes 262144 | tf_op jit(solution)/shard_map/all_to_all | solution.py:355
  10.9 7.0 %collective-permute-start = (f32[256,128]{1,0:T(8,128)}, f32[256,128]{1,0:T(8,128)S(1)}, u32[]{:S(2)}, u32[]{:S(2)}) collective-permute-start(f32[256,128]{1,0:T(8,128)} %get-tuple-element.11), channel_id=1, source_target_pairs={{0,16},{16,0},{1,17},{17,1},{2,18},{18,2},{3,19},{19,3},{4,20},{20... | collective-permute-start | bytes 393224 | tf_op jit(solution)/shard_map/ppermute | solution.py:352
  12.8 12.7 %collective-permute-start.1 = (f32[64,8,128]{2,1,0:T(8,128)}, f32[64,8,128]{2,1,0:T(8,128)S(1)}, u32[]{:S(2)}, u32[]{:S(2)}) collective-permute-start(f32[64,8,128]{2,1,0:T(8,128)} %get-tuple-element.12), channel_id=1, source_target_pairs={{0,1},{1,0},{2,3},{3,2},{4,5},{5,4},{6,7},{7,6},{8,9},{9,8},{10,11... | collective-permute-start | bytes 786440 | tf_op jit(solution)/shard_map/ppermute | solution.py:348
  12.8 12.7 %collective-permute-start.2 = (f32[64,8,128]{2,1,0:T(8,128)}, f32[64,8,128]{2,1,0:T(8,128)S(1)}, u32[]{:S(2)}, u32[]{:S(2)}) collective-permute-start(f32[64,8,128]{2,1,0:T(8,128)} %get-tuple-element.13), channel_id=1, source_target_pairs={{1,2},{2,1},{3,4},{4,3},{5,6},{6,5},{7,8},{8,7},{9,10},{10,9},{11,... | collective-permute-start | bytes 786440 | tf_op jit(solution)/shard_map/ppermute | solution.py:348
  14.9 11.6 %copy-start = (f32[64,4,8,128]{3,2,1,0:T(8,128)S(1)}, f32[64,4,8,128]{3,2,1,0:T(8,128)}, u32[]{:S(2)}) copy-start(f32[64,4,8,128]{3,2,1,0:T(8,128)} %param.6) | copy-start | bytes 3145732
  14.9 11.6 %copy-start.1 = (f32[64,1,1,384]{3,2,1,0:T(1,128)S(1)}, f32[64,1,1,384]{3,2,1,0:T(1,128)}, u32[]{:S(2)}) copy-start(f32[64,1,1,384]{3,2,1,0:T(1,128)} %param.8) | copy-start | bytes 294916
  14.9 11.6 %copy-start.2 = (f32[4,8,128]{2,1,0:T(8,128)S(1)}, f32[4,8,128]{2,1,0:T(8,128)}, u32[]{:S(2)}) copy-start(f32[4,8,128]{2,1,0:T(8,128)} %param.7) | copy-start | bytes 49156
  14.9 11.6 %copy-start.3 = (s32[1,1,384]{2,1,0:T(1,128)S(1)}, s32[1,1,384]{2,1,0:T(1,128)}, u32[]{:S(2)}) copy-start(s32[1,1,384]{2,1,0:T(1,128)} %param.9) | copy-start | bytes 4612
  20.6 8.9 %all-to-all-start.1 = ((bf16[16,16,128]{2,1,0:T(8,128)(2,1)}), bf16[16,16,128]{2,1,0:T(8,128)(2,1)S(1)}, u32[]{:S(2)}, u32[]{:S(2)}) async-start(bf16[16,16,128]{2,1,0:T(8,128)(2,1)} %boundary.1), calls=%async_computation.1 | async-start | bytes 131072 | tf_op jit(solution)/shard_map/all_to_all | solution.py:367
  25.5 4.0 %collective-permute-start.3 = (bf16[128,128]{1,0:T(8,128)(2,1)S(1)}, bf16[128,128]{1,0:T(8,128)(2,1)S(1)}, u32[]{:S(2)}, u32[]{:S(2)}) collective-permute-start(bf16[128,128]{1,0:T(8,128)(2,1)S(1)} %corners.1), channel_id=1, source_target_pairs={{0,16},{16,0},{1,17},{17,1},{2,18},{18,2},{3,19},{19,3},{4,20},{20... | collective-permute-start | bytes 98312 | tf_op jit(solution)/shard_map/ppermute | solution.py:380

commit v5 on v4

--- a/solution.py
+++ b/solution.py
@@ -7,7 +7,6 @@
 from jax.experimental.pallas import tpu as pltpu
 from jax.sharding import PartitionSpec as P
 
-TILE_ROWS = 16
 SMALL = 8 * 2**20
 WHOLE = 64560 * 2**10
 
@@ -30,8 +29,13 @@
 
 
 def root_first(count):
-    root = count * 11 // 16
+    root = count * 9 // 16
     return [root] + [index for index in range(count) if index != root]
+
+
+def tile_shape(slot_len, comps):
+    groups = 3 if slot_len % 6 == 0 else 1
+    return slot_len // (2 * groups), groups
 
 
 def trace_kernel(dims, row_swaps, target_hbm, cell_hbm, field_hbm, tile_hbm, *rest):
@@ -91,26 +95,18 @@
     row_odd = lax.rem(lax.axis_index("row"), 2)
     for swap, face_ref in enumerate(row_faces):
         layer = jnp.where(row_odd == swap, width_y - 1, 0)
-        side_ref[swap] = flat[pl.ds(layer, comps * width_x, stride=width_y), :]
+        side_ref[swap] = flat[pl.ds(layer, comps * width_x, stride=width_y), :].astype(jnp.bfloat16)
         sent.append(pltpu.make_async_copy(side_ref.at[swap], face_ref, left_sem.at[2 + swap]))
         sent[-1].start()
     by_node = jnp.concatenate(found, axis=0).T
     copies[-1].wait()
-    left_len = min(slot_len, TILE_ROWS)
+    tile_rows, groups = tile_shape(slot_len, comps)
     for slot in range(cols):
-        piece = by_node[slot * slot_len : (slot + 1) * slot_len]
-        left = piece[:left_len]
-        right = piece[left_len:]
-        if left_len < TILE_ROWS:
-            left = jnp.concatenate(
-                [left, jnp.zeros((TILE_ROWS - left_len, comps), jnp.float32)], axis=0
-            )
-        gap = TILE_ROWS - (slot_len - left_len)
-        if slot_len == left_len:
-            right = jnp.zeros((TILE_ROWS, comps), jnp.float32)
-        elif gap:
-            right = jnp.concatenate([right, jnp.zeros((gap, comps), jnp.float32)], axis=0)
-        tile = jnp.concatenate([left, right], axis=1).astype(jnp.bfloat16)
+        pieces = []
+        for group in range(2 * groups):
+            start = slot * slot_len + group * tile_rows
+            pieces.append(by_node[start : start + tile_rows])
+        tile = jnp.concatenate(pieces, axis=1).astype(jnp.bfloat16)
         for row in range(rows):
             tile_ref[row * cols + target_ref[0, slot]] = tile
     sent.append(pltpu.make_async_copy(tile_ref, tile_hbm, left_sem.at[2 + row_swaps]))
@@ -130,20 +126,15 @@
             ].astype(out_ref.dtype)
 
 
-def unpack_tiles(tiles, slot_len, comps):
-    left_len = min(slot_len, TILE_ROWS)
-    parts = [tiles[:, :left_len, :comps]]
-    if slot_len > left_len:
-        parts.append(tiles[:, : slot_len - left_len, comps:])
-    both = jnp.concatenate(parts, axis=1) if len(parts) > 1 else parts[0]
-    return both.reshape(tiles.shape[0] * slot_len, comps)
+def unpack_tiles(tiles, comps):
+    groups = tiles.shape[2] // comps
+    parts = [tiles[:, :, group * comps : (group + 1) * comps] for group in range(groups)]
+    return jnp.concatenate(parts, axis=1).reshape(-1, comps)
 
 
 def boundary_kernel(slot_len, own_rows, trace_ref, real_ref, imag_ref, row_ref, out_ref):
     if len(trace_ref.shape) == 3:
-        traces = unpack_tiles(
-            trace_ref[...].astype(jnp.float32), slot_len, trace_ref.shape[2] // 2
-        )
+        traces = unpack_tiles(trace_ref[...].astype(jnp.float32), 2 * out_ref.shape[2] // 4)
     else:
         traces = trace_ref[...].astype(jnp.float32)
     comps = traces.shape[1]
@@ -175,7 +166,9 @@
     field_ref, medium_ref, flux_ref, cell_ref = refs[:4]
     row_refs = refs[4 : 4 + row_swaps]
     first_ref, second_ref = refs[4 + row_swaps : 6 + row_swaps]
-    out_ref, edge_ref, lhs_ref, taken_ref = refs[6 + row_swaps :]
+    out_hbm, edge_ref, lhs_ref, taken_ref, out_ref, side_ref, sent = refs[6 + row_swaps :]
+    for index, row_ref in enumerate(row_refs):
+        side_ref[index] = row_ref[...].astype(jnp.float32)
     lines = width_x * width_y
     nodes = cell_ref.shape[1]
     fold = 2
@@ -222,7 +215,7 @@
         )
         ends = []
         for x in range(width_x):
-            line = [wide(row_ref, comp * width_x + x) for row_ref in row_refs]
+            line = [wide(side_ref.at[index], comp * width_x + x) for index in range(row_swaps)]
             ends.append(jnp.where(from_first, line[0], line[1] if row_swaps > 1 else 0.0))
         none = jnp.zeros(shape, jnp.float32)
         ends = [none] + ends + [none]
@@ -251,8 +244,19 @@
                 if x == side * (width_x - 1):
                     edge_ref[side, face, :] = image
 
-    for comp in range(comps):
-        component(comp)
+    steps = sent.shape[0]
+    together = comps // steps
+    copies = []
+    for step in range(steps):
+        for comp in range(step * together, (step + 1) * together):
+            component(comp)
+        here = pl.ds(step * together * lines, together * lines)
+        copies.append(
+            pltpu.make_async_copy(out_ref.at[here, :], out_hbm.at[here, :], sent.at[step])
+        )
+        copies[-1].start()
+    for copy in copies:
+        copy.wait()
 
 
 def last_kernel(
@@ -318,6 +322,8 @@
     params = pltpu.CompilerParams(vmem_limit_bytes=SMALL)
 
     chunks, fold = 2, 4
+    tile_rows, groups = tile_shape(slot_len, comps)
+    tile_dims = (tile_rows, 2 * groups * comps)
     field = wave_field.reshape(comps * lines, depth)
     cells = node_cell.reshape(1, nodes)
     targets = block_target.reshape(1, cols)
@@ -326,8 +332,8 @@
 
     tiles, *faces = pl.pallas_call(
         functools.partial(trace_kernel, dims, row_swaps),
-        out_shape=[jax.ShapeDtypeStruct((rows * cols, TILE_ROWS, 2 * comps), bf16)]
-        + [jax.ShapeDtypeStruct((comps * width_x, depth), f32)] * row_swaps
+        out_shape=[jax.ShapeDtypeStruct((rows * cols,) + tile_dims, bf16)]
+        + [jax.ShapeDtypeStruct((comps * width_x, depth), bf16)] * row_swaps
         + [jax.ShapeDtypeStruct((comps, width_y, depth), f32)] * 2,
         in_specs=[hbm()] * 3,
         out_specs=[hbm()] * (3 + row_swaps),
@@ -336,8 +342,8 @@
             pltpu.VMEM((1, nodes), jnp.int32),
             pltpu.VMEM((comps, lines, depth), f32),
             pltpu.VMEM((chunks, lines // fold, comps // chunks, fold * depth), bf16),
-            pltpu.VMEM((rows * cols, TILE_ROWS, 2 * comps), bf16),
-            pltpu.VMEM((row_swaps, comps * width_x, depth), f32),
+            pltpu.VMEM((rows * cols,) + tile_dims, bf16),
+            pltpu.VMEM((row_swaps, comps * width_x, depth), bf16),
             pltpu.SemaphoreType.DMA((chunks + 2,)),
             pltpu.SemaphoreType.DMA((3 + row_swaps,)),
         ],
@@ -355,7 +361,7 @@
     received = lax.all_to_all(tiles, ("row", "col"), 0, 0, tiled=True)
 
     if slot_len % 8:
-        received = unpack_tiles(received, slot_len, comps)
+        received = unpack_tiles(received, comps)
     shares = pl.pallas_call(
         functools.partial(boundary_kernel, slot_len, own_rows),
         out_shape=jax.ShapeDtypeStruct((cols, own_rows // 2, 2 * comps), bf16),
@@ -388,10 +394,13 @@
             jax.ShapeDtypeStruct((2, comps * width_y, depth), f32),
         ],
         in_specs=[vmem()] * (6 + row_swaps),
-        out_specs=[vmem()] * 2,
+        out_specs=[hbm(), vmem()],
         scratch_shapes=[
             pltpu.VMEM((comps * lines // 2, nodes), bf16),
             pltpu.VMEM((comps * lines // 2, 2 * depth), f32),
+            pltpu.VMEM((comps * lines, depth), f32),
+            pltpu.VMEM((row_swaps, comps * width_x, depth), f32),
+            pltpu.SemaphoreType.DMA((8,)),
         ],
         compiler_params=params,
         name="volume",

time: 30.7 us -> 30.1 us (0.980)
  starting transfers between devices: 15.6 us -> 14.7 us
  waiting for transfers between devices: 4.82 us -> 5.4 us
    ppermute x1, waiting for transfers between devices: 2.99 us -> 0.91 us  [on_device(): lax.ppermute(face, 'row', swap_pairs(rows, swap))]
    all_to_all x1, waiting for transfers between devices: 1.3 us -> 2.96 us  [on_device(): received = lax.all_to_all(tiles, ('row', 'col'), 0, 0, tiled=True)]
    ppermute x1, waiting for transfers between devices: 0.52 us -> 1.11 us  [on_device(): lax.ppermute(lines_of, 'row', swap_pairs(rows, swap))]
    all_to_all x1, starting transfers between devices: 4.83 us -> 4.25 us  [on_device(): lax.all_to_all(shares, 'col', 0, 0, tiled=True, axis_index_groups=[root_f...]
    all_to_all x1, waiting for transfers between devices: 0.01 us -> 0.41 us  [on_device(): lax.all_to_all(shares, 'col', 0, 0, tiled=True, axis_index_groups=[root_f...]
    ppermute x1, starting transfers between devices: 0.98 us -> 0.61 us  [on_device(): lax.ppermute(lines_of, 'row', swap_pairs(rows, swap))]
  transfers between devices with their start and end apart: 6 -> 6, of which waited for: 3 -> 4; matrix products, arithmetic and copies ran while one was open for 5% -> 5% of each run, Pallas kernels for 13% -> 12%
where the time goes in v5:
time: 30.1 us; the launch traced here: 29.8 us
  starting transfers between devices  14.7 us (49%)
  Pallas kernels  7.56 us (25%)
  waiting for transfers between devices  5.4 us (18%)
  local copies, waits for them, and re-layouts  1.5 us (5%)
  between operations  0.72 us (2%)
    all_to_all x1, starting transfers between devices, on_device(): received = lax.all_to_all(tiles, ('row', 'col'), 0, 0, tiled=True)  7.3 us
    all_to_all x1, starting transfers between devices, on_device(): lax.all_to_all(shares, 'col', 0, 0, tiled=True, axis_index_groups=[root_f...  4.25 us
    pallas_call x1, Pallas kernels, on_device(): pl.pallas_call(functools.partial(trace_kernel, dims, row_swaps), out_shap...  2.97 us
    all_to_all x1, waiting for transfers between devices, on_device(): received = lax.all_to_all(tiles, ('row', 'col'), 0, 0, tiled=True)  2.96 us
    pallas_call x1, Pallas kernels, on_device(): pl.pallas_call(functools.partial(volume_kernel, dims, row_swaps), out_sha...  2.23 us
    ppermute x1, starting transfers between devices, on_device(): lax.ppermute(face, 'row', swap_pairs(rows, swap))  1.83 us
    squeeze x1, local copies, waits for them, and re-layouts, on_device(): boundary_matrix[1]  1.48 us
    pallas_call x1, Pallas kernels, on_device(): pl.pallas_call(functools.partial(boundary_kernel, slot_len, own_rows), ou...  1.39 us
  transfers between devices with their start and end apart: 6, of which 4 were waited for; matrix products, arithmetic and copies ran while one was open for 5% of the time, Pallas kernels for 12%

profile of v5, /device:TPU:0, one launch (start us, length us, event | category | flops | bytes accessed | tf_op | source)
XLA Modules:
  0.0 29.8 jit_solution(4771166248687053306)
XLA Ops:
  0.6 3.0 %traces.1 = (bf16[32,4,384]{2,1,0:T(4,128)(2,1)}, bf16[256,128]{1,0:T(8,128)(2,1)}, f32[64,8,128]{2,1,0:T(8,128)}, f32[64,8,128]{2,1,0:T(8,128)}) custom-call(s32[1,16]{1,0:T(1,128)} %bitcast.27, s32[1,384]{1,0:T(1,128)} %bitcast.23, f32[64,32,128]{2,1,0:T(8,128)} %bitcast.14), custom_call_target="tpu_custom_call" | custom-call | tf_op jit(solution)/shard_map/traces/pallas_call | solution.py:333
  3.6 7.3 %all-to-all-start = ((bf16[32,4,384]{2,1,0:T(4,128)(2,1)}), bf16[32,4,384]{2,1,0:T(4,128)(2,1)S(1)}, u32[]{:S(2)}, u32[]{:S(2)}) async-start(bf16[32,4,384]{2,1,0:T(4,128)(2,1)} %get-tuple-element.10), calls=%async_computation | async-start | bytes 196608 | tf_op jit(solution)/shard_map/all_to_all | solution.py:361
  10.9 1.8 %collective-permute-start = (bf16[256,128]{1,0:T(8,128)(2,1)}, bf16[256,128]{1,0:T(8,128)(2,1)S(1)}, u32[]{:S(2)}, u32[]{:S(2)}) collective-permute-start(bf16[256,128]{1,0:T(8,128)(2,1)} %get-tuple-element.11), channel_id=1, source_target_pairs={{0,16},{16,0},{1,17},{17,1},{2,18},{18,2},{3,19},{19,3},{4,20},{20... | collective-permute-start | bytes 196616 | tf_op jit(solution)/shard_map/ppermute | solution.py:358
  12.8 0.0 collective-permute-start.1
  12.8 0.7 %collective-permute-start.2 = (f32[64,8,128]{2,1,0:T(8,128)}, f32[64,8,128]{2,1,0:T(8,128)S(1)}, u32[]{:S(2)}, u32[]{:S(2)}) collective-permute-start(f32[64,8,128]{2,1,0:T(8,128)} %get-tuple-element.13), channel_id=1, source_target_pairs={{1,2},{2,1},{3,4},{4,3},{5,6},{6,5},{7,8},{8,7},{9,10},{10,9},{11,... | collective-permute-start | bytes 786440 | tf_op jit(solution)/shard_map/ppermute | solution.py:354
  13.4 1.5 %slice_bitcast_fusion = (bf16[512,768]{1,0:T(8,128)(2,1)S(1)}, bf16[512,768]{1,0:T(8,128)(2,1)S(1)}) fusion(bf16[2,512,768]{2,1,0:T(8,128)(2,1)} %param.11), kind=kLoop, calls=%fused_computation | loop fusion | bytes 3145728 | tf_op jit(solution)/shard_map/squeeze | solution.py:372
  14.9 0.0 copy-start
  14.9 0.0 copy-start.1
  14.9 0.0 copy-start.2
  14.9 0.0 copy-start.3
  15.0 0.9 %collective-permute-done.row_ref.refs_4_ = bf16[256,128]{1,0:T(8,128)(2,1)S(1)} collective-permute-done((bf16[256,128]{1,0:T(8,128)(2,1)}, bf16[256,128]{1,0:T(8,128)(2,1)S(1)}, u32[]{:S(2)}, u32[]{:S(2)}) %collective-permute-start) | collective-permute-done | bytes 65568 | tf_op jit(solution)/shard_map/ppermute | solution.py:358
  15.9 3.0 %all-to-all-done.trace_ref = bf16[32,4,384]{2,1,0:T(4,128)(2,1)S(1)} async-done(((bf16[32,4,384]{2,1,0:T(4,128)(2,1)}), bf16[32,4,384]{2,1,0:T(4,128)(2,1)S(1)}, u32[]{:S(2)}, u32[]{:S(2)}) %all-to-all-start) | async-done | bytes 98336 | tf_op jit(solution)/shard_map/all_to_all | solution.py:361
  18.8 1.4 %boundary.1 = bf16[16,16,128]{2,1,0:T(8,128)(2,1)} custom-call(bf16[32,4,384]{2,1,0:T(4,128)(2,1)S(1)} %all-to-all-done.trace_ref, bf16[512,768]{1,0:T(8,128)(2,1)S(1)} %get-tuple-element.19.real_ref, bf16[512,768]{1,0:T(8,128)(2,1)S(1)} %get-tuple-element.18.imag_ref, bf16[256,128]{1,0:T(8,128)(2,1)S(1)} %collective-permute-done.row_ref.refs_4_), custom_call_target="tpu_custom_call" | custom-call | tf_op jit(solution)/shard_map/boundary/pallas_call | solution.py:365
  20.2 4.2 %all-to-all-start.1 = ((bf16[16,16,128]{2,1,0:T(8,128)(2,1)}), bf16[16,16,128]{2,1,0:T(8,128)(2,1)S(1)}, u32[]{:S(2)}, u32[]{:S(2)}) async-start(bf16[16,16,128]{2,1,0:T(8,128)(2,1)} %boundary.1), calls=%async_computation.1 | async-start | bytes 131072 | tf_op jit(solution)/shard_map/all_to_all | solution.py:373
  24.5 0.0 collective-permute-done.1
  24.5 0.0 collective-permute-done.2
  24.5 0.6 %collective-permute-start.3 = (bf16[128,128]{1,0:T(8,128)(2,1)S(1)}, bf16[128,128]{1,0:T(8,128)(2,1)S(1)}, u32[]{:S(2)}, u32[]{:S(2)}) collective-permute-start(bf16[128,128]{1,0:T(8,128)(2,1)S(1)} %corners.1), channel_id=1, source_target_pairs={{0,16},{16,0},{1,17},{17,1},{2,18},{18,2},{3,19},{19,3},{4,20},{20... | collective-permute-start | bytes 98312 | tf_op jit(solution)/shard_map/ppermute | solution.py:386
  25.1 0.0 copy-done
  25.1 0.0 copy-done.1
  25.1 0.0 copy-done.2
  25.1 0.0 copy-done.3
  25.2 2.2 %volume.1 = (f32[2048,128]{1,0:T(8,128)}, f32[2,512,128]{2,1,0:T(8,128)S(1)}) custom-call(f32[2048,128]{1,0:T(8,128)S(1)} %bitcast.15, f32[32,128]{1,0:T(8,128)S(1)} %bitcast.21, f32[64,1,384]{2,1,0:T(1,128)S(1)} %bitcast.20, s32[1,384]{1,0:T(1,128)S(1)} %bitcast.24, bf16[256,128]{1,0:T(8,128)(2,1)S(1)} %collective-permute-done.row_ref.refs_4_, ...), custom_call_target="tpu_custom_call" | custom-call | tf_op jit(solution)/shard_map/volume/pallas_call | solution.py:390
  27.4 1.1 %collective-permute-done.3.refs_0_ = bf16[128,128]{1,0:T(8,128)(2,1)S(1)} collective-permute-done((bf16[128,128]{1,0:T(8,128)(2,1)S(1)}, bf16[128,128]{1,0:T(8,128)(2,1)S(1)}, u32[]{:S(2)}, u32[]{:S(2)}) %collective-permute-start.3) | collective-permute-done | bytes 32800 | tf_op jit(solution)/shard_map/ppermute | solution.py:386
  28.5 0.4 %all-to-all-done.1.part_ref = bf16[16,16,128]{2,1,0:T(8,128)(2,1)S(1)} async-done(((bf16[16,16,128]{2,1,0:T(8,128)(2,1)}), bf16[16,16,128]{2,1,0:T(8,128)(2,1)S(1)}, u32[]{:S(2)}, u32[]{:S(2)}) %all-to-all-start.1) | async-done | bytes 65568 | tf_op jit(solution)/shard_map/all_to_all | solution.py:373
  28.9 0.9 %last.1 = (f32[32,64]{1,0:T(8,128)}, f32[64,32,128]{2,1,0:T(8,128)}) custom-call(bf16[16,16,128]{2,1,0:T(8,128)(2,1)S(1)} %all-to-all-done.1.part_ref, f32[32,128]{1,0:T(8,128)S(1)} %bitcast.22, f32[2,512,128]{2,1,0:T(8,128)S(1)} %get-tuple-element.14.edge_ref, bf16[128,128]{1,0:T(8,128)(2,1)S(1)} %collective-permute-done.3.refs_0_, ...), custom_call_target="tpu_custom_call", output_to_operand_aliasing={{1}: (4, {})} | custom-call | tf_op jit(solution)/shard_map/last/pallas_call | solution.py:409
  (1 shorter events, 0.0 us)
Async XLA Ops:
  3.6 15.2 %all-to-all-start = ((bf16[32,4,384]{2,1,0:T(4,128)(2,1)}), bf16[32,4,384]{2,1,0:T(4,128)(2,1)S(1)}, u32[]{:S(2)}, u32[]{:S(2)}) async-start(bf16[32,4,384]{2,1,0:T(4,128)(2,1)} %get-tuple-element.10), calls=%async_computation | async-start | bytes 196608 | tf_op jit(solution)/shard_map/all_to_all | solution.py:361
  10.9 5.0 %collective-permute-start = (bf16[256,128]{1,0:T(8,128)(2,1)}, bf16[256,128]{1,0:T(8,128)(2,1)S(1)}, u32[]{:S(2)}, u32[]{:S(2)}) collective-permute-start(bf16[256,128]{1,0:T(8,128)(2,1)} %get-tuple-element.11), channel_id=1, source_target_pairs={{0,16},{16,0},{1,17},{17,1},{2,18},{18,2},{3,19},{19,3},{4,20},{20... | collective-permute-start | bytes 196616 | tf_op jit(solution)/shard_map/ppermute | solution.py:358
  12.8 11.7 %collective-permute-start.1 = (f32[64,8,128]{2,1,0:T(8,128)}, f32[64,8,128]{2,1,0:T(8,128)S(1)}, u32[]{:S(2)}, u32[]{:S(2)}) collective-permute-start(f32[64,8,128]{2,1,0:T(8,128)} %get-tuple-element.12), channel_id=1, source_target_pairs={{0,1},{1,0},{2,3},{3,2},{4,5},{5,4},{6,7},{7,6},{8,9},{9,8},{10,11... | collective-permute-start | bytes 786440 | tf_op jit(solution)/shard_map/ppermute | solution.py:354
  12.8 11.7 %collective-permute-start.2 = (f32[64,8,128]{2,1,0:T(8,128)}, f32[64,8,128]{2,1,0:T(8,128)S(1)}, u32[]{:S(2)}, u32[]{:S(2)}) collective-permute-start(f32[64,8,128]{2,1,0:T(8,128)} %get-tuple-element.13), channel_id=1, source_target_pairs={{1,2},{2,1},{3,4},{4,3},{5,6},{6,5},{7,8},{8,7},{9,10},{10,9},{11,... | collective-permute-start | bytes 786440 | tf_op jit(solution)/shard_map/ppermute | solution.py:354
  14.9 10.2 %copy-start = (f32[64,4,8,128]{3,2,1,0:T(8,128)S(1)}, f32[64,4,8,128]{3,2,1,0:T(8,128)}, u32[]{:S(2)}) copy-start(f32[64,4,8,128]{3,2,1,0:T(8,128)} %param.6) | copy-start | bytes 3145732
  14.9 10.2 %copy-start.1 = (f32[64,1,1,384]{3,2,1,0:T(1,128)S(1)}, f32[64,1,1,384]{3,2,1,0:T(1,128)}, u32[]{:S(2)}) copy-start(f32[64,1,1,384]{3,2,1,0:T(1,128)} %param.8) | copy-start | bytes 294916
  14.9 10.2 %copy-start.2 = (f32[4,8,128]{2,1,0:T(8,128)S(1)}, f32[4,8,128]{2,1,0:T(8,128)}, u32[]{:S(2)}) copy-start(f32[4,8,128]{2,1,0:T(8,128)} %param.7) | copy-start | bytes 49156
  14.9 10.2 %copy-start.3 = (s32[1,1,384]{2,1,0:T(1,128)S(1)}, s32[1,1,384]{2,1,0:T(1,128)}, u32[]{:S(2)}) copy-start(s32[1,1,384]{2,1,0:T(1,128)} %param.9) | copy-start | bytes 4612
  20.2 8.7 %all-to-all-start.1 = ((bf16[16,16,128]{2,1,0:T(8,128)(2,1)}), bf16[16,16,128]{2,1,0:T(8,128)(2,1)S(1)}, u32[]{:S(2)}, u32[]{:S(2)}) async-start(bf16[16,16,128]{2,1,0:T(8,128)(2,1)} %boundary.1), calls=%async_computation.1 | async-start | bytes 131072 | tf_op jit(solution)/shard_map/all_to_all | solution.py:373
  24.5 4.0 %collective-permute-start.3 = (bf16[128,128]{1,0:T(8,128)(2,1)S(1)}, bf16[128,128]{1,0:T(8,128)(2,1)S(1)}, u32[]{:S(2)}, u32[]{:S(2)}) collective-permute-start(bf16[128,128]{1,0:T(8,128)(2,1)S(1)} %corners.1), channel_id=1, source_target_pairs={{0,16},{16,0},{1,17},{17,1},{2,18},{18,2},{3,19},{19,3},{4,20},{20... | collective-permute-start | bytes 98312 | tf_op jit(solution)/shard_map/ppermute | solution.py:386

commit v6 on v4

--- a/solution.py
+++ b/solution.py
@@ -30,7 +30,7 @@
 
 
 def root_first(count):
-    root = count * 11 // 16
+    root = count * 9 // 16
     return [root] + [index for index in range(count) if index != root]
 
 
@@ -90,8 +90,10 @@
         sent[-1].start()
     row_odd = lax.rem(lax.axis_index("row"), 2)
     for swap, face_ref in enumerate(row_faces):
-        layer = jnp.where(row_odd == swap, width_y - 1, 0)
-        side_ref[swap] = flat[pl.ds(layer, comps * width_x, stride=width_y), :]
+        low, high = (
+            flat[pl.ds(layer, comps * width_x, stride=width_y), :] for layer in (0, width_y - 1)
+        )
+        side_ref[swap] = jnp.where(row_odd == swap, high, low).astype(jnp.bfloat16)
         sent.append(pltpu.make_async_copy(side_ref.at[swap], face_ref, left_sem.at[2 + swap]))
         sent[-1].start()
     by_node = jnp.concatenate(found, axis=0).T
@@ -123,11 +125,11 @@
     comps, width_x, width_y = dims[:3]
     odd = lax.rem(lax.axis_index("row"), 2)
     for swap, out_ref in enumerate(out_refs):
-        layer = jnp.where(odd == swap, width_y - 1, 0)
         for index, ref in enumerate((first_ref, second_ref)):
-            out_ref[pl.ds(index * comps, comps), :] = ref[
-                pl.ds(layer, comps, stride=width_y), :
-            ].astype(out_ref.dtype)
+            low, high = (ref[pl.ds(layer, comps, stride=width_y), :] for layer in (0, width_y - 1))
+            out_ref[pl.ds(index * comps, comps), :] = jnp.where(odd == swap, high, low).astype(
+                out_ref.dtype
+            )
 
 
 def unpack_tiles(tiles, slot_len, comps):
@@ -175,7 +177,9 @@
     field_ref, medium_ref, flux_ref, cell_ref = refs[:4]
     row_refs = refs[4 : 4 + row_swaps]
     first_ref, second_ref = refs[4 + row_swaps : 6 + row_swaps]
-    out_ref, edge_ref, lhs_ref, taken_ref = refs[6 + row_swaps :]
+    out_hbm, edge_ref, lhs_ref, taken_ref, out_ref, side_ref, sent = refs[6 + row_swaps :]
+    for index, row_ref in enumerate(row_refs):
+        side_ref[index] = row_ref[...].astype(jnp.float32)
     lines = width_x * width_y
     nodes = cell_ref.shape[1]
     fold = 2
@@ -222,7 +226,7 @@
         )
         ends = []
         for x in range(width_x):
-            line = [wide(row_ref, comp * width_x + x) for row_ref in row_refs]
+            line = [wide(side_ref.at[index], comp * width_x + x) for index in range(row_swaps)]
             ends.append(jnp.where(from_first, line[0], line[1] if row_swaps > 1 else 0.0))
         none = jnp.zeros(shape, jnp.float32)
         ends = [none] + ends + [none]
@@ -251,8 +255,19 @@
                 if x == side * (width_x - 1):
                     edge_ref[side, face, :] = image
 
-    for comp in range(comps):
-        component(comp)
+    steps = sent.shape[0]
+    together = comps // steps
+    copies = []
+    for step in range(steps):
+        for comp in range(step * together, (step + 1) * together):
+            component(comp)
+        here = pl.ds(step * together * lines, together * lines)
+        copies.append(
+            pltpu.make_async_copy(out_ref.at[here, :], out_hbm.at[here, :], sent.at[step])
+        )
+        copies[-1].start()
+    for copy in copies:
+        copy.wait()
 
 
 def last_kernel(
@@ -263,28 +278,21 @@
     image_ref, volume_ref, plane_ref, total_ref, sent = refs[row_swaps + 1 :]
     row_odd = lax.rem(lax.axis_index("row"), 2)
     col_odd = lax.rem(lax.axis_index("col"), 2) == 1
-    total = jnp.sum(part_ref[...].astype(jnp.float32), axis=0)
-    half, lanes = total.shape
-    total_ref[:half] = total[:, : lanes // 2]
-    total_ref[half:] = total[:, lanes // 2 :]
-    copies = [pltpu.make_async_copy(total_ref, image_ref, sent.at[2])]
-    copies[-1].start()
+    copies = []
+    at_row = lax.broadcasted_iota(jnp.int32, (width_y, depth), 0)
     for side in range(2):
         at_x = side * (width_x - 1)
-        plane_ref[side] = edge_ref[side]
+        weight = 1.0 / 12.0 + medium_ref[pl.ds(at_x * width_y, width_y), :] / 27.0
+        plane = edge_ref[side].reshape(comps, width_y, depth)
         for index in range(row_swaps):
             first = corner_refs[index][pl.ds(0, comps), :].astype(jnp.float32)
             second = corner_refs[index][pl.ds(comps, comps), :].astype(jnp.float32)
-            if side:
-                line = jnp.where(col_odd, second, first)
-            else:
-                line = jnp.where(col_odd, first, second)
+            line = jnp.where(col_odd, second, first) if side else jnp.where(col_odd, first, second)
+            line = 2.0 * line + side_z(line)
             at_y = jnp.where(row_odd == index, width_y - 1, 0)
-            weight = 1.0 / 12.0 + medium_ref[pl.ds(at_x * width_y + at_y, 1), :] / 27.0
-            here = pl.ds(at_y, comps, stride=width_y)
-            plane_ref[side, here, :] = plane_ref[side, here, :] - weight * (
-                2.0 * line + side_z(line)
-            )
+            share = jnp.where(at_row == at_y, weight, 0.0)
+            plane = plane - share[None] * line[:, None, :]
+        plane_ref[side] = plane.reshape(comps * width_y, depth)
         copies.append(
             pltpu.make_async_copy(
                 plane_ref.at[side].reshape(comps, width_y, depth),
@@ -293,6 +301,12 @@
             )
         )
         copies[-1].start()
+    total = jnp.sum(part_ref[...].astype(jnp.float32), axis=0)
+    half, lanes = total.shape
+    total_ref[:half] = total[:, : lanes // 2]
+    total_ref[half:] = total[:, lanes // 2 :]
+    copies.append(pltpu.make_async_copy(total_ref, image_ref, sent.at[2]))
+    copies[-1].start()
     for copy in copies:
         copy.wait()
 
@@ -327,7 +341,7 @@
     tiles, *faces = pl.pallas_call(
         functools.partial(trace_kernel, dims, row_swaps),
         out_shape=[jax.ShapeDtypeStruct((rows * cols, TILE_ROWS, 2 * comps), bf16)]
-        + [jax.ShapeDtypeStruct((comps * width_x, depth), f32)] * row_swaps
+        + [jax.ShapeDtypeStruct((comps * width_x, depth), bf16)] * row_swaps
         + [jax.ShapeDtypeStruct((comps, width_y, depth), f32)] * 2,
         in_specs=[hbm()] * 3,
         out_specs=[hbm()] * (3 + row_swaps),
@@ -337,7 +351,7 @@
             pltpu.VMEM((comps, lines, depth), f32),
             pltpu.VMEM((chunks, lines // fold, comps // chunks, fold * depth), bf16),
             pltpu.VMEM((rows * cols, TILE_ROWS, 2 * comps), bf16),
-            pltpu.VMEM((row_swaps, comps * width_x, depth), f32),
+            pltpu.VMEM((row_swaps, comps * width_x, depth), bf16),
             pltpu.SemaphoreType.DMA((chunks + 2,)),
             pltpu.SemaphoreType.DMA((3 + row_swaps,)),
         ],
@@ -388,10 +402,13 @@
             jax.ShapeDtypeStruct((2, comps * width_y, depth), f32),
         ],
         in_specs=[vmem()] * (6 + row_swaps),
-        out_specs=[vmem()] * 2,
+        out_specs=[hbm(), vmem()],
         scratch_shapes=[
             pltpu.VMEM((comps * lines // 2, nodes), bf16),
             pltpu.VMEM((comps * lines // 2, 2 * depth), f32),
+            pltpu.VMEM((comps * lines, depth), f32),
+            pltpu.VMEM((row_swaps, comps * width_x, depth), f32),
+            pltpu.SemaphoreType.DMA((8,)),
         ],
         compiler_params=params,
         name="volume",

time: 30.7 us -> 30.2 us (0.984)
  starting transfers between devices: 15.6 us -> 14.5 us
  waiting for transfers between devices: 4.82 us -> 5.61 us
    ppermute x1, waiting for transfers between devices: 2.99 us -> 1.1 us  [on_device(): lax.ppermute(face, 'row', swap_pairs(rows, swap))]
    all_to_all x1, waiting for transfers between devices: 1.3 us -> 3.19 us  [on_device(): received = lax.all_to_all(tiles, ('row', 'col'), 0, 0, tiled=True)]
    all_to_all x1, starting transfers between devices: 4.83 us -> 3.93 us  [on_device(): lax.all_to_all(shares, 'col', 0, 0, tiled=True, axis_index_groups=[root_f...]
    ppermute x1, waiting for transfers between devices: 0.52 us -> 0.97 us  [on_device(): lax.ppermute(lines_of, 'row', swap_pairs(rows, swap))]
    all_to_all x1, waiting for transfers between devices: 0.01 us -> 0.34 us  [on_device(): lax.all_to_all(shares, 'col', 0, 0, tiled=True, axis_index_groups=[root_f...]
  transfers between devices with their start and end apart: 6 -> 6, of which waited for: 3 -> 4; matrix products, arithmetic and copies ran while one was open for 5% -> 5% of each run, Pallas kernels for 13% -> 12%
where the time goes in v6:
time: 30.2 us; the launch traced here: 29.9 us
  starting transfers between devices  14.5 us (48%)
  Pallas kernels  7.58 us (25%)
  waiting for transfers between devices  5.61 us (19%)
  local copies, waits for them, and re-layouts  1.5 us (5%)
  between operations  0.72 us (2%)
    all_to_all x1, starting transfers between devices, on_device(): received = lax.all_to_all(tiles, ('row', 'col'), 0, 0, tiled=True)  7.3 us
    all_to_all x1, starting transfers between devices, on_device(): lax.all_to_all(shares, 'col', 0, 0, tiled=True, axis_index_groups=[root_f...  3.93 us
    all_to_all x1, waiting for transfers between devices, on_device(): received = lax.all_to_all(tiles, ('row', 'col'), 0, 0, tiled=True)  3.19 us
    pallas_call x1, Pallas kernels, on_device(): pl.pallas_call(functools.partial(trace_kernel, dims, row_swaps), out_shap...  2.97 us
    pallas_call x1, Pallas kernels, on_device(): pl.pallas_call(functools.partial(volume_kernel, dims, row_swaps), out_sha...  2.23 us
    ppermute x1, starting transfers between devices, on_device(): lax.ppermute(face, 'row', swap_pairs(rows, swap))  1.83 us
    squeeze x1, local copies, waits for them, and re-layouts, on_device(): boundary_matrix[1]  1.48 us
    pallas_call x1, Pallas kernels, on_device(): pl.pallas_call(functools.partial(boundary_kernel, slot_len, own_rows), ou...  1.39 us
  transfers between devices with their start and end apart: 6, of which 4 were waited for; matrix products, arithmetic and copies ran while one was open for 5% of the time, Pallas kernels for 12%

profile of v6, /device:TPU:0, one launch (start us, length us, event | category | flops | bytes accessed | tf_op | source)
XLA Modules:
  0.0 29.9 jit_solution(17088053587912710005)
XLA Ops:
  0.6 3.0 %traces.1 = (bf16[32,16,128]{2,1,0:T(8,128)(2,1)}, bf16[256,128]{1,0:T(8,128)(2,1)}, f32[64,8,128]{2,1,0:T(8,128)}, f32[64,8,128]{2,1,0:T(8,128)}) custom-call(s32[1,16]{1,0:T(1,128)} %bitcast.27, s32[1,384]{1,0:T(1,128)} %bitcast.23, f32[64,32,128]{2,1,0:T(8,128)} %bitcast.14), custom_call_target="tpu_custom_call" | custom-call | tf_op jit(solution)/shard_map/traces/pallas_call | solution.py:341
  3.6 7.3 %all-to-all-start = ((bf16[32,16,128]{2,1,0:T(8,128)(2,1)}), bf16[32,16,128]{2,1,0:T(8,128)(2,1)S(1)}, u32[]{:S(2)}, u32[]{:S(2)}) async-start(bf16[32,16,128]{2,1,0:T(8,128)(2,1)} %get-tuple-element.10), calls=%async_computation | async-start | bytes 262144 | tf_op jit(solution)/shard_map/all_to_all | solution.py:369
  10.9 1.8 %collective-permute-start = (bf16[256,128]{1,0:T(8,128)(2,1)}, bf16[256,128]{1,0:T(8,128)(2,1)S(1)}, u32[]{:S(2)}, u32[]{:S(2)}) collective-permute-start(bf16[256,128]{1,0:T(8,128)(2,1)} %get-tuple-element.11), channel_id=1, source_target_pairs={{0,16},{16,0},{1,17},{17,1},{2,18},{18,2},{3,19},{19,3},{4,20},{20... | collective-permute-start | bytes 196616 | tf_op jit(solution)/shard_map/ppermute | solution.py:366
  12.8 0.0 collective-permute-start.1
  12.8 0.7 %collective-permute-start.2 = (f32[64,8,128]{2,1,0:T(8,128)}, f32[64,8,128]{2,1,0:T(8,128)S(1)}, u32[]{:S(2)}, u32[]{:S(2)}) collective-permute-start(f32[64,8,128]{2,1,0:T(8,128)} %get-tuple-element.13), channel_id=1, source_target_pairs={{1,2},{2,1},{3,4},{4,3},{5,6},{6,5},{7,8},{8,7},{9,10},{10,9},{11,... | collective-permute-start | bytes 786440 | tf_op jit(solution)/shard_map/ppermute | solution.py:362
  13.4 1.5 %slice_bitcast_fusion = (bf16[512,768]{1,0:T(8,128)(2,1)S(1)}, bf16[512,768]{1,0:T(8,128)(2,1)S(1)}) fusion(bf16[2,512,768]{2,1,0:T(8,128)(2,1)} %param.11), kind=kLoop, calls=%fused_computation | loop fusion | bytes 3145728 | tf_op jit(solution)/shard_map/squeeze | solution.py:380
  14.9 0.0 copy-start
  14.9 0.0 copy-start.1
  14.9 0.0 copy-start.2
  14.9 0.0 copy-start.3
  15.0 1.1 %collective-permute-done.row_ref.refs_4_ = bf16[256,128]{1,0:T(8,128)(2,1)S(1)} collective-permute-done((bf16[256,128]{1,0:T(8,128)(2,1)}, bf16[256,128]{1,0:T(8,128)(2,1)S(1)}, u32[]{:S(2)}, u32[]{:S(2)}) %collective-permute-start) | collective-permute-done | bytes 65568 | tf_op jit(solution)/shard_map/ppermute | solution.py:366
  16.1 3.2 %all-to-all-done.trace_ref = bf16[32,16,128]{2,1,0:T(8,128)(2,1)S(1)} async-done(((bf16[32,16,128]{2,1,0:T(8,128)(2,1)}), bf16[32,16,128]{2,1,0:T(8,128)(2,1)S(1)}, u32[]{:S(2)}, u32[]{:S(2)}) %all-to-all-start) | async-done | bytes 131104 | tf_op jit(solution)/shard_map/all_to_all | solution.py:369
  19.2 1.4 %boundary.1 = bf16[16,16,128]{2,1,0:T(8,128)(2,1)} custom-call(bf16[32,16,128]{2,1,0:T(8,128)(2,1)S(1)} %all-to-all-done.trace_ref, bf16[512,768]{1,0:T(8,128)(2,1)S(1)} %get-tuple-element.19.real_ref, bf16[512,768]{1,0:T(8,128)(2,1)S(1)} %get-tuple-element.18.imag_ref, bf16[256,128]{1,0:T(8,128)(2,1)S(1)} %collective-permute-done.row_ref.refs_4_), custom_call_target="tpu_custom_call" | custom-call | tf_op jit(solution)/shard_map/boundary/pallas_call | solution.py:373
  20.6 3.9 %all-to-all-start.1 = ((bf16[16,16,128]{2,1,0:T(8,128)(2,1)}), bf16[16,16,128]{2,1,0:T(8,128)(2,1)S(1)}, u32[]{:S(2)}, u32[]{:S(2)}) async-start(bf16[16,16,128]{2,1,0:T(8,128)(2,1)} %boundary.1), calls=%async_computation.1 | async-start | bytes 131072 | tf_op jit(solution)/shard_map/all_to_all | solution.py:381
  24.6 0.0 collective-permute-done.1
  24.6 0.0 collective-permute-done.2
  24.6 0.7 %collective-permute-start.3 = (bf16[128,128]{1,0:T(8,128)(2,1)S(1)}, bf16[128,128]{1,0:T(8,128)(2,1)S(1)}, u32[]{:S(2)}, u32[]{:S(2)}) collective-permute-start(bf16[128,128]{1,0:T(8,128)(2,1)S(1)} %corners.1), channel_id=1, source_target_pairs={{0,16},{16,0},{1,17},{17,1},{2,18},{18,2},{3,19},{19,3},{4,20},{20... | collective-permute-start | bytes 98312 | tf_op jit(solution)/shard_map/ppermute | solution.py:394
  25.4 0.0 copy-done
  25.4 0.0 copy-done.1
  25.4 0.0 copy-done.2
  25.4 0.0 copy-done.3
  25.4 2.2 %volume.1 = (f32[2048,128]{1,0:T(8,128)}, f32[2,512,128]{2,1,0:T(8,128)S(1)}) custom-call(f32[2048,128]{1,0:T(8,128)S(1)} %bitcast.15, f32[32,128]{1,0:T(8,128)S(1)} %bitcast.21, f32[64,1,384]{2,1,0:T(1,128)S(1)} %bitcast.20, s32[1,384]{1,0:T(1,128)S(1)} %bitcast.24, bf16[256,128]{1,0:T(8,128)(2,1)S(1)} %collective-permute-done.row_ref.refs_4_, ...), custom_call_target="tpu_custom_call" | custom-call | tf_op jit(solution)/shard_map/volume/pallas_call | solution.py:398
  27.6 1.0 %collective-permute-done.3.refs_0_ = bf16[128,128]{1,0:T(8,128)(2,1)S(1)} collective-permute-done((bf16[128,128]{1,0:T(8,128)(2,1)S(1)}, bf16[128,128]{1,0:T(8,128)(2,1)S(1)}, u32[]{:S(2)}, u32[]{:S(2)}) %collective-permute-start.3) | collective-permute-done | bytes 32800 | tf_op jit(solution)/shard_map/ppermute | solution.py:394
  28.6 0.3 %all-to-all-done.1.part_ref = bf16[16,16,128]{2,1,0:T(8,128)(2,1)S(1)} async-done(((bf16[16,16,128]{2,1,0:T(8,128)(2,1)}), bf16[16,16,128]{2,1,0:T(8,128)(2,1)S(1)}, u32[]{:S(2)}, u32[]{:S(2)}) %all-to-all-start.1) | async-done | bytes 65568 | tf_op jit(solution)/shard_map/all_to_all | solution.py:381
  28.9 1.0 %last.1 = (f32[32,64]{1,0:T(8,128)}, f32[64,32,128]{2,1,0:T(8,128)}) custom-call(bf16[16,16,128]{2,1,0:T(8,128)(2,1)S(1)} %all-to-all-done.1.part_ref, f32[32,128]{1,0:T(8,128)S(1)} %bitcast.22, f32[2,512,128]{2,1,0:T(8,128)S(1)} %get-tuple-element.14.edge_ref, bf16[128,128]{1,0:T(8,128)(2,1)S(1)} %collective-permute-done.3.refs_0_, ...), custom_call_target="tpu_custom_call", output_to_operand_aliasing={{1}: (4, {})} | custom-call | tf_op jit(solution)/shard_map/last/pallas_call | solution.py:417
  (1 shorter events, 0.0 us)
Async XLA Ops:
  3.6 15.6 %all-to-all-start = ((bf16[32,16,128]{2,1,0:T(8,128)(2,1)}), bf16[32,16,128]{2,1,0:T(8,128)(2,1)S(1)}, u32[]{:S(2)}, u32[]{:S(2)}) async-start(bf16[32,16,128]{2,1,0:T(8,128)(2,1)} %get-tuple-element.10), calls=%async_computation | async-start | bytes 262144 | tf_op jit(solution)/shard_map/all_to_all | solution.py:369
  10.9 5.1 %collective-permute-start = (bf16[256,128]{1,0:T(8,128)(2,1)}, bf16[256,128]{1,0:T(8,128)(2,1)S(1)}, u32[]{:S(2)}, u32[]{:S(2)}) collective-permute-start(bf16[256,128]{1,0:T(8,128)(2,1)} %get-tuple-element.11), channel_id=1, source_target_pairs={{0,16},{16,0},{1,17},{17,1},{2,18},{18,2},{3,19},{19,3},{4,20},{20... | collective-permute-start | bytes 196616 | tf_op jit(solution)/shard_map/ppermute | solution.py:366
  12.8 11.8 %collective-permute-start.1 = (f32[64,8,128]{2,1,0:T(8,128)}, f32[64,8,128]{2,1,0:T(8,128)S(1)}, u32[]{:S(2)}, u32[]{:S(2)}) collective-permute-start(f32[64,8,128]{2,1,0:T(8,128)} %get-tuple-element.12), channel_id=1, source_target_pairs={{0,1},{1,0},{2,3},{3,2},{4,5},{5,4},{6,7},{7,6},{8,9},{9,8},{10,11... | collective-permute-start | bytes 786440 | tf_op jit(solution)/shard_map/ppermute | solution.py:362
  12.8 11.8 %collective-permute-start.2 = (f32[64,8,128]{2,1,0:T(8,128)}, f32[64,8,128]{2,1,0:T(8,128)S(1)}, u32[]{:S(2)}, u32[]{:S(2)}) collective-permute-start(f32[64,8,128]{2,1,0:T(8,128)} %get-tuple-element.13), channel_id=1, source_target_pairs={{1,2},{2,1},{3,4},{4,3},{5,6},{6,5},{7,8},{8,7},{9,10},{10,9},{11,... | collective-permute-start | bytes 786440 | tf_op jit(solution)/shard_map/ppermute | solution.py:362
  14.9 10.5 %copy-start = (f32[64,4,8,128]{3,2,1,0:T(8,128)S(1)}, f32[64,4,8,128]{3,2,1,0:T(8,128)}, u32[]{:S(2)}) copy-start(f32[64,4,8,128]{3,2,1,0:T(8,128)} %param.6) | copy-start | bytes 3145732
  14.9 10.5 %copy-start.1 = (f32[64,1,1,384]{3,2,1,0:T(1,128)S(1)}, f32[64,1,1,384]{3,2,1,0:T(1,128)}, u32[]{:S(2)}) copy-start(f32[64,1,1,384]{3,2,1,0:T(1,128)} %param.8) | copy-start | bytes 294916
  14.9 10.4 %copy-start.2 = (f32[4,8,128]{2,1,0:T(8,128)S(1)}, f32[4,8,128]{2,1,0:T(8,128)}, u32[]{:S(2)}) copy-start(f32[4,8,128]{2,1,0:T(8,128)} %param.7) | copy-start | bytes 49156
  14.9 10.4 %copy-start.3 = (s32[1,1,384]{2,1,0:T(1,128)S(1)}, s32[1,1,384]{2,1,0:T(1,128)}, u32[]{:S(2)}) copy-start(s32[1,1,384]{2,1,0:T(1,128)} %param.9) | copy-start | bytes 4612
  20.6 8.3 %all-to-all-start.1 = ((bf16[16,16,128]{2,1,0:T(8,128)(2,1)}), bf16[16,16,128]{2,1,0:T(8,128)(2,1)S(1)}, u32[]{:S(2)}, u32[]{:S(2)}) async-start(bf16[16,16,128]{2,1,0:T(8,128)(2,1)} %boundary.1), calls=%async_computation.1 | async-start | bytes 131072 | tf_op jit(solution)/shard_map/all_to_all | solution.py:381
  24.6 4.0 %collective-permute-start.3 = (bf16[128,128]{1,0:T(8,128)(2,1)S(1)}, bf16[128,128]{1,0:T(8,128)(2,1)S(1)}, u32[]{:S(2)}, u32[]{:S(2)}) collective-permute-start(bf16[128,128]{1,0:T(8,128)(2,1)S(1)} %corners.1), channel_id=1, source_target_pairs={{0,16},{16,0},{1,17},{17,1},{2,18},{18,2},{3,19},{19,3},{4,20},{20... | collective-permute-start | bytes 98312 | tf_op jit(solution)/shard_map/ppermute | solution.py:394

commit v7 on v6

--- a/solution.py
+++ b/solution.py
@@ -88,14 +88,6 @@
             )
         )
         sent[-1].start()
-    row_odd = lax.rem(lax.axis_index("row"), 2)
-    for swap, face_ref in enumerate(row_faces):
-        low, high = (
-            flat[pl.ds(layer, comps * width_x, stride=width_y), :] for layer in (0, width_y - 1)
-        )
-        side_ref[swap] = jnp.where(row_odd == swap, high, low).astype(jnp.bfloat16)
-        sent.append(pltpu.make_async_copy(side_ref.at[swap], face_ref, left_sem.at[2 + swap]))
-        sent[-1].start()
     by_node = jnp.concatenate(found, axis=0).T
     copies[-1].wait()
     left_len = min(slot_len, TILE_ROWS)
@@ -117,6 +109,14 @@
             tile_ref[row * cols + target_ref[0, slot]] = tile
     sent.append(pltpu.make_async_copy(tile_ref, tile_hbm, left_sem.at[2 + row_swaps]))
     sent[-1].start()
+    row_odd = lax.rem(lax.axis_index("row"), 2)
+    for swap, face_ref in enumerate(row_faces):
+        low, high = (
+            flat[pl.ds(layer, comps * width_x, stride=width_y), :] for layer in (0, width_y - 1)
+        )
+        side_ref[swap] = jnp.where(row_odd == swap, high, low).astype(jnp.bfloat16)
+        sent.append(pltpu.make_async_copy(side_ref.at[swap], face_ref, left_sem.at[2 + swap]))
+        sent[-1].start()
     for copy in sent:
         copy.wait()
 
@@ -127,7 +127,8 @@
     for swap, out_ref in enumerate(out_refs):
         for index, ref in enumerate((first_ref, second_ref)):
             low, high = (ref[pl.ds(layer, comps, stride=width_y), :] for layer in (0, width_y - 1))
-            out_ref[pl.ds(index * comps, comps), :] = jnp.where(odd == swap, high, low).astype(
+            line = jnp.where(odd == swap, high, low)
+            out_ref[pl.ds(index * comps, comps), :] = (2.0 * line + side_z(line)).astype(
                 out_ref.dtype
             )
 
@@ -150,10 +151,10 @@
         traces = trace_ref[...].astype(jnp.float32)
     comps = traces.shape[1]
     angles = comps // 2
-    turned = jnp.concatenate([-traces[:, angles:], traces[:, :angles]], axis=1)
-    image = jnp.dot(
-        real_ref[...], traces.astype(jnp.bfloat16), preferred_element_type=jnp.float32
-    ) + jnp.dot(imag_ref[...], turned.astype(jnp.bfloat16), preferred_element_type=jnp.float32)
+    traces = traces.astype(jnp.bfloat16)
+    image = jnp.dot(real_ref[...], traces, preferred_element_type=jnp.float32)
+    other = jnp.dot(imag_ref[...], traces, preferred_element_type=jnp.float32)
+    image = image + jnp.concatenate([-other[:, angles:], other[:, :angles]], axis=1)
     image = image.reshape(image.shape[0] // own_rows, own_rows, comps)
     half = own_rows // 2
     packed = jnp.concatenate([image[:, :half], image[:, half:]], axis=2).astype(out_ref.dtype)
@@ -288,7 +289,6 @@
             first = corner_refs[index][pl.ds(0, comps), :].astype(jnp.float32)
             second = corner_refs[index][pl.ds(comps, comps), :].astype(jnp.float32)
             line = jnp.where(col_odd, second, first) if side else jnp.where(col_odd, first, second)
-            line = 2.0 * line + side_z(line)
             at_y = jnp.where(row_odd == index, width_y - 1, 0)
             share = jnp.where(at_row == at_y, weight, 0.0)
             plane = plane - share[None] * line[:, None, :]

time: 30.2 us -> 30.2 us (level)
  transfers between devices with their start and end apart: 6 -> 6, of which waited for: 4 -> 4; matrix products, arithmetic and copies ran while one was open for 5% -> 5% of each run, Pallas kernels for 12% -> 13%
where the time goes in v7:
time: 30.2 us; the launch traced here: 29.9 us
  starting transfers between devices  14.5 us (48%)
  Pallas kernels  7.62 us (25%)
  waiting for transfers between devices  5.53 us (18%)
  local copies, waits for them, and re-layouts  1.5 us (5%)
  between operations  0.72 us (2%)
    all_to_all x1, starting transfers between devices, on_device(): received = lax.all_to_all(tiles, ('row', 'col'), 0, 0, tiled=True)  7.3 us
    all_to_all x1, starting transfers between devices, on_device(): lax.all_to_all(shares, 'col', 0, 0, tiled=True, axis_index_groups=[root_f...  3.93 us
    all_to_all x1, waiting for transfers between devices, on_device(): received = lax.all_to_all(tiles, ('row', 'col'), 0, 0, tiled=True)  3.19 us
    pallas_call x1, Pallas kernels, on_device(): pl.pallas_call(functools.partial(trace_kernel, dims, row_swaps), out_shap...  2.98 us
    pallas_call x1, Pallas kernels, on_device(): pl.pallas_call(functools.partial(volume_kernel, dims, row_swaps), out_sha...  2.23 us
    ppermute x1, starting transfers between devices, on_device(): lax.ppermute(face, 'row', swap_pairs(rows, swap))  1.83 us
    squeeze x1, local copies, waits for them, and re-layouts, on_device(): boundary_matrix[1]  1.48 us
    pallas_call x1, Pallas kernels, on_device(): pl.pallas_call(functools.partial(boundary_kernel, slot_len, own_rows), ou...  1.4 us
  transfers between devices with their start and end apart: 6, of which 4 were waited for; matrix products, arithmetic and copies ran while one was open for 5% of the time, Pallas kernels for 13%

profile of v7, /device:TPU:0, one launch (start us, length us, event | category | flops | bytes accessed | tf_op | source)
XLA Modules:
  0.0 29.9 jit_solution(9665503117653847723)
XLA Ops:
  0.6 3.0 %traces.1 = (bf16[32,16,128]{2,1,0:T(8,128)(2,1)}, bf16[256,128]{1,0:T(8,128)(2,1)}, f32[64,8,128]{2,1,0:T(8,128)}, f32[64,8,128]{2,1,0:T(8,128)}) custom-call(s32[1,16]{1,0:T(1,128)} %bitcast.27, s32[1,384]{1,0:T(1,128)} %bitcast.23, f32[64,32,128]{2,1,0:T(8,128)} %bitcast.14), custom_call_target="tpu_custom_call" | custom-call | tf_op jit(solution)/shard_map/traces/pallas_call | solution.py:341
  3.6 7.3 %all-to-all-start = ((bf16[32,16,128]{2,1,0:T(8,128)(2,1)}), bf16[32,16,128]{2,1,0:T(8,128)(2,1)S(1)}, u32[]{:S(2)}, u32[]{:S(2)}) async-start(bf16[32,16,128]{2,1,0:T(8,128)(2,1)} %get-tuple-element.10), calls=%async_computation | async-start | bytes 262144 | tf_op jit(solution)/shard_map/all_to_all | solution.py:369
  10.9 1.8 %collective-permute-start = (bf16[256,128]{1,0:T(8,128)(2,1)}, bf16[256,128]{1,0:T(8,128)(2,1)S(1)}, u32[]{:S(2)}, u32[]{:S(2)}) collective-permute-start(bf16[256,128]{1,0:T(8,128)(2,1)} %get-tuple-element.11), channel_id=1, source_target_pairs={{0,16},{16,0},{1,17},{17,1},{2,18},{18,2},{3,19},{19,3},{4,20},{20... | collective-permute-start | bytes 196616 | tf_op jit(solution)/shard_map/ppermute | solution.py:366
  12.8 0.0 collective-permute-start.1
  12.8 0.7 %collective-permute-start.2 = (f32[64,8,128]{2,1,0:T(8,128)}, f32[64,8,128]{2,1,0:T(8,128)S(1)}, u32[]{:S(2)}, u32[]{:S(2)}) collective-permute-start(f32[64,8,128]{2,1,0:T(8,128)} %get-tuple-element.13), channel_id=1, source_target_pairs={{1,2},{2,1},{3,4},{4,3},{5,6},{6,5},{7,8},{8,7},{9,10},{10,9},{11,... | collective-permute-start | bytes 786440 | tf_op jit(solution)/shard_map/ppermute | solution.py:362
  13.4 1.5 %slice_bitcast_fusion = (bf16[512,768]{1,0:T(8,128)(2,1)S(1)}, bf16[512,768]{1,0:T(8,128)(2,1)S(1)}) fusion(bf16[2,512,768]{2,1,0:T(8,128)(2,1)} %param.11), kind=kLoop, calls=%fused_computation | loop fusion | bytes 3145728 | tf_op jit(solution)/shard_map/squeeze | solution.py:380
  14.9 0.0 copy-start
  14.9 0.0 copy-start.1
  14.9 0.0 copy-start.2
  15.0 0.0 copy-start.3
  15.0 1.1 %collective-permute-done.row_ref.refs_4_ = bf16[256,128]{1,0:T(8,128)(2,1)S(1)} collective-permute-done((bf16[256,128]{1,0:T(8,128)(2,1)}, bf16[256,128]{1,0:T(8,128)(2,1)S(1)}, u32[]{:S(2)}, u32[]{:S(2)}) %collective-permute-start) | collective-permute-done | bytes 65568 | tf_op jit(solution)/shard_map/ppermute | solution.py:366
  16.1 3.2 %all-to-all-done.trace_ref = bf16[32,16,128]{2,1,0:T(8,128)(2,1)S(1)} async-done(((bf16[32,16,128]{2,1,0:T(8,128)(2,1)}), bf16[32,16,128]{2,1,0:T(8,128)(2,1)S(1)}, u32[]{:S(2)}, u32[]{:S(2)}) %all-to-all-start) | async-done | bytes 131104 | tf_op jit(solution)/shard_map/all_to_all | solution.py:369
  19.3 1.4 %boundary.1 = bf16[16,16,128]{2,1,0:T(8,128)(2,1)} custom-call(bf16[32,16,128]{2,1,0:T(8,128)(2,1)S(1)} %all-to-all-done.trace_ref, bf16[512,768]{1,0:T(8,128)(2,1)S(1)} %get-tuple-element.19.real_ref, bf16[512,768]{1,0:T(8,128)(2,1)S(1)} %get-tuple-element.18.imag_ref, bf16[256,128]{1,0:T(8,128)(2,1)S(1)} %collective-permute-done.row_ref.refs_4_), custom_call_target="tpu_custom_call" | custom-call | tf_op jit(solution)/shard_map/boundary/pallas_call | solution.py:373
  20.7 3.9 %all-to-all-start.1 = ((bf16[16,16,128]{2,1,0:T(8,128)(2,1)}), bf16[16,16,128]{2,1,0:T(8,128)(2,1)S(1)}, u32[]{:S(2)}, u32[]{:S(2)}) async-start(bf16[16,16,128]{2,1,0:T(8,128)(2,1)} %boundary.1), calls=%async_computation.1 | async-start | bytes 131072 | tf_op jit(solution)/shard_map/all_to_all | solution.py:381
  24.6 0.0 collective-permute-done.1
  24.6 0.0 collective-permute-done.2
  24.6 0.1 corners.1
  24.7 0.7 %collective-permute-start.3 = (bf16[128,128]{1,0:T(8,128)(2,1)S(1)}, bf16[128,128]{1,0:T(8,128)(2,1)S(1)}, u32[]{:S(2)}, u32[]{:S(2)}) collective-permute-start(bf16[128,128]{1,0:T(8,128)(2,1)S(1)} %corners.1), channel_id=1, source_target_pairs={{0,16},{16,0},{1,17},{17,1},{2,18},{18,2},{3,19},{19,3},{4,20},{20... | collective-permute-start | bytes 98312 | tf_op jit(solution)/shard_map/ppermute | solution.py:394
  25.5 0.0 copy-done
  25.5 0.0 copy-done.1
  25.5 0.0 copy-done.2
  25.5 0.0 copy-done.3
  25.5 2.2 %volume.1 = (f32[2048,128]{1,0:T(8,128)}, f32[2,512,128]{2,1,0:T(8,128)S(1)}) custom-call(f32[2048,128]{1,0:T(8,128)S(1)} %bitcast.15, f32[32,128]{1,0:T(8,128)S(1)} %bitcast.21, f32[64,1,384]{2,1,0:T(1,128)S(1)} %bitcast.20, s32[1,384]{1,0:T(1,128)S(1)} %bitcast.24, bf16[256,128]{1,0:T(8,128)(2,1)S(1)} %collective-permute-done.row_ref.refs_4_, ...), custom_call_target="tpu_custom_call" | custom-call | tf_op jit(solution)/shard_map/volume/pallas_call | solution.py:398
  27.7 1.0 %collective-permute-done.3.refs_0_ = bf16[128,128]{1,0:T(8,128)(2,1)S(1)} collective-permute-done((bf16[128,128]{1,0:T(8,128)(2,1)S(1)}, bf16[128,128]{1,0:T(8,128)(2,1)S(1)}, u32[]{:S(2)}, u32[]{:S(2)}) %collective-permute-start.3) | collective-permute-done | bytes 32800 | tf_op jit(solution)/shard_map/ppermute | solution.py:394
  28.7 0.3 all-to-all-done.1.part_ref
  29.0 0.9 %last.1 = (f32[32,64]{1,0:T(8,128)}, f32[64,32,128]{2,1,0:T(8,128)}) custom-call(bf16[16,16,128]{2,1,0:T(8,128)(2,1)S(1)} %all-to-all-done.1.part_ref, f32[32,128]{1,0:T(8,128)S(1)} %bitcast.22, f32[2,512,128]{2,1,0:T(8,128)S(1)} %get-tuple-element.14.edge_ref, bf16[128,128]{1,0:T(8,128)(2,1)S(1)} %collective-permute-done.3.refs_0_, ...), custom_call_target="tpu_custom_call", output_to_operand_aliasing={{1}: (4, {})} | custom-call | tf_op jit(solution)/shard_map/last/pallas_call | solution.py:417
Async XLA Ops:
  3.6 15.6 %all-to-all-start = ((bf16[32,16,128]{2,1,0:T(8,128)(2,1)}), bf16[32,16,128]{2,1,0:T(8,128)(2,1)S(1)}, u32[]{:S(2)}, u32[]{:S(2)}) async-start(bf16[32,16,128]{2,1,0:T(8,128)(2,1)} %get-tuple-element.10), calls=%async_computation | async-start | bytes 262144 | tf_op jit(solution)/shard_map/all_to_all | solution.py:369
  10.9 5.1 %collective-permute-start = (bf16[256,128]{1,0:T(8,128)(2,1)}, bf16[256,128]{1,0:T(8,128)(2,1)S(1)}, u32[]{:S(2)}, u32[]{:S(2)}) collective-permute-start(bf16[256,128]{1,0:T(8,128)(2,1)} %get-tuple-element.11), channel_id=1, source_target_pairs={{0,16},{16,0},{1,17},{17,1},{2,18},{18,2},{3,19},{19,3},{4,20},{20... | collective-permute-start | bytes 196616 | tf_op jit(solution)/shard_map/ppermute | solution.py:366
  12.8 11.8 %collective-permute-start.1 = (f32[64,8,128]{2,1,0:T(8,128)}, f32[64,8,128]{2,1,0:T(8,128)S(1)}, u32[]{:S(2)}, u32[]{:S(2)}) collective-permute-start(f32[64,8,128]{2,1,0:T(8,128)} %get-tuple-element.12), channel_id=1, source_target_pairs={{0,1},{1,0},{2,3},{3,2},{4,5},{5,4},{6,7},{7,6},{8,9},{9,8},{10,11... | collective-permute-start | bytes 786440 | tf_op jit(solution)/shard_map/ppermute | solution.py:362
  12.8 11.8 %collective-permute-start.2 = (f32[64,8,128]{2,1,0:T(8,128)}, f32[64,8,128]{2,1,0:T(8,128)S(1)}, u32[]{:S(2)}, u32[]{:S(2)}) collective-permute-start(f32[64,8,128]{2,1,0:T(8,128)} %get-tuple-element.13), channel_id=1, source_target_pairs={{1,2},{2,1},{3,4},{4,3},{5,6},{6,5},{7,8},{8,7},{9,10},{10,9},{11,... | collective-permute-start | bytes 786440 | tf_op jit(solution)/shard_map/ppermute | solution.py:362
  14.9 10.6 %copy-start = (f32[64,4,8,128]{3,2,1,0:T(8,128)S(1)}, f32[64,4,8,128]{3,2,1,0:T(8,128)}, u32[]{:S(2)}) copy-start(f32[64,4,8,128]{3,2,1,0:T(8,128)} %param.6) | copy-start | bytes 3145732
  14.9 10.5 %copy-start.1 = (f32[64,1,1,384]{3,2,1,0:T(1,128)S(1)}, f32[64,1,1,384]{3,2,1,0:T(1,128)}, u32[]{:S(2)}) copy-start(f32[64,1,1,384]{3,2,1,0:T(1,128)} %param.8) | copy-start | bytes 294916
  14.9 10.5 %copy-start.2 = (f32[4,8,128]{2,1,0:T(8,128)S(1)}, f32[4,8,128]{2,1,0:T(8,128)}, u32[]{:S(2)}) copy-start(f32[4,8,128]{2,1,0:T(8,128)} %param.7) | copy-start | bytes 49156
  15.0 10.5 %copy-start.3 = (s32[1,1,384]{2,1,0:T(1,128)S(1)}, s32[1,1,384]{2,1,0:T(1,128)}, u32[]{:S(2)}) copy-start(s32[1,1,384]{2,1,0:T(1,128)} %param.9) | copy-start | bytes 4612
  20.7 8.3 %all-to-all-start.1 = ((bf16[16,16,128]{2,1,0:T(8,128)(2,1)}), bf16[16,16,128]{2,1,0:T(8,128)(2,1)S(1)}, u32[]{:S(2)}, u32[]{:S(2)}) async-start(bf16[16,16,128]{2,1,0:T(8,128)(2,1)} %boundary.1), calls=%async_computation.1 | async-start | bytes 131072 | tf_op jit(solution)/shard_map/all_to_all | solution.py:381
  24.7 4.0 %collective-permute-start.3 = (bf16[128,128]{1,0:T(8,128)(2,1)S(1)}, bf16[128,128]{1,0:T(8,128)(2,1)S(1)}, u32[]{:S(2)}, u32[]{:S(2)}) collective-permute-start(bf16[128,128]{1,0:T(8,128)(2,1)S(1)} %corners.1), channel_id=1, source_target_pairs={{0,16},{16,0},{1,17},{17,1},{2,18},{18,2},{3,19},{19,3},{4,20},{20... | collective-permute-start | bytes 98312 | tf_op jit(solution)/shard_map/ppermute | solution.py:394

commit v8 on v7

--- a/solution.py
+++ b/solution.py
@@ -7,7 +7,6 @@
 from jax.experimental.pallas import tpu as pltpu
 from jax.sharding import PartitionSpec as P
 
-TILE_ROWS = 16
 SMALL = 8 * 2**20
 WHOLE = 64560 * 2**10
 
@@ -32,6 +31,28 @@
 def root_first(count):
     root = count * 9 // 16
     return [root] + [index for index in range(count) if index != root]
+
+
+def far_first(rows, cols):
+    share = cols // 4
+    return [
+        row * cols + quarter * share + col
+        for quarter in range(4)[::-1]
+        for col in range(share)
+        for row in range(rows)
+    ]
+
+
+def by_sender(tiles, rows, cols):
+    share = cols // 4
+    parts = tiles.reshape((4, share, rows) + tiles.shape[1:])
+    blocks = [parts[3 - quarter, :, row] for row in range(rows) for quarter in range(4)]
+    return jnp.concatenate(blocks, axis=0)
+
+
+def tile_shape(slot_len, comps):
+    groups = 3 if slot_len % 6 == 0 else 1
+    return slot_len // (2 * groups), groups
 
 
 def trace_kernel(dims, row_swaps, target_hbm, cell_hbm, field_hbm, tile_hbm, *rest):
@@ -90,23 +111,19 @@
         sent[-1].start()
     by_node = jnp.concatenate(found, axis=0).T
     copies[-1].wait()
-    left_len = min(slot_len, TILE_ROWS)
+    tile_rows, groups = tile_shape(slot_len, comps)
     for slot in range(cols):
-        piece = by_node[slot * slot_len : (slot + 1) * slot_len]
-        left = piece[:left_len]
-        right = piece[left_len:]
-        if left_len < TILE_ROWS:
-            left = jnp.concatenate(
-                [left, jnp.zeros((TILE_ROWS - left_len, comps), jnp.float32)], axis=0
-            )
-        gap = TILE_ROWS - (slot_len - left_len)
-        if slot_len == left_len:
-            right = jnp.zeros((TILE_ROWS, comps), jnp.float32)
-        elif gap:
-            right = jnp.concatenate([right, jnp.zeros((gap, comps), jnp.float32)], axis=0)
-        tile = jnp.concatenate([left, right], axis=1).astype(jnp.bfloat16)
+        pieces = []
+        for group in range(2 * groups):
+            node = slot * slot_len + group * tile_rows
+            pieces.append(by_node[node : node + tile_rows])
+        tile = jnp.concatenate(pieces, axis=1).astype(jnp.bfloat16)
+        target = target_ref[0, slot]
+        share = cols // 4
+        quarter = jnp.right_shift(target, share.bit_length() - 1)
+        place = ((3 - quarter) * share + jnp.bitwise_and(target, share - 1)) * rows
         for row in range(rows):
-            tile_ref[row * cols + target_ref[0, slot]] = tile
+            tile_ref[place + row] = tile
     sent.append(pltpu.make_async_copy(tile_ref, tile_hbm, left_sem.at[2 + row_swaps]))
     sent[-1].start()
     row_odd = lax.rem(lax.axis_index("row"), 2)
@@ -133,20 +150,16 @@
             )
 
 
-def unpack_tiles(tiles, slot_len, comps):
-    left_len = min(slot_len, TILE_ROWS)
-    parts = [tiles[:, :left_len, :comps]]
-    if slot_len > left_len:
-        parts.append(tiles[:, : slot_len - left_len, comps:])
-    both = jnp.concatenate(parts, axis=1) if len(parts) > 1 else parts[0]
-    return both.reshape(tiles.shape[0] * slot_len, comps)
-
-
-def boundary_kernel(slot_len, own_rows, trace_ref, real_ref, imag_ref, row_ref, out_ref):
+def unpack_tiles(tiles, comps):
+    groups = tiles.shape[2] // comps
+    parts = [tiles[:, :, group * comps : (group + 1) * comps] for group in range(groups)]
+    return jnp.concatenate(parts, axis=1).reshape(-1, comps)
+
+
+def boundary_kernel(dims, own_rows, trace_ref, real_ref, imag_ref, row_ref, out_ref):
     if len(trace_ref.shape) == 3:
-        traces = unpack_tiles(
-            trace_ref[...].astype(jnp.float32), slot_len, trace_ref.shape[2] // 2
-        )
+        tiles = by_sender(trace_ref[...].astype(jnp.float32), *dims[-2:])
+        traces = unpack_tiles(tiles, out_ref.shape[2] // 2)
     else:
         traces = trace_ref[...].astype(jnp.float32)
     comps = traces.shape[1]
@@ -332,6 +345,8 @@
     params = pltpu.CompilerParams(vmem_limit_bytes=SMALL)
 
     chunks, fold = 2, 4
+    tile_rows, groups = tile_shape(slot_len, comps)
+    tile_dims = (tile_rows, 2 * groups * comps)
     field = wave_field.reshape(comps * lines, depth)
     cells = node_cell.reshape(1, nodes)
     targets = block_target.reshape(1, cols)
@@ -340,7 +355,7 @@
 
     tiles, *faces = pl.pallas_call(
         functools.partial(trace_kernel, dims, row_swaps),
-        out_shape=[jax.ShapeDtypeStruct((rows * cols, TILE_ROWS, 2 * comps), bf16)]
+        out_shape=[jax.ShapeDtypeStruct((rows * cols,) + tile_dims, bf16)]
         + [jax.ShapeDtypeStruct((comps * width_x, depth), bf16)] * row_swaps
         + [jax.ShapeDtypeStruct((comps, width_y, depth), f32)] * 2,
         in_specs=[hbm()] * 3,
@@ -350,7 +365,7 @@
             pltpu.VMEM((1, nodes), jnp.int32),
             pltpu.VMEM((comps, lines, depth), f32),
             pltpu.VMEM((chunks, lines // fold, comps // chunks, fold * depth), bf16),
-            pltpu.VMEM((rows * cols, TILE_ROWS, 2 * comps), bf16),
+            pltpu.VMEM((rows * cols,) + tile_dims, bf16),
             pltpu.VMEM((row_swaps, comps * width_x, depth), bf16),
             pltpu.SemaphoreType.DMA((chunks + 2,)),
             pltpu.SemaphoreType.DMA((3 + row_swaps,)),
@@ -366,12 +381,14 @@
         lax.ppermute(face, "row", swap_pairs(rows, swap))
         for swap, face in enumerate(faces[:row_swaps])
     ]
-    received = lax.all_to_all(tiles, ("row", "col"), 0, 0, tiled=True)
+    received = lax.all_to_all(
+        tiles, ("row", "col"), 0, 0, tiled=True, axis_index_groups=[far_first(rows, cols)]
+    )
 
     if slot_len % 8:
-        received = unpack_tiles(received, slot_len, comps)
+        received = unpack_tiles(by_sender(received, rows, cols), comps)
     shares = pl.pallas_call(
-        functools.partial(boundary_kernel, slot_len, own_rows),
+        functools.partial(boundary_kernel, dims, own_rows),
         out_shape=jax.ShapeDtypeStruct((cols, own_rows // 2, 2 * comps), bf16),
         in_specs=[vmem()] * 4,
         out_specs=vmem(),

time: 30.2 us -> 30.1 us (level)
  waiting for transfers between devices: 5.53 us -> 4.71 us
  starting transfers between devices: 14.5 us -> 15.3 us
    all_to_all x1, starting transfers between devices: 3.93 us -> 4.86 us  [on_device(): lax.all_to_all(shares, 'col', 0, 0, tiled=True, axis_index_groups=[root_f...]
    all_to_all x1, waiting for transfers between devices: 3.19 us -> 2.28 us  [on_device(): lax.all_to_all(tiles, ('row', 'col'), 0, 0, tiled=True, axis_index_groups...]
where the time goes in v8:
time: 30.1 us; the launch traced here: 29.8 us
  starting transfers between devices  15.3 us (51%)
  Pallas kernels  7.63 us (25%)
  waiting for transfers between devices  4.71 us (16%)
  local copies, waits for them, and re-layouts  1.5 us (5%)
  between operations  0.72 us (2%)
    all_to_all x1, starting transfers between devices, on_device(): lax.all_to_all(tiles, ('row', 'col'), 0, 0, tiled=True, axis_index_groups...  7.3 us
    all_to_all x1, starting transfers between devices, on_device(): lax.all_to_all(shares, 'col', 0, 0, tiled=True, axis_index_groups=[root_f...  4.86 us
    pallas_call x1, Pallas kernels, on_device(): pl.pallas_call(functools.partial(trace_kernel, dims, row_swaps), out_shap...  2.98 us
    all_to_all x1, waiting for transfers between devices, on_device(): lax.all_to_all(tiles, ('row', 'col'), 0, 0, tiled=True, axis_index_groups...  2.28 us
    pallas_call x1, Pallas kernels, on_device(): pl.pallas_call(functools.partial(volume_kernel, dims, row_swaps), out_sha...  2.23 us
    ppermute x1, starting transfers between devices, on_device(): lax.ppermute(face, 'row', swap_pairs(rows, swap))  1.83 us
    squeeze x1, local copies, waits for them, and re-layouts, on_device(): boundary_matrix[1]  1.48 us
    pallas_call x1, Pallas kernels, on_device(): pl.pallas_call(functools.partial(boundary_kernel, dims, own_rows), out_sh...  1.41 us
  transfers between devices with their start and end apart: 6, of which 4 were waited for; matrix products, arithmetic and copies ran while one was open for 5% of the time, Pallas kernels for 13%

profile of v8, /device:TPU:0, one launch (start us, length us, event | category | flops | bytes accessed | tf_op | source)
XLA Modules:
  0.0 29.8 jit_solution(3133597979402933171)
XLA Ops:
  0.6 3.0 %traces.1 = (bf16[32,4,384]{2,1,0:T(4,128)(2,1)}, bf16[256,128]{1,0:T(8,128)(2,1)}, f32[64,8,128]{2,1,0:T(8,128)}, f32[64,8,128]{2,1,0:T(8,128)}) custom-call(s32[1,16]{1,0:T(1,128)} %bitcast.27, s32[1,384]{1,0:T(1,128)} %bitcast.23, f32[64,32,128]{2,1,0:T(8,128)} %bitcast.14), custom_call_target="tpu_custom_call" | custom-call | tf_op jit(solution)/shard_map/traces/pallas_call | solution.py:356
  3.6 7.3 %all-to-all-start = ((bf16[32,4,384]{2,1,0:T(4,128)(2,1)}), bf16[32,4,384]{2,1,0:T(4,128)(2,1)S(1)}, u32[]{:S(2)}, u32[]{:S(2)}) async-start(bf16[32,4,384]{2,1,0:T(4,128)(2,1)} %get-tuple-element.10), calls=%async_computation | async-start | bytes 196608 | tf_op jit(solution)/shard_map/all_to_all | solution.py:384
  10.9 1.8 %collective-permute-start = (bf16[256,128]{1,0:T(8,128)(2,1)}, bf16[256,128]{1,0:T(8,128)(2,1)S(1)}, u32[]{:S(2)}, u32[]{:S(2)}) collective-permute-start(bf16[256,128]{1,0:T(8,128)(2,1)} %get-tuple-element.11), channel_id=1, source_target_pairs={{0,16},{16,0},{1,17},{17,1},{2,18},{18,2},{3,19},{19,3},{4,20},{20... | collective-permute-start | bytes 196616 | tf_op jit(solution)/shard_map/ppermute | solution.py:381
  12.8 0.0 collective-permute-start.1
  12.8 0.7 %collective-permute-start.2 = (f32[64,8,128]{2,1,0:T(8,128)}, f32[64,8,128]{2,1,0:T(8,128)S(1)}, u32[]{:S(2)}, u32[]{:S(2)}) collective-permute-start(f32[64,8,128]{2,1,0:T(8,128)} %get-tuple-element.13), channel_id=1, source_target_pairs={{1,2},{2,1},{3,4},{4,3},{5,6},{6,5},{7,8},{8,7},{9,10},{10,9},{11,... | collective-permute-start | bytes 786440 | tf_op jit(solution)/shard_map/ppermute | solution.py:377
  13.4 1.5 %slice_bitcast_fusion = (bf16[512,768]{1,0:T(8,128)(2,1)S(1)}, bf16[512,768]{1,0:T(8,128)(2,1)S(1)}) fusion(bf16[2,512,768]{2,1,0:T(8,128)(2,1)} %param.11), kind=kLoop, calls=%fused_computation | loop fusion | bytes 3145728 | tf_op jit(solution)/shard_map/squeeze | solution.py:397
  14.9 0.0 copy-start
  14.9 0.0 copy-start.1
  14.9 0.0 copy-start.2
  15.0 0.0 copy-start.3
  15.0 1.0 %collective-permute-done.row_ref.refs_4_ = bf16[256,128]{1,0:T(8,128)(2,1)S(1)} collective-permute-done((bf16[256,128]{1,0:T(8,128)(2,1)}, bf16[256,128]{1,0:T(8,128)(2,1)S(1)}, u32[]{:S(2)}, u32[]{:S(2)}) %collective-permute-start) | collective-permute-done | bytes 65568 | tf_op jit(solution)/shard_map/ppermute | solution.py:381
  16.0 2.3 %all-to-all-done.trace_ref = bf16[32,4,384]{2,1,0:T(4,128)(2,1)S(1)} async-done(((bf16[32,4,384]{2,1,0:T(4,128)(2,1)}), bf16[32,4,384]{2,1,0:T(4,128)(2,1)S(1)}, u32[]{:S(2)}, u32[]{:S(2)}) %all-to-all-start) | async-done | bytes 98336 | tf_op jit(solution)/shard_map/all_to_all | solution.py:384
  18.2 1.4 %boundary.1 = bf16[16,16,128]{2,1,0:T(8,128)(2,1)} custom-call(bf16[32,4,384]{2,1,0:T(4,128)(2,1)S(1)} %all-to-all-done.trace_ref, bf16[512,768]{1,0:T(8,128)(2,1)S(1)} %get-tuple-element.19.real_ref, bf16[512,768]{1,0:T(8,128)(2,1)S(1)} %get-tuple-element.18.imag_ref, bf16[256,128]{1,0:T(8,128)(2,1)S(1)} %collective-permute-done.row_ref.refs_4_), custom_call_target="tpu_custom_call" | custom-call | tf_op jit(solution)/shard_map/boundary/pallas_call | solution.py:390
  19.6 4.9 %all-to-all-start.1 = ((bf16[16,16,128]{2,1,0:T(8,128)(2,1)}), bf16[16,16,128]{2,1,0:T(8,128)(2,1)S(1)}, u32[]{:S(2)}, u32[]{:S(2)}) async-start(bf16[16,16,128]{2,1,0:T(8,128)(2,1)} %boundary.1), calls=%async_computation.1 | async-start | bytes 131072 | tf_op jit(solution)/shard_map/all_to_all | solution.py:398
  24.5 0.0 collective-permute-done.1
  24.5 0.0 collective-permute-done.2
  24.5 0.1 corners.1
  24.6 0.6 %collective-permute-start.3 = (bf16[128,128]{1,0:T(8,128)(2,1)S(1)}, bf16[128,128]{1,0:T(8,128)(2,1)S(1)}, u32[]{:S(2)}, u32[]{:S(2)}) collective-permute-start(bf16[128,128]{1,0:T(8,128)(2,1)S(1)} %corners.1), channel_id=1, source_target_pairs={{0,16},{16,0},{1,17},{17,1},{2,18},{18,2},{3,19},{19,3},{4,20},{20... | collective-permute-start | bytes 98312 | tf_op jit(solution)/shard_map/ppermute | solution.py:411
  25.2 0.0 copy-done
  25.2 0.0 copy-done.1
  25.2 0.0 copy-done.2
  25.2 0.0 copy-done.3
  25.3 2.2 %volume.1 = (f32[2048,128]{1,0:T(8,128)}, f32[2,512,128]{2,1,0:T(8,128)S(1)}) custom-call(f32[2048,128]{1,0:T(8,128)S(1)} %bitcast.15, f32[32,128]{1,0:T(8,128)S(1)} %bitcast.21, f32[64,1,384]{2,1,0:T(1,128)S(1)} %bitcast.20, s32[1,384]{1,0:T(1,128)S(1)} %bitcast.24, bf16[256,128]{1,0:T(8,128)(2,1)S(1)} %collective-permute-done.row_ref.refs_4_, ...), custom_call_target="tpu_custom_call" | custom-call | tf_op jit(solution)/shard_map/volume/pallas_call | solution.py:415
  27.5 1.1 %collective-permute-done.3.refs_0_ = bf16[128,128]{1,0:T(8,128)(2,1)S(1)} collective-permute-done((bf16[128,128]{1,0:T(8,128)(2,1)S(1)}, bf16[128,128]{1,0:T(8,128)(2,1)S(1)}, u32[]{:S(2)}, u32[]{:S(2)}) %collective-permute-start.3) | collective-permute-done | bytes 32800 | tf_op jit(solution)/shard_map/ppermute | solution.py:411
  28.6 0.3 %all-to-all-done.1.part_ref = bf16[16,16,128]{2,1,0:T(8,128)(2,1)S(1)} async-done(((bf16[16,16,128]{2,1,0:T(8,128)(2,1)}), bf16[16,16,128]{2,1,0:T(8,128)(2,1)S(1)}, u32[]{:S(2)}, u32[]{:S(2)}) %all-to-all-start.1) | async-done | bytes 65568 | tf_op jit(solution)/shard_map/all_to_all | solution.py:398
  28.9 0.9 %last.1 = (f32[32,64]{1,0:T(8,128)}, f32[64,32,128]{2,1,0:T(8,128)}) custom-call(bf16[16,16,128]{2,1,0:T(8,128)(2,1)S(1)} %all-to-all-done.1.part_ref, f32[32,128]{1,0:T(8,128)S(1)} %bitcast.22, f32[2,512,128]{2,1,0:T(8,128)S(1)} %get-tuple-element.14.edge_ref, bf16[128,128]{1,0:T(8,128)(2,1)S(1)} %collective-permute-done.3.refs_0_, ...), custom_call_target="tpu_custom_call", output_to_operand_aliasing={{1}: (4, {})} | custom-call | tf_op jit(solution)/shard_map/last/pallas_call | solution.py:434
Async XLA Ops:
  3.6 14.6 %all-to-all-start = ((bf16[32,4,384]{2,1,0:T(4,128)(2,1)}), bf16[32,4,384]{2,1,0:T(4,128)(2,1)S(1)}, u32[]{:S(2)}, u32[]{:S(2)}) async-start(bf16[32,4,384]{2,1,0:T(4,128)(2,1)} %get-tuple-element.10), calls=%async_computation | async-start | bytes 196608 | tf_op jit(solution)/shard_map/all_to_all | solution.py:384
  10.9 5.0 %collective-permute-start = (bf16[256,128]{1,0:T(8,128)(2,1)}, bf16[256,128]{1,0:T(8,128)(2,1)S(1)}, u32[]{:S(2)}, u32[]{:S(2)}) collective-permute-start(bf16[256,128]{1,0:T(8,128)(2,1)} %get-tuple-element.11), channel_id=1, source_target_pairs={{0,16},{16,0},{1,17},{17,1},{2,18},{18,2},{3,19},{19,3},{4,20},{20... | collective-permute-start | bytes 196616 | tf_op jit(solution)/shard_map/ppermute | solution.py:381
  12.8 11.7 %collective-permute-start.1 = (f32[64,8,128]{2,1,0:T(8,128)}, f32[64,8,128]{2,1,0:T(8,128)S(1)}, u32[]{:S(2)}, u32[]{:S(2)}) collective-permute-start(f32[64,8,128]{2,1,0:T(8,128)} %get-tuple-element.12), channel_id=1, source_target_pairs={{0,1},{1,0},{2,3},{3,2},{4,5},{5,4},{6,7},{7,6},{8,9},{9,8},{10,11... | collective-permute-start | bytes 786440 | tf_op jit(solution)/shard_map/ppermute | solution.py:377
  12.8 11.7 %collective-permute-start.2 = (f32[64,8,128]{2,1,0:T(8,128)}, f32[64,8,128]{2,1,0:T(8,128)S(1)}, u32[]{:S(2)}, u32[]{:S(2)}) collective-permute-start(f32[64,8,128]{2,1,0:T(8,128)} %get-tuple-element.13), channel_id=1, source_target_pairs={{1,2},{2,1},{3,4},{4,3},{5,6},{6,5},{7,8},{8,7},{9,10},{10,9},{11,... | collective-permute-start | bytes 786440 | tf_op jit(solution)/shard_map/ppermute | solution.py:377
  14.9 10.3 %copy-start = (f32[64,4,8,128]{3,2,1,0:T(8,128)S(1)}, f32[64,4,8,128]{3,2,1,0:T(8,128)}, u32[]{:S(2)}) copy-start(f32[64,4,8,128]{3,2,1,0:T(8,128)} %param.6) | copy-start | bytes 3145732
  14.9 10.3 %copy-start.1 = (f32[64,1,1,384]{3,2,1,0:T(1,128)S(1)}, f32[64,1,1,384]{3,2,1,0:T(1,128)}, u32[]{:S(2)}) copy-start(f32[64,1,1,384]{3,2,1,0:T(1,128)} %param.8) | copy-start | bytes 294916
  14.9 10.3 %copy-start.2 = (f32[4,8,128]{2,1,0:T(8,128)S(1)}, f32[4,8,128]{2,1,0:T(8,128)}, u32[]{:S(2)}) copy-start(f32[4,8,128]{2,1,0:T(8,128)} %param.7) | copy-start | bytes 49156
  15.0 10.3 %copy-start.3 = (s32[1,1,384]{2,1,0:T(1,128)S(1)}, s32[1,1,384]{2,1,0:T(1,128)}, u32[]{:S(2)}) copy-start(s32[1,1,384]{2,1,0:T(1,128)} %param.9) | copy-start | bytes 4612
  19.6 9.3 %all-to-all-start.1 = ((bf16[16,16,128]{2,1,0:T(8,128)(2,1)}), bf16[16,16,128]{2,1,0:T(8,128)(2,1)S(1)}, u32[]{:S(2)}, u32[]{:S(2)}) async-start(bf16[16,16,128]{2,1,0:T(8,128)(2,1)} %boundary.1), calls=%async_computation.1 | async-start | bytes 131072 | tf_op jit(solution)/shard_map/all_to_all | solution.py:398
  24.6 4.0 %collective-permute-start.3 = (bf16[128,128]{1,0:T(8,128)(2,1)S(1)}, bf16[128,128]{1,0:T(8,128)(2,1)S(1)}, u32[]{:S(2)}, u32[]{:S(2)}) collective-permute-start(bf16[128,128]{1,0:T(8,128)(2,1)S(1)} %corners.1), channel_id=1, source_target_pairs={{0,16},{16,0},{1,17},{17,1},{2,18},{18,2},{3,19},{19,3},{4,20},{20... | collective-permute-start | bytes 98312 | tf_op jit(solution)/shard_map/ppermute | solution.py:411

commit v9 on v7

--- a/solution.py
+++ b/solution.py
@@ -408,7 +408,7 @@
             pltpu.VMEM((comps * lines // 2, 2 * depth), f32),
             pltpu.VMEM((comps * lines, depth), f32),
             pltpu.VMEM((row_swaps, comps * width_x, depth), f32),
-            pltpu.SemaphoreType.DMA((8,)),
+            pltpu.SemaphoreType.DMA((16,)),
         ],
         compiler_params=params,
         name="volume",

time: 30.2 us -> 30.2 us (level)
  no operation moved by 1% of the time
where the time goes in v9:
time: 30.2 us; the launch traced here: 29.9 us
  starting transfers between devices  14.5 us (48%)
  Pallas kernels  7.67 us (25%)
  waiting for transfers between devices  5.48 us (18%)
  local copies, waits for them, and re-layouts  1.5 us (5%)
  between operations  0.72 us (2%)
    all_to_all x1, starting transfers between devices, on_device(): received = lax.all_to_all(tiles, ('row', 'col'), 0, 0, tiled=True)  7.3 us
    all_to_all x1, starting transfers between devices, on_device(): lax.all_to_all(shares, 'col', 0, 0, tiled=True, axis_index_groups=[root_f...  3.93 us
    all_to_all x1, waiting for transfers between devices, on_device(): received = lax.all_to_all(tiles, ('row', 'col'), 0, 0, tiled=True)  3.19 us
    pallas_call x1, Pallas kernels, on_device(): pl.pallas_call(functools.partial(trace_kernel, dims, row_swaps), out_shap...  2.98 us
    pallas_call x1, Pallas kernels, on_device(): pl.pallas_call(functools.partial(volume_kernel, dims, row_swaps), out_sha...  2.28 us
    ppermute x1, starting transfers between devices, on_device(): lax.ppermute(face, 'row', swap_pairs(rows, swap))  1.83 us
    squeeze x1, local copies, waits for them, and re-layouts, on_device(): boundary_matrix[1]  1.48 us
    pallas_call x1, Pallas kernels, on_device(): pl.pallas_call(functools.partial(boundary_kernel, slot_len, own_rows), ou...  1.4 us
  transfers between devices with their start and end apart: 6, of which 4 were waited for; matrix products, arithmetic and copies ran while one was open for 5% of the time, Pallas kernels for 13%

profile of v9, /device:TPU:0, one launch (start us, length us, event | category | flops | bytes accessed | tf_op | source)
XLA Modules:
  0.0 29.9 jit_solution(12619274044335200107)
XLA Ops:
  0.6 3.0 %traces.1 = (bf16[32,16,128]{2,1,0:T(8,128)(2,1)}, bf16[256,128]{1,0:T(8,128)(2,1)}, f32[64,8,128]{2,1,0:T(8,128)}, f32[64,8,128]{2,1,0:T(8,128)}) custom-call(s32[1,16]{1,0:T(1,128)} %bitcast.27, s32[1,384]{1,0:T(1,128)} %bitcast.23, f32[64,32,128]{2,1,0:T(8,128)} %bitcast.14), custom_call_target="tpu_custom_call" | custom-call | tf_op jit(solution)/shard_map/traces/pallas_call | solution.py:341
  3.6 7.3 %all-to-all-start = ((bf16[32,16,128]{2,1,0:T(8,128)(2,1)}), bf16[32,16,128]{2,1,0:T(8,128)(2,1)S(1)}, u32[]{:S(2)}, u32[]{:S(2)}) async-start(bf16[32,16,128]{2,1,0:T(8,128)(2,1)} %get-tuple-element.10), calls=%async_computation | async-start | bytes 262144 | tf_op jit(solution)/shard_map/all_to_all | solution.py:369
  10.9 1.8 %collective-permute-start = (bf16[256,128]{1,0:T(8,128)(2,1)}, bf16[256,128]{1,0:T(8,128)(2,1)S(1)}, u32[]{:S(2)}, u32[]{:S(2)}) collective-permute-start(bf16[256,128]{1,0:T(8,128)(2,1)} %get-tuple-element.11), channel_id=1, source_target_pairs={{0,16},{16,0},{1,17},{17,1},{2,18},{18,2},{3,19},{19,3},{4,20},{20... | collective-permute-start | bytes 196616 | tf_op jit(solution)/shard_map/ppermute | solution.py:366
  12.8 0.0 collective-permute-start.1
  12.8 0.7 %collective-permute-start.2 = (f32[64,8,128]{2,1,0:T(8,128)}, f32[64,8,128]{2,1,0:T(8,128)S(1)}, u32[]{:S(2)}, u32[]{:S(2)}) collective-permute-start(f32[64,8,128]{2,1,0:T(8,128)} %get-tuple-element.13), channel_id=1, source_target_pairs={{1,2},{2,1},{3,4},{4,3},{5,6},{6,5},{7,8},{8,7},{9,10},{10,9},{11,... | collective-permute-start | bytes 786440 | tf_op jit(solution)/shard_map/ppermute | solution.py:362
  13.4 1.5 %slice_bitcast_fusion = (bf16[512,768]{1,0:T(8,128)(2,1)S(1)}, bf16[512,768]{1,0:T(8,128)(2,1)S(1)}) fusion(bf16[2,512,768]{2,1,0:T(8,128)(2,1)} %param.11), kind=kLoop, calls=%fused_computation | loop fusion | bytes 3145728 | tf_op jit(solution)/shard_map/squeeze | solution.py:380
  14.9 0.0 copy-start
  14.9 0.0 copy-start.1
  14.9 0.0 copy-start.2
  15.0 0.0 copy-start.3
  15.0 1.1 %collective-permute-done.row_ref.refs_4_ = bf16[256,128]{1,0:T(8,128)(2,1)S(1)} collective-permute-done((bf16[256,128]{1,0:T(8,128)(2,1)}, bf16[256,128]{1,0:T(8,128)(2,1)S(1)}, u32[]{:S(2)}, u32[]{:S(2)}) %collective-permute-start) | collective-permute-done | bytes 65568 | tf_op jit(solution)/shard_map/ppermute | solution.py:366
  16.1 3.2 %all-to-all-done.trace_ref = bf16[32,16,128]{2,1,0:T(8,128)(2,1)S(1)} async-done(((bf16[32,16,128]{2,1,0:T(8,128)(2,1)}), bf16[32,16,128]{2,1,0:T(8,128)(2,1)S(1)}, u32[]{:S(2)}, u32[]{:S(2)}) %all-to-all-start) | async-done | bytes 131104 | tf_op jit(solution)/shard_map/all_to_all | solution.py:369
  19.3 1.4 %boundary.1 = bf16[16,16,128]{2,1,0:T(8,128)(2,1)} custom-call(bf16[32,16,128]{2,1,0:T(8,128)(2,1)S(1)} %all-to-all-done.trace_ref, bf16[512,768]{1,0:T(8,128)(2,1)S(1)} %get-tuple-element.19.real_ref, bf16[512,768]{1,0:T(8,128)(2,1)S(1)} %get-tuple-element.18.imag_ref, bf16[256,128]{1,0:T(8,128)(2,1)S(1)} %collective-permute-done.row_ref.refs_4_), custom_call_target="tpu_custom_call" | custom-call | tf_op jit(solution)/shard_map/boundary/pallas_call | solution.py:373
  20.7 3.9 %all-to-all-start.1 = ((bf16[16,16,128]{2,1,0:T(8,128)(2,1)}), bf16[16,16,128]{2,1,0:T(8,128)(2,1)S(1)}, u32[]{:S(2)}, u32[]{:S(2)}) async-start(bf16[16,16,128]{2,1,0:T(8,128)(2,1)} %boundary.1), calls=%async_computation.1 | async-start | bytes 131072 | tf_op jit(solution)/shard_map/all_to_all | solution.py:381
  24.6 0.0 collective-permute-done.1
  24.6 0.0 collective-permute-done.2
  24.6 0.1 corners.1
  24.7 0.7 %collective-permute-start.3 = (bf16[128,128]{1,0:T(8,128)(2,1)S(1)}, bf16[128,128]{1,0:T(8,128)(2,1)S(1)}, u32[]{:S(2)}, u32[]{:S(2)}) collective-permute-start(bf16[128,128]{1,0:T(8,128)(2,1)S(1)} %corners.1), channel_id=1, source_target_pairs={{0,16},{16,0},{1,17},{17,1},{2,18},{18,2},{3,19},{19,3},{4,20},{20... | collective-permute-start | bytes 98312 | tf_op jit(solution)/shard_map/ppermute | solution.py:394
  25.5 0.0 copy-done
  25.5 0.0 copy-done.1
  25.5 0.0 copy-done.2
  25.5 0.0 copy-done.3
  25.5 2.3 %volume.1 = (f32[2048,128]{1,0:T(8,128)}, f32[2,512,128]{2,1,0:T(8,128)S(1)}) custom-call(f32[2048,128]{1,0:T(8,128)S(1)} %bitcast.15, f32[32,128]{1,0:T(8,128)S(1)} %bitcast.21, f32[64,1,384]{2,1,0:T(1,128)S(1)} %bitcast.20, s32[1,384]{1,0:T(1,128)S(1)} %bitcast.24, bf16[256,128]{1,0:T(8,128)(2,1)S(1)} %collective-permute-done.row_ref.refs_4_, ...), custom_call_target="tpu_custom_call" | custom-call | tf_op jit(solution)/shard_map/volume/pallas_call | solution.py:398
  27.8 0.9 %collective-permute-done.3.refs_0_ = bf16[128,128]{1,0:T(8,128)(2,1)S(1)} collective-permute-done((bf16[128,128]{1,0:T(8,128)(2,1)S(1)}, bf16[128,128]{1,0:T(8,128)(2,1)S(1)}, u32[]{:S(2)}, u32[]{:S(2)}) %collective-permute-start.3) | collective-permute-done | bytes 32800 | tf_op jit(solution)/shard_map/ppermute | solution.py:394
  28.7 0.3 all-to-all-done.1.part_ref
  29.0 0.9 %last.1 = (f32[32,64]{1,0:T(8,128)}, f32[64,32,128]{2,1,0:T(8,128)}) custom-call(bf16[16,16,128]{2,1,0:T(8,128)(2,1)S(1)} %all-to-all-done.1.part_ref, f32[32,128]{1,0:T(8,128)S(1)} %bitcast.22, f32[2,512,128]{2,1,0:T(8,128)S(1)} %get-tuple-element.14.edge_ref, bf16[128,128]{1,0:T(8,128)(2,1)S(1)} %collective-permute-done.3.refs_0_, ...), custom_call_target="tpu_custom_call", output_to_operand_aliasing={{1}: (4, {})} | custom-call | tf_op jit(solution)/shard_map/last/pallas_call | solution.py:417
Async XLA Ops:
  3.6 15.6 %all-to-all-start = ((bf16[32,16,128]{2,1,0:T(8,128)(2,1)}), bf16[32,16,128]{2,1,0:T(8,128)(2,1)S(1)}, u32[]{:S(2)}, u32[]{:S(2)}) async-start(bf16[32,16,128]{2,1,0:T(8,128)(2,1)} %get-tuple-element.10), calls=%async_computation | async-start | bytes 262144 | tf_op jit(solution)/shard_map/all_to_all | solution.py:369
  10.9 5.1 %collective-permute-start = (bf16[256,128]{1,0:T(8,128)(2,1)}, bf16[256,128]{1,0:T(8,128)(2,1)S(1)}, u32[]{:S(2)}, u32[]{:S(2)}) collective-permute-start(bf16[256,128]{1,0:T(8,128)(2,1)} %get-tuple-element.11), channel_id=1, source_target_pairs={{0,16},{16,0},{1,17},{17,1},{2,18},{18,2},{3,19},{19,3},{4,20},{20... | collective-permute-start | bytes 196616 | tf_op jit(solution)/shard_map/ppermute | solution.py:366
  12.8 11.8 %collective-permute-start.1 = (f32[64,8,128]{2,1,0:T(8,128)}, f32[64,8,128]{2,1,0:T(8,128)S(1)}, u32[]{:S(2)}, u32[]{:S(2)}) collective-permute-start(f32[64,8,128]{2,1,0:T(8,128)} %get-tuple-element.12), channel_id=1, source_target_pairs={{0,1},{1,0},{2,3},{3,2},{4,5},{5,4},{6,7},{7,6},{8,9},{9,8},{10,11... | collective-permute-start | bytes 786440 | tf_op jit(solution)/shard_map/ppermute | solution.py:362
  12.8 11.8 %collective-permute-start.2 = (f32[64,8,128]{2,1,0:T(8,128)}, f32[64,8,128]{2,1,0:T(8,128)S(1)}, u32[]{:S(2)}, u32[]{:S(2)}) collective-permute-start(f32[64,8,128]{2,1,0:T(8,128)} %get-tuple-element.13), channel_id=1, source_target_pairs={{1,2},{2,1},{3,4},{4,3},{5,6},{6,5},{7,8},{8,7},{9,10},{10,9},{11,... | collective-permute-start | bytes 786440 | tf_op jit(solution)/shard_map/ppermute | solution.py:362
  14.9 10.6 %copy-start = (f32[64,4,8,128]{3,2,1,0:T(8,128)S(1)}, f32[64,4,8,128]{3,2,1,0:T(8,128)}, u32[]{:S(2)}) copy-start(f32[64,4,8,128]{3,2,1,0:T(8,128)} %param.6) | copy-start | bytes 3145732
  14.9 10.5 %copy-start.1 = (f32[64,1,1,384]{3,2,1,0:T(1,128)S(1)}, f32[64,1,1,384]{3,2,1,0:T(1,128)}, u32[]{:S(2)}) copy-start(f32[64,1,1,384]{3,2,1,0:T(1,128)} %param.8) | copy-start | bytes 294916
  14.9 10.5 %copy-start.2 = (f32[4,8,128]{2,1,0:T(8,128)S(1)}, f32[4,8,128]{2,1,0:T(8,128)}, u32[]{:S(2)}) copy-start(f32[4,8,128]{2,1,0:T(8,128)} %param.7) | copy-start | bytes 49156
  15.0 10.5 %copy-start.3 = (s32[1,1,384]{2,1,0:T(1,128)S(1)}, s32[1,1,384]{2,1,0:T(1,128)}, u32[]{:S(2)}) copy-start(s32[1,1,384]{2,1,0:T(1,128)} %param.9) | copy-start | bytes 4612
  20.7 8.3 %all-to-all-start.1 = ((bf16[16,16,128]{2,1,0:T(8,128)(2,1)}), bf16[16,16,128]{2,1,0:T(8,128)(2,1)S(1)}, u32[]{:S(2)}, u32[]{:S(2)}) async-start(bf16[16,16,128]{2,1,0:T(8,128)(2,1)} %boundary.1), calls=%async_computation.1 | async-start | bytes 131072 | tf_op jit(solution)/shard_map/all_to_all | solution.py:381
  24.7 4.0 %collective-permute-start.3 = (bf16[128,128]{1,0:T(8,128)(2,1)S(1)}, bf16[128,128]{1,0:T(8,128)(2,1)S(1)}, u32[]{:S(2)}, u32[]{:S(2)}) collective-permute-start(bf16[128,128]{1,0:T(8,128)(2,1)S(1)} %corners.1), channel_id=1, source_target_pairs={{0,16},{16,0},{1,17},{17,1},{2,18},{18,2},{3,19},{19,3},{4,20},{20... | collective-permute-start | bytes 98312 | tf_op jit(solution)/shard_map/ppermute | solution.py:394
